TPU v7x, 32 devices: a whole 2x2x4 slice. The times are simulated.
32 devices in a mesh: blk: 16 (over z, x, core), tp: 2 (over y).
Axes of the slice: x: 2, y: 2, z: 4, core: 2. Of those that a mesh axis runs over, the one named last changes fastest.
Arguments:
- tokens: bfloat16 [4096, 8192], P('blk', 'tp'), may hold values from -6 to 6
- weight: bfloat16 [8192, 2048], P('tp'), may hold values from -0.0625 to 0.0625
- bank_a: bfloat16 [16, 8192, 32], P('blk', 'tp'), may hold values from -0.0625 to 0.0625
- bank_b: bfloat16 [16, 32, 1024], P('blk'), may hold values from -1.5 to 1.5
- tile_map: int32 [32, 1], P('blk'), may hold values from 0 to 15
- grad_out: bfloat16 [4096, 2048], P(('blk', 'tp')), may hold values from -6 to 6
Outputs:
- key_value_output: bfloat16 [4096, 2048], P(('blk', 'tp'))
- token_gradient: bfloat16 [4096, 8192], P('blk', 'tp')
- grad_a: float32 [16, 8192, 32], P('blk', 'tp')
- grad_b: float32 [16, 32, 1024], P('blk', None, 'tp')
Inputs may be any that keep to these rules, and one draw needn't show every extreme that they name: `tile_map`: every one of the 16 adapters is the adapter of at least one tile.
All inputs are finite; a program needn't handle non-finite values.
Results may differ from a plain program's by a relative error of at most 0.003.
Values may be sent and summed in bfloat16 or wider, within the bound.
No kernel may reach another device: no remote copies, remote signals or barrier semaphores. Data moves between devices by JAX's collectives and lax.ppermute only.
A program may use at most 128 MiB of HBM per device.

v0:
```python
import jax
import jax.numpy as jnp
from jax import lax
from jax.sharding import PartitionSpec as P

adapter_scale = 0.5


def on_device(tokens, weight, bank_a, bank_b, tile_map, grad_out):
    tile_index_list = tile_map[:, 0]
    grouped_row_count = tokens.shape[0]
    feature_shard = tokens.shape[1]
    tile_count = tile_index_list.shape[0]
    tile_rows = grouped_row_count // tile_count
    rank_two = bank_a.shape[2]
    rank_one = rank_two // 2
    kv_width = bank_b.shape[2]
    tp_count = lax.axis_size("tp")
    local_row_block = grouped_row_count // tp_count
    kv_dev = kv_width // tp_count
    adapt_local = bank_a.shape[0]
    empty = (
        jnp.zeros((tile_count, feature_shard, rank_two), jnp.bfloat16),
        jnp.zeros((tile_count, rank_two, kv_width), jnp.bfloat16),
    )
    whole_a, whole_b = (
        lax.all_gather(bank_a, "blk", axis=0, tiled=True),
        lax.all_gather(bank_b, "blk", axis=0, tiled=True),
    )
    pieces = (whole_a, whole_b)
    piece_rows = pieces[0].shape[0]
    one_hot = (tile_index_list[:, None] == jnp.arange(piece_rows, dtype=jnp.int32)[None, :]).astype(
        jnp.bfloat16
    )
    picked_a = jnp.dot(
        one_hot, pieces[0].reshape(piece_rows, -1), preferred_element_type=jnp.float32
    )
    picked_b = jnp.dot(
        one_hot, pieces[1].reshape(piece_rows, -1), preferred_element_type=jnp.float32
    )
    factor_down = picked_a.reshape(empty[0].shape).astype(jnp.bfloat16)
    fac_b = picked_b.reshape(empty[1].shape).astype(jnp.bfloat16)
    token_tile_index = tokens.reshape(tile_count, tile_rows, feature_shard)
    rank_part = jnp.einsum(
        "tre,tek->trk", token_tile_index, factor_down, preferred_element_type=jnp.float32
    )
    rank_act = lax.psum(rank_part, "tp").astype(jnp.bfloat16)
    base_local_rows = lax.psum_scatter(
        jnp.dot(tokens, weight, preferred_element_type=jnp.float32),
        "tp",
        scatter_dimension=0,
        tiled=True,
    )
    adapter_complete = jnp.concatenate(
        [
            jnp.einsum(
                "trk,tkc->trc",
                rank_act[:, :, :rank_one],
                fac_b[:, :rank_one],
                preferred_element_type=jnp.float32,
            ),
            jnp.einsum(
                "trk,tkc->trc",
                rank_act[:, :, rank_one:],
                fac_b[:, rank_one:],
                preferred_element_type=jnp.float32,
            ),
        ],
        axis=2,
    ).reshape(grouped_row_count, 2 * kv_width)
    first_row_index = lax.axis_index("tp") * local_row_block
    adapter_local_rows = lax.dynamic_slice_in_dim(
        adapter_complete, first_row_index, local_row_block, 0
    )
    key_value_output = (base_local_rows + adapter_scale * adapter_local_rows).astype(jnp.bfloat16)
    grad_rows = lax.all_gather(grad_out, "tp", axis=0, tiled=True)
    gradient_per_tile = grad_rows.reshape(tile_count, tile_rows, 2 * kv_width)
    low_rank_gradient = jnp.concatenate(
        [
            jnp.einsum(
                "trc,tkc->trk",
                gradient_per_tile[:, :, :kv_width],
                fac_b[:, :rank_one],
                preferred_element_type=jnp.float32,
            ),
            jnp.einsum(
                "trc,tkc->trk",
                gradient_per_tile[:, :, kv_width:],
                fac_b[:, rank_one:],
                preferred_element_type=jnp.float32,
            ),
        ],
        axis=2,
    ).astype(jnp.bfloat16)
    backward_pass = jnp.einsum("rc,ec->re", grad_rows, weight, preferred_element_type=jnp.float32)
    backward_adapter_term = jnp.einsum(
        "qdu,qyu->qdy", low_rank_gradient, factor_down, preferred_element_type=jnp.float32
    )
    token_gradient = (
        backward_pass
        + adapter_scale * backward_adapter_term.reshape(grouped_row_count, feature_shard)
    ).astype(jnp.bfloat16)
    tile_down_gradient = adapter_scale * jnp.einsum(
        "tre,trk->tek", token_tile_index, low_rank_gradient, preferred_element_type=jnp.float32
    )
    col_start = lax.axis_index("tp") * kv_dev
    key_cols = lax.dynamic_slice_in_dim(gradient_per_tile[:, :, :kv_width], col_start, kv_dev, 2)
    value_cols = lax.dynamic_slice_in_dim(gradient_per_tile[:, :, kv_width:], col_start, kv_dev, 2)
    tile_up_gradient = adapter_scale * jnp.concatenate(
        [
            jnp.einsum(
                "trk,trc->tkc",
                rank_act[:, :, :rank_one],
                key_cols,
                preferred_element_type=jnp.float32,
            ),
            jnp.einsum(
                "trk,trc->tkc",
                rank_act[:, :, rank_one:],
                value_cols,
                preferred_element_type=jnp.float32,
            ),
        ],
        axis=1,
    )
    size_a = feature_shard * rank_two
    flat_grads = jnp.concatenate(
        [tile_down_gradient.reshape(tile_count, -1), tile_up_gradient.reshape(tile_count, -1)],
        axis=1,
    )
    one_hot = (
        tile_index_list[:, None]
        == jnp.arange(adapt_local * lax.axis_size("blk"), dtype=jnp.int32)[None, :]
    ).astype(jnp.float32)
    summed = lax.psum_scatter(
        jnp.dot(
            one_hot.T,
            flat_grads,
            precision=lax.Precision.HIGHEST,
            preferred_element_type=jnp.float32,
        ),
        "blk",
        scatter_dimension=0,
        tiled=True,
    )
    grad_a = summed[:, :size_a].reshape(adapt_local, feature_shard, rank_two)
    grad_b = summed[:, size_a:].reshape(adapt_local, rank_two, kv_dev)
    return (key_value_output, token_gradient, grad_a, grad_b)


def solution(mesh):
    in_specs = (
        P("blk", "tp"),
        P("tp", None),
        P("blk", "tp", None),
        P("blk", None, None),
        P("blk", None),
        P(("blk", "tp"), None),
    )
    out_specs = (P(("blk", "tp"), None), P("blk", "tp"), P("blk", "tp", None), P("blk", None, "tp"))
    return jax.shard_map(
        on_device, mesh=mesh, in_specs=in_specs, out_specs=out_specs, check_vma=False
    )
```

profile of v0, /device:TPU:0, one launch (start us, length us, event | category | flops | bytes accessed | tf_op | source)
XLA Modules:
  0.0 429.2 jit_solution(3340746102403498111)
XLA Ops:
  7.2 0.0 copy-start
  7.2 0.0 all-gather.8.cloned.1.call-start
  7.2 0.7 all-gather.8.cloned.1.call-update
  7.9 0.0 all-gather.6.cloned.1.call-start
  8.0 0.7 all-gather.6.cloned.1.call-update
  8.7 0.0 all-gather.4.cloned.1.call-start
  8.7 0.7 all-gather.4.cloned.1.call-update
  9.4 0.0 reduce-scatter.2.cloned.1.call-start
  9.5 9.4 %fusion.41 = f32[256,2048]{1,0:T(8,128)} fusion(bf16[256,4096]{1,0:T(8,128)(2,1)S(1)} %copy-done, bf16[4096,2048]{1,0:T(8,128)(2,1)} %param.7), kind=kOutput, calls=%fused_computation.57 | convolution fusion | flops 4294967296 | bytes 20971520 | tf_op jit(solution)/shard_map/dot_general | solution.py:49
  18.9 0.0 reduce-scatter.2.cloned.1.call-update
  18.9 0.0 all-reduce.3.cloned.1.call-start
  19.0 14.6 %all-gather.8.cloned.1.call-done = bf16[256,2048]{1,0:T(8,128)(2,1)} async-done(((bf16[128,2048]{1,0:T(8,128)(2,1)}), bf16[256,2048]{1,0:T(8,128)(2,1)}) %all-gather.8.cloned.1.call-update) | async-done | bytes 1048592 | tf_op jit(solution)/shard_map/all_gather | solution.py:76
  33.6 2.3 fusion.39
  35.9 37.8 %all-gather.6.cloned.1.call-done = bf16[16,32,1024]{2,1,0:T(8,128)(2,1)} async-done(((bf16[1,32,1024]{2,1,0:T(8,128)(2,1)}), bf16[16,32,1024]{2,1,0:T(8,128)(2,1)}) %all-gather.6.cloned.1.call-update) | async-done | bytes 1048592 | tf_op jit(solution)/shard_map/all_gather | solution.py:28
  73.7 1.9 convolution_convert_fusion.1
  75.7 0.1 fusion.40
  75.8 1.3 fusion.6
  77.0 0.3 fusion.7
  77.3 0.4 fusion.1
  77.7 2.8 copy.37
  80.5 5.3 %reshape.48 = f32[2,131072]{1,0:T(2,128)} reshape(f32[2,4096,32]{2,1,0:T(8,128)} %copy.37) | data formatting | bytes 2097152 | tf_op jit(solution)/shard_map/reshape | solution.py:128
  85.9 39.5 %all-gather.4.cloned.1.call-done = bf16[16,4096,32]{1,2,0:T(8,128)(2,1)} async-done(((bf16[1,4096,32]{1,2,0:T(8,128)(2,1)}), bf16[16,4096,32]{1,2,0:T(8,128)(2,1)}) %all-gather.4.cloned.1.call-update) | async-done | bytes 4194320 | tf_op jit(solution)/shard_map/all_gather | solution.py:27
  125.4 14.3 %copy.28 = bf16[16,4096,32]{2,1,0:T(8,128)(2,1)} copy(bf16[16,4096,32]{1,2,0:T(8,128)(2,1)} %all-gather.4.cloned.1.call-done) | data formatting | bytes 8388608 | tf_op jit(solution)/shard_map/all_gather | solution.py:27
  139.8 27.3 %reshape.43 = bf16[16,131072]{1,0:T(8,128)(2,1)} reshape(bf16[16,4096,32]{2,1,0:T(8,128)(2,1)} %copy.28) | data formatting | bytes 8388608 | tf_op jit(solution)/shard_map/reshape | solution.py:36
  167.0 22.5 %dot_general.58 = bf16[4096,32,16]{1,0,2:T(8,128)(2,1)} reshape(bf16[131072,16]{0,1:T(8,128)(2,1)} %bitcast.45) | data formatting | bytes 8388608 | tf_op jit(solution)/shard_map/dot_general | solution.py:35
  189.5 16.1 %copy.29 = bf16[4096,32,16]{0,2,1:T(8,128)(2,1)} copy(bf16[4096,32,16]{1,0,2:T(8,128)(2,1)} %dot_general.58) | data formatting | bytes 8388608 | tf_op jit(solution)/shard_map/dot_general | solution.py:35
  205.6 3.1 convolution_convert_fusion
  208.7 0.8 convolution_bitcast_fusion
  209.5 8.3 %psum.7 = bf16[2,128,32]{1,2,0:T(8,128)(2,1)S(1)} all-reduce(f32[2,128,32]{1,2,0:T(8,128)S(1)} %convolution_bitcast_fusion), channel_id=1, replica_groups=mesh['blk'=16,'tp'=2] {'tp'}, use_global_device_ids=true, to_apply=%region_1.0 | all-reduce | flops 8192 | bytes 49152 | tf_op jit(solution)/shard_map/psum | solution.py:47
  217.9 1.1 fusion.12
  219.0 0.2 fusion.14
  219.1 0.1 copy.41
  219.3 9.3 %fusion.2 = f32[16,147456]{1,0:T(8,128)} fusion(f32[2,16384]{1,0:T(2,128)S(1)} %bitcast.51, f32[2,131072]{1,0:T(2,128)} %reshape.48, s32[2]{0:T(128)S(1)} %bitcast.54), kind=kOutput, calls=%fused_computation.7 | convolution fusion | flops 56918048 | bytes 10616840 | tf_op jit(solution)/shard_map/dot_general | solution.py:136
  228.6 0.0 all-reduce.3.cloned.1.call-update
  228.6 0.6 copy-done.4
  229.2 0.6 dynamic-slice
  229.8 0.3 fusion.18
  230.1 0.3 fusion.21
  230.5 1.5 pad_maximum_fusion
  232.0 3.0 convolution_multiply_fusion
  235.0 2.5 add_convert_fusion
  237.5 13.5 %fusion = bf16[256,4096]{1,0:T(8,128)(2,1)} fusion(f32[256,4096]{1,0:T(8,128)} %bitcast.47, bf16[256,2048]{1,0:T(8,128)(2,1)} %all-gather.8.cloned.1.call-done, bf16[4096,2048]{1,0:T(8,128)(2,1)} %param.7), kind=kOutput, calls=%fused_computation.2 | convolution fusion | flops 4297064448 | bytes 24117248 | tf_op jit(solution)/shard_map/rc,ec->re/dot_general | solution.py:95
  251.0 160.2 %all-reduce.3.cloned.1.call-done = f32[16,147456]{1,0:T(8,128)} async-done(((f32[16,147456]{1,0:T(8,128)}), f32[16,147456]{1,0:T(8,128)}) %all-reduce.3.cloned.1.call-update) | async-done | bytes 9437200
  411.2 4.2 dynamic-slice_reduce_fusion
  415.4 1.8 reshape.49
  417.2 3.0 copy.38
  420.1 1.9 dynamic-slice_reduce_fusion.1
  422.1 0.6 reshape.50
  (10 shorter events, 0.0 us)
Async XLA Ops:
  7.2 2.3 copy-start
  7.2 26.4 %all-gather.8.cloned.1.call-start = ((), (), s32[]{:S(2)}) async-start(), calls=%async_computation.4 | async-start | bytes 1572864 | tf_op jit(solution)/shard_map/all_gather | solution.py:76
  7.9 65.8 %all-gather.6.cloned.1.call-start = ((), (), s32[]{:S(2)}) async-start(), calls=%async_computation.3 | async-start | bytes 1114112 | tf_op jit(solution)/shard_map/all_gather | solution.py:28
  8.7 116.7 %all-gather.4.cloned.1.call-start = ((), (), s32[]{:S(2)}) async-start(), calls=%async_computation.2 | async-start | bytes 4456448 | tf_op jit(solution)/shard_map/all_gather | solution.py:27
  9.4 225.6 %reduce-scatter.2.cloned.1.call-start = ((), (), s32[]{:S(2)}) async-start(), calls=%async_computation.1 | async-start | bytes 3145728 | tf_op jit(solution)/shard_map/reduce_scatter | solution.py:48
  18.9 54.8 %copy-start.3 = (s32[2,1]{0,1:T(1,128)S(1)}, s32[2,1]{0,1:T(1,128)}, u32[]{:S(2)}) copy-start(s32[2,1]{0,1:T(1,128)} %param.10) | copy-start | bytes 28
  18.9 392.2 %all-reduce.3.cloned.1.call-start = ((), (), s32[]{:S(2)}) async-start(), calls=%async_computation.5 | async-start | bytes 18874368
  33.6 43.4 %copy-start.2 = (bf16[256,2048]{1,0:T(8,128)(2,1)S(1)}, bf16[256,2048]{1,0:T(8,128)(2,1)}, u32[]{:S(2)}) copy-start(bf16[256,2048]{1,0:T(8,128)(2,1)} %all-gather.8.cloned.1.call-done) | copy-start | bytes 3145732
  205.6 13.3 %copy-start.1 = (bf16[2,128,1024]{2,1,0:T(8,128)(2,1)S(1)}, bf16[2,128,1024]{2,1,0:T(8,128)(2,1)}, u32[]{:S(2)}) copy-start(bf16[2,128,1024]{2,1,0:T(8,128)(2,1)} %get-tuple-element.16) | copy-start | bytes 1572868
  228.6 0.7 copy-start.4
Sparse Core Ops, SparseCore 0:
  9.6 23.9 all-gather.7
  35.8 37.9 all-gather.5
  75.9 49.4 all-gather.3
  128.1 30.3 reduce-scatter.1
  228.7 182.4 all-reduce.2
where the time goes:
time: 431 us; the launch traced here: 429 us
  waiting for transfers between devices  254 us (59%)
  local copies, waits for them, and re-layouts  104 us (24%)
  matrix products  45 us (10%)
  between operations  13.9 us (3%)
  blocking collectives  8.34 us (2%)
    unnamed x6, waiting for transfers between devices  162 us
    all_gather x1, waiting for transfers between devices, on_device(): lax.all_gather(bank_a, 'blk', axis=0, tiled=True)  39.5 us
    dot_general x2, local copies, waits for them, and re-layouts, on_device(): jnp.dot(one_hot, pieces[0].reshape(piece_rows, -1), preferred_element_typ...  38.6 us
    all_gather x1, waiting for transfers between devices, on_device(): lax.all_gather(bank_b, 'blk', axis=0, tiled=True)  37.8 us
    reshape x1, local copies, waits for them, and re-layouts, on_device(): pieces[0].reshape(piece_rows, -1)  27.3 us
    all_gather x1, waiting for transfers between devices, on_device(): grad_rows = lax.all_gather(grad_out, 'tp', axis=0, tiled=True)  14.6 us
    all_gather x1, local copies, waits for them, and re-layouts, on_device(): lax.all_gather(bank_a, 'blk', axis=0, tiled=True)  14.3 us
    dot_general x1, matrix products, on_device(): jnp.einsum('rc,ec->re', grad_rows, weight, preferred_element_type=jnp.flo...  13.5 us
  transfers between devices with their start and end apart: 5, of which 4 were waited for; matrix products, arithmetic and copies ran while one was open for 33% of the time, Pallas kernels for 0%

commit v1 on v0

v1 whole, which is shorter than its diff:
```python
import jax
import jax.numpy as jnp
from jax import lax
from jax.sharding import PartitionSpec as P

adapter_scale = 0.5
f32 = jnp.float32
bf16 = jnp.bfloat16


def swap(value, bit):
    count = lax.axis_size("blk")
    return lax.ppermute(value, "blk", [(i, i ^ (1 << bit)) for i in range(count)])


def dot(a, b, contract):
    return lax.dot_general(a, b, ((contract[:1], contract[1:]), ((), ())), preferred_element_type=f32)


def pick(blocks, hits):
    out = jnp.where(hits[0], blocks[0], jnp.zeros_like(blocks[0]))
    for block, hit in zip(blocks[1:], hits[1:]):
        out = jnp.where(hit, block, out)
    return out


def blend(blocks, hits):
    out = jnp.zeros(blocks[0].shape, f32)
    for block, hit in zip(blocks, hits):
        out = out + jnp.where(hit, block.astype(f32), 0.0)
    return out


def gather_high(own, high_bits):
    blocks = [own]
    for bit in high_bits:
        blocks = blocks + [swap(block, bit) for block in blocks]
    return blocks


def on_device(tokens, weight, bank_a, bank_b, tile_map, grad_out):
    blk_count = lax.axis_size("blk")
    tp_count = lax.axis_size("tp")
    me = lax.axis_index("blk")
    col = lax.axis_index("tp")
    bit_count = blk_count.bit_length() - 1
    core_bit, cross_bit = 0, 1
    high_bits = list(range(bit_count - 1, 1, -1))
    offsets = [0]
    for bit in high_bits:
        offsets = offsets + [o | (1 << bit) for o in offsets]
    both = offsets + [o | 1 for o in offsets]

    rows = tokens.shape[0]
    tile_count = tile_map.shape[0]
    tile_rows = rows // tile_count
    rank_two = bank_a.shape[2]
    rank_one = rank_two // 2
    kv_width = bank_b.shape[2]
    kv_dev = kv_width // tp_count
    local_rows = rows // tp_count

    own_a = bank_a[0].T
    own_b = bank_b[0]
    mine = [tile_map[k, 0] for k in range(tile_count)]
    map_far = swap(tile_map, cross_bit)
    theirs = [map_far[k, 0] for k in range(tile_count)]

    def gather(own):
        blocks = gather_high(own, high_bits)
        blocks = blocks + [swap(block, core_bit) for block in blocks]
        sent = [pick(blocks, [(m ^ me) == o for o in both]) for m in theirs]
        got = [swap(s, cross_bit) for s in sent]
        here = [pick(blocks, [(m ^ me) == o for o in both]) for m in mine]
        return [
            jnp.where(((m ^ me) & 2) == 0, h, g) for m, h, g in zip(mine, here, got)
        ]

    def give_back(parts):
        sent = [p.astype(bf16) for p in parts]
        got = [swap(s, cross_bit) for s in sent]
        held = list(parts) + got
        owner = mine + theirs
        away = [blend(held, [(m ^ me) == (o | 1) for m in owner]).astype(bf16) for o in offsets]
        keep = [blend(held, [(m ^ me) == o for m in owner]) for o in offsets]
        back = [swap(a, core_bit) for a in away]
        total = {o: k + b.astype(f32) for o, k, b in zip(offsets, keep, back)}
        for bit in reversed(high_bits):
            far = [o for o in total if o >> bit & 1]
            far.sort(reverse=True)
            came = {o: swap(total[o].astype(bf16), bit) for o in far}
            total = {o: total[o] + came[o | 1 << bit].astype(f32) for o in total if not o >> bit & 1}
        return total[0]

    if tp_count == 2:
        other = lax.ppermute(grad_out, "tp", [(0, 1), (1, 0)])
        grad_rows = jnp.where(
            col == 0,
            jnp.concatenate([grad_out, other], axis=0),
            jnp.concatenate([other, grad_out], axis=0),
        )
    else:
        grad_rows = lax.all_gather(grad_out, "tp", axis=0, tiled=True)

    factor_b = gather(own_b)
    zero = jnp.zeros((rank_one, kv_width), bf16)
    wide_b = [
        jnp.concatenate(
            [
                jnp.concatenate([b[:rank_one], zero], axis=1),
                jnp.concatenate([zero, b[rank_one:]], axis=1),
            ],
            axis=0,
        )
        for b in factor_b
    ]
    factor_a = gather(own_a)

    base = dot(tokens, weight, (1, 0))
    if tp_count == 2:
        far_base = lax.dynamic_slice_in_dim(base, (1 - col) * local_rows, local_rows, 0)
        near_base = lax.dynamic_slice_in_dim(base, col * local_rows, local_rows, 0)
        base_rows = near_base + lax.ppermute(far_base.astype(bf16), "tp", [(0, 1), (1, 0)]).astype(f32)
    else:
        base_rows = lax.psum_scatter(base, "tp", scatter_dimension=0, tiled=True)

    tiles = [tokens[k * tile_rows : (k + 1) * tile_rows] for k in range(tile_count)]
    grads = [grad_rows[k * tile_rows : (k + 1) * tile_rows] for k in range(tile_count)]

    rank_grad = [dot(b, g, (1, 1)).astype(bf16) for b, g in zip(wide_b, grads)]
    grad_a = give_back([adapter_scale * dot(r, x, (1, 0)) for r, x in zip(rank_grad, tiles)])

    rank_part = jnp.concatenate([dot(a, x, (1, 1)) for a, x in zip(factor_a, tiles)], axis=1)
    if tp_count == 2:
        rank_sum = rank_part + lax.ppermute(rank_part, "tp", [(0, 1), (1, 0)])
    else:
        rank_sum = lax.psum(rank_part, "tp")
    rank_act = rank_sum.astype(bf16)

    first = col * local_rows
    local_act = lax.dynamic_slice_in_dim(rank_act, first, local_rows, 1)
    local_b = pick(wide_b, [first // tile_rows == k for k in range(tile_count)])
    key_value_output = (base_rows + adapter_scale * dot(local_act, local_b, (0, 0))).astype(bf16)

    up = []
    for k in range(tile_count):
        whole = adapter_scale * dot(
            rank_act[:, k * tile_rows : (k + 1) * tile_rows], grads[k], (1, 0)
        )
        up.append(
            jnp.concatenate(
                [
                    lax.dynamic_slice(whole[:rank_one, :kv_width], (0, col * kv_dev), (rank_one, kv_dev)),
                    lax.dynamic_slice(whole[rank_one:, kv_width:], (0, col * kv_dev), (rank_one, kv_dev)),
                ],
                axis=0,
            )
        )
    grad_b = give_back(up)

    backward = dot(grad_rows, weight, (1, 1))
    lora = jnp.concatenate([dot(r, a, (0, 0)) for r, a in zip(rank_grad, factor_a)], axis=0)
    token_gradient = (backward + adapter_scale * lora).astype(bf16)
    return key_value_output, token_gradient, grad_a.T[None], grad_b[None]


def solution(mesh):
    in_specs = (
        P("blk", "tp"),
        P("tp", None),
        P("blk", "tp", None),
        P("blk", None, None),
        P("blk", None),
        P(("blk", "tp"), None),
    )
    out_specs = (P(("blk", "tp"), None), P("blk", "tp"), P("blk", "tp", None), P("blk", None, "tp"))
    return jax.shard_map(
        on_device, mesh=mesh, in_specs=in_specs, out_specs=out_specs, check_vma=False
    )
```

time: 431 us -> 125 us (0.29)
  waiting for transfers between devices: 254 us -> 47.1 us
  local copies, waits for them, and re-layouts: 104 us -> 2.55 us
  starting transfers between devices: 0.19 us -> 32.4 us
  between operations: 13.9 us -> 3.68 us
  matrix products: 45 us -> 35.1 us
  blocking collectives: 8.34 us -> 0 us
    unnamed x6 -> x0, waiting for transfers between devices: 162 us -> none
    all_gather x3 -> x0, waiting for transfers between devices: 92 us -> none  [the longest x1 39.5 us: on_device(): lax.all_gather(bank_a, 'blk', axis=0, tiled=True)]
    ppermute x0 -> x40, waiting for transfers between devices: none -> 47.1 us  [the longest x37 37.6 us: swap(): return lax.ppermute(value, 'blk', [(i, i ^ 1 << bit) for i in range(count)])]
    dot_general x2 -> x0, local copies, waits for them, and re-layouts: 38.6 us -> none  [on_device(): jnp.dot(one_hot, pieces[0].reshape(piece_rows, -1), preferred_element_typ...]
    reshape x4 -> x0, local copies, waits for them, and re-layouts: 35 us -> none  [the longest x1 27.3 us: on_device(): pieces[0].reshape(piece_rows, -1)]
    ppermute x0 -> x40, starting transfers between devices: none -> 32.4 us  [the longest x37 27.7 us: swap(): return lax.ppermute(value, 'blk', [(i, i ^ 1 << bit) for i in range(count)])]
    all_gather x1 -> x0, local copies, waits for them, and re-layouts: 14.3 us -> none  [on_device(): lax.all_gather(bank_a, 'blk', axis=0, tiled=True)]
    dot_general x14 -> x13, matrix products: 45 us -> 35.1 us  [dot(): lax.dot_general(a, b, ((contract[:1], contract[1:]), ((), ())), preferred...]
  transfers between devices with their start and end apart: 5 -> 40, of which waited for: 4 -> 14; matrix products, arithmetic and copies ran while one was open for 33% -> 32% of each run, Pallas kernels for 0% -> 0%
where the time goes in v1:
time: 125 us
  waiting for transfers between devices  47.1 us (38%)
  matrix products  35.1 us (28%)
  starting transfers between devices  32.4 us (26%)
  other arithmetic  4.07 us (3%)
  between operations  3.68 us (3%)
  local copies, waits for them, and re-layouts  2.55 us (2%)
    ppermute x37, waiting for transfers between devices, swap(): return lax.ppermute(value, 'blk', [(i, i ^ 1 << bit) for i in range(count)])  37.6 us
    dot_general x13, matrix products, dot(): lax.dot_general(a, b, ((contract[:1], contract[1:]), ((), ())), preferred...  35.1 us
    ppermute x37, starting transfers between devices, swap(): return lax.ppermute(value, 'blk', [(i, i ^ 1 << bit) for i in range(count)])  27.7 us
    ppermute x1, waiting for transfers between devices, on_device(): lax.ppermute(far_base.astype(bf16), 'tp', [(0, 1), (1, 0)]).astype(f32)  6.2 us
    ppermute x1, waiting for transfers between devices, on_device(): other = lax.ppermute(grad_out, 'tp', [(0, 1), (1, 0)])  3.37 us
  transfers between devices with their start and end apart: 40, of which 14 were waited for; matrix products, arithmetic and copies ran while one was open for 32% of the time, Pallas kernels for 0%

profile of v1, /device:TPU:0, one launch (start us, length us, event | category | flops | bytes accessed | tf_op | source)
XLA Modules:
  0.0 124.9 jit_solution(1854092020175935698)
XLA Ops:
  0.6 4.1 %collective-permute-start.12 = (bf16[32,1024]{1,0:T(8,128)(2,1)}, bf16[32,1024]{1,0:T(8,128)(2,1)S(1)}, u32[]{:S(2)}, u32[]{:S(2)}) collective-permute-start(bf16[32,1024]{1,0:T(8,128)(2,1)} %bitcast.37), channel_id=1, source_target_pairs={{0,16},{2,18},{4,20},{6,22},{8,24},{10,26},{12,28},{14,30},{16,0},... | collective-permute-start | bytes 196616 | tf_op jit(solution)/shard_map/ppermute | solution.py:13
  4.7 1.6 %collective-permute-start.15 = (bf16[32,1024]{1,0:T(8,128)(2,1)}, bf16[32,1024]{1,0:T(8,128)(2,1)S(1)}, u32[]{:S(2)}, u32[]{:S(2)}) collective-permute-start(bf16[32,1024]{1,0:T(8,128)(2,1)} %bitcast.38), channel_id=1, source_target_pairs={{0,8},{2,10},{4,12},{6,14},{8,0},{10,2},{12,4},{14,6},{16,24},{18,... | collective-permute-start | bytes 196616 | tf_op jit(solution)/shard_map/ppermute | solution.py:13
  6.3 1.5 %collective-permute-start.8 = (s32[2,1]{0,1:T(1,128)}, s32[2,1]{0,1:T(1,128)S(1)}, u32[]{:S(2)}, u32[]{:S(2)}) collective-permute-start(s32[2,1]{0,1:T(1,128)} %param.10), channel_id=1, source_target_pairs={{0,4},{2,6},{4,0},{6,2},{8,12},{10,14},{12,8},{14,10},{16,20},{18,... | collective-permute-start | bytes 32 | tf_op jit(solution)/shard_map/ppermute | solution.py:13
  8.2 12.3 %fusion.111 = f32[256,2048]{1,0:T(8,128)} fusion(bf16[256,4096]{1,0:T(8,128)(2,1)} %param.6, bf16[4096,2048]{1,0:T(8,128)(2,1)} %param.7), kind=kOutput, calls=%fused_computation.169 | convolution fusion | flops 4294967296 | bytes 20971520 | tf_op jit(solution)/shard_map/dot_general | solution.py:17
  20.5 1.3 %dynamic-slice_convert_fusion = bf16[128,2048]{1,0:T(8,128)(2,1)S(1)} fusion(f32[256,2048]{1,0:T(8,128)} %fusion.111, s32[]{:T(128)S(6)} %select_n.778), kind=kLoop, calls=%fused_computation.28 | loop fusion | bytes 1048580 | tf_op jit(solution)/shard_map/convert_element_type | solution.py:123
  21.8 0.5 collective-permute-start.13
  22.3 0.6 fusion.107
  24.3 0.5 collective-permute-start.16
  24.8 1.3 %collective-permute-done.13 = bf16[32,1024]{1,0:T(8,128)(2,1)S(1)} collective-permute-done((bf16[32,1024]{1,0:T(8,128)(2,1)S(1)}, bf16[32,1024]{1,0:T(8,128)(2,1)S(1)}, u32[]{:S(2)}, u32[]{:S(2)}) %collective-permute-start.13) | collective-permute-done | bytes 65568 | tf_op jit(solution)/shard_map/ppermute | solution.py:13
  26.1 0.6 fusion.108
  28.1 0.5 collective-permute-start.4
  28.8 1.5 %collective-permute-start.21 = (bf16[128,2048]{1,0:T(8,128)(2,1)S(1)}, bf16[128,2048]{1,0:T(8,128)(2,1)S(1)}, u32[]{:S(2)}, u32[]{:S(2)}) collective-permute-start(bf16[128,2048]{1,0:T(8,128)(2,1)S(1)} %copy-done.3), channel_id=1, source_target_pairs={{0,1},{1,0},{2,3},{3,2},{4,5},{5,4},{6,7},{7,6},{8,9},{9,8},{10,11... | collective-permute-start | bytes 1572872 | tf_op jit(solution)/shard_map/ppermute | solution.py:96
  30.4 0.6 collective-permute-start.20
  31.0 3.7 %collective-permute-done.20 = bf16[32,1024]{1,0:T(8,128)(2,1)S(1)} collective-permute-done((bf16[32,1024]{1,0:T(8,128)(2,1)S(1)}, bf16[32,1024]{1,0:T(8,128)(2,1)S(1)}, u32[]{:S(2)}, u32[]{:S(2)}) %collective-permute-start.20) | collective-permute-done | bytes 65568 | tf_op jit(solution)/shard_map/ppermute | solution.py:13
  34.7 0.5 collective-permute-start.19
  35.3 1.6 %collective-permute-start.2 = (bf16[32,4096]{1,0:T(8,128)(2,1)S(1)}, bf16[32,4096]{1,0:T(8,128)(2,1)S(1)}, u32[]{:S(2)}, u32[]{:S(2)}) collective-permute-start(bf16[32,4096]{1,0:T(8,128)(2,1)S(1)} %collective-permute-done.1), channel_id=1, source_target_pairs={{0,8},{2,10},{4,12},{6,14},{8,0},{10,2},{12,4},{14,6},{16,24},{18,... | collective-permute-start | bytes 786440 | tf_op jit(solution)/shard_map/ppermute | solution.py:13
  37.0 2.0 %collective-permute-done.19 = bf16[32,1024]{1,0:T(8,128)(2,1)S(1)} collective-permute-done((bf16[32,1024]{1,0:T(8,128)(2,1)S(1)}, bf16[32,1024]{1,0:T(8,128)(2,1)S(1)}, u32[]{:S(2)}, u32[]{:S(2)}) %collective-permute-start.19) | collective-permute-done | bytes 65568 | tf_op jit(solution)/shard_map/ppermute | solution.py:13
  39.0 0.5 collective-permute-start.5
  39.6 3.4 %collective-permute-done.21 = bf16[128,2048]{1,0:T(8,128)(2,1)S(1)} collective-permute-done((bf16[128,2048]{1,0:T(8,128)(2,1)S(1)}, bf16[128,2048]{1,0:T(8,128)(2,1)S(1)}, u32[]{:S(2)}, u32[]{:S(2)}) %collective-permute-start.21) | collective-permute-done | bytes 524320 | tf_op jit(solution)/shard_map/ppermute | solution.py:96
  43.8 0.5 collective-permute-start.22
  44.9 1.6 %collective-permute-start.23 = (bf16[32,4096]{1,0:T(8,128)(2,1)S(1)}, bf16[32,4096]{1,0:T(8,128)(2,1)S(1)}, u32[]{:S(2)}, u32[]{:S(2)}) collective-permute-start(bf16[32,4096]{1,0:T(8,128)(2,1)S(1)} %get-tuple-element.28), channel_id=1, source_target_pairs={{0,4},{2,6},{4,0},{6,2},{8,12},{10,14},{12,8},{14,10},{16,20},{18,... | collective-permute-start | bytes 786440 | tf_op jit(solution)/shard_map/ppermute | solution.py:13
  46.7 1.2 collective-permute-start.10
  48.1 0.9 collective-permute-start.9
  49.0 4.1 %collective-permute-done.22 = bf16[32,4096]{1,0:T(8,128)(2,1)S(1)} collective-permute-done((bf16[32,4096]{1,0:T(8,128)(2,1)S(1)}, bf16[32,4096]{1,0:T(8,128)(2,1)S(1)}, u32[]{:S(2)}, u32[]{:S(2)}) %collective-permute-start.22) | collective-permute-done | bytes 262176 | tf_op jit(solution)/shard_map/ppermute | solution.py:13
  53.1 5.6 %collective-permute-done.23 = bf16[32,4096]{1,0:T(8,128)(2,1)S(1)} collective-permute-done((bf16[32,4096]{1,0:T(8,128)(2,1)S(1)}, bf16[32,4096]{1,0:T(8,128)(2,1)S(1)}, u32[]{:S(2)}, u32[]{:S(2)}) %collective-permute-start.23) | collective-permute-done | bytes 262176 | tf_op jit(solution)/shard_map/ppermute | solution.py:13
  58.9 5.4 %collective-permute-done.10 = bf16[32,4096]{1,0:T(8,128)(2,1)S(1)} collective-permute-done((bf16[32,4096]{1,0:T(8,128)(2,1)S(1)}, bf16[32,4096]{1,0:T(8,128)(2,1)S(1)}, u32[]{:S(2)}, u32[]{:S(2)}) %collective-permute-start.10) | collective-permute-done | bytes 262176 | tf_op jit(solution)/shard_map/ppermute | solution.py:13
  64.9 3.5 %collective-permute-done.9 = bf16[32,4096]{1,0:T(8,128)(2,1)S(1)} collective-permute-done((bf16[32,4096]{1,0:T(8,128)(2,1)S(1)}, bf16[32,4096]{1,0:T(8,128)(2,1)S(1)}, u32[]{:S(2)}, u32[]{:S(2)}) %collective-permute-start.9) | collective-permute-done | bytes 262176 | tf_op jit(solution)/shard_map/ppermute | solution.py:13
  69.0 1.6 %collective-permute-start.11 = (f32[32,256]{1,0:T(8,128)S(1)}, f32[32,256]{1,0:T(8,128)S(1)}, u32[]{:S(2)}, u32[]{:S(2)}) collective-permute-start(f32[32,256]{1,0:T(8,128)S(1)} %pad_maximum_fusion.2), channel_id=1, source_target_pairs={{0,1},{1,0},{2,3},{3,2},{4,5},{5,4},{6,7},{7,6},{8,9},{9,8},{10,11... | collective-permute-start | bytes 98312 | tf_op jit(solution)/shard_map/ppermute | solution.py:135
  72.0 1.6 %collective-permute-start.29 = (bf16[32,4096]{1,0:T(8,128)(2,1)S(1)}, bf16[32,4096]{1,0:T(8,128)(2,1)S(1)}, u32[]{:S(2)}, u32[]{:S(2)}) collective-permute-start(bf16[32,4096]{1,0:T(8,128)(2,1)S(1)} %get-tuple-element.9), channel_id=1, source_target_pairs={{0,8},{2,10},{4,12},{6,14},{8,0},{10,2},{12,4},{14,6},{16,24},{18,... | collective-permute-start | bytes 786440 | tf_op jit(solution)/shard_map/ppermute | solution.py:13
  74.3 0.6 collective-permute-start.31
  75.0 1.5 %collective-permute-start.32 = (bf16[32,512]{1,0:T(8,128)(2,1)S(1)}, bf16[32,512]{1,0:T(8,128)(2,1)S(1)}, u32[]{:S(2)}, u32[]{:S(2)}) collective-permute-start(bf16[32,512]{1,0:T(8,128)(2,1)S(1)} %fusion.101), channel_id=1, source_target_pairs={{0,4},{2,6},{4,0},{6,2},{8,12},{10,14},{12,8},{14,10},{16,20},{18,... | collective-permute-start | bytes 98312 | tf_op jit(solution)/shard_map/ppermute | solution.py:13
  76.5 18.3 %fusion = bf16[256,4096]{1,0:T(8,128)(2,1)} fusion(bf16[256,2048]{1,0:T(8,128)(2,1)S(1)} %maximum_select_fusion, bf16[4096,2048]{1,0:T(8,128)(2,1)} %param.7, f32[128,4096]{1,0:T(8,128)S(1)} %fusion.113, f32[128,4096]{1,0:T(8,128)S(1)} %fusion.112), kind=kOutput, calls=%fused_computation.1 | convolution fusion | flops 4299161600 | bytes 24117248 | tf_op jit(solution)/shard_map/dot_general | solution.py:17
  95.0 0.6 collective-permute-start.36
  95.6 0.6 collective-permute-done.37
  96.3 1.0 collective-permute-done.34
  97.4 0.7 collective-permute-start.38
  98.1 1.6 %collective-permute-start = (bf16[128,2048]{1,0:T(8,128)(2,1)S(1)}, bf16[128,2048]{1,0:T(8,128)(2,1)S(1)}, u32[]{:S(2)}, u32[]{:S(2)}) collective-permute-start(bf16[128,2048]{1,0:T(8,128)(2,1)S(1)} %dynamic-slice_convert_fusion), channel_id=1, source_target_pairs={{0,1},{1,0},{2,3},{3,2},{4,5},{5,4},{6,7},{7,6},{8,9},{9,8},{10,11... | collective-permute-start | bytes 1572872 | tf_op jit(solution)/shard_map/ppermute | solution.py:123
  99.7 1.6 %collective-permute-done.38 = bf16[32,512]{1,0:T(8,128)(2,1)S(1)} collective-permute-done((bf16[32,512]{1,0:T(8,128)(2,1)S(1)}, bf16[32,512]{1,0:T(8,128)(2,1)S(1)}, u32[]{:S(2)}, u32[]{:S(2)}) %collective-permute-start.38) | collective-permute-done | bytes 32800 | tf_op jit(solution)/shard_map/ppermute | solution.py:13
  101.3 0.7 collective-permute-start.35
  102.1 2.7 %collective-permute-start.39 = (bf16[32,512]{1,0:T(8,128)(2,1)S(1)}, bf16[32,512]{1,0:T(8,128)(2,1)S(1)}, u32[]{:S(2)}, u32[]{:S(2)}) collective-permute-start(bf16[32,512]{1,0:T(8,128)(2,1)S(1)} %fusion.72), channel_id=1, source_target_pairs={{0,16},{2,18},{4,20},{6,22},{8,24},{10,26},{12,28},{14,30},{16,0},... | collective-permute-start | bytes 98312 | tf_op jit(solution)/shard_map/ppermute | solution.py:13
  104.8 0.5 fusion.15
  105.7 6.2 %collective-permute-done = bf16[128,2048]{1,0:T(8,128)(2,1)S(1)} collective-permute-done((bf16[128,2048]{1,0:T(8,128)(2,1)S(1)}, bf16[128,2048]{1,0:T(8,128)(2,1)S(1)}, u32[]{:S(2)}, u32[]{:S(2)}) %collective-permute-start) | collective-permute-done | bytes 524320 | tf_op jit(solution)/shard_map/ppermute | solution.py:123
  111.9 1.3 %collective-permute-start.26 = (bf16[32,4096]{1,0:T(8,128)(2,1)S(1)}, bf16[32,4096]{1,0:T(8,128)(2,1)S(1)}, u32[]{:S(2)}, u32[]{:S(2)}) collective-permute-start(bf16[32,4096]{1,0:T(8,128)(2,1)S(1)} %get-tuple-element.5), channel_id=1, source_target_pairs={{0,8},{2,10},{4,12},{6,14},{8,0},{10,2},{12,4},{14,6},{16,24},{18,... | collective-permute-start | bytes 786440 | tf_op jit(solution)/shard_map/ppermute | solution.py:13
  113.2 1.1 add_convert_fusion
  114.4 0.7 fusion.57
  115.0 5.3 %collective-permute-done.30 = bf16[32,4096]{1,0:T(8,128)(2,1)S(1)} collective-permute-done((bf16[32,4096]{1,0:T(8,128)(2,1)S(1)}, bf16[32,4096]{1,0:T(8,128)(2,1)S(1)}, u32[]{:S(2)}, u32[]{:S(2)}) %collective-permute-start.30) | collective-permute-done | bytes 262176 | tf_op jit(solution)/shard_map/ppermute | solution.py:13
  120.3 3.5 %collective-permute-done.26 = bf16[32,4096]{1,0:T(8,128)(2,1)S(1)} collective-permute-done((bf16[32,4096]{1,0:T(8,128)(2,1)S(1)}, bf16[32,4096]{1,0:T(8,128)(2,1)S(1)}, u32[]{:S(2)}, u32[]{:S(2)}) %collective-permute-start.26) | collective-permute-done | bytes 262176 | tf_op jit(solution)/shard_map/ppermute | solution.py:13
  123.9 1.1 fusion.12
  (89 shorter events, 7.0 us)
Async XLA Ops:
  0.6 21.2 %collective-permute-start.12 = (bf16[32,1024]{1,0:T(8,128)(2,1)}, bf16[32,1024]{1,0:T(8,128)(2,1)S(1)}, u32[]{:S(2)}, u32[]{:S(2)}) collective-permute-start(bf16[32,1024]{1,0:T(8,128)(2,1)} %bitcast.37), channel_id=1, source_target_pairs={{0,16},{2,18},{4,20},{6,22},{8,24},{10,26},{12,28},{14,30},{16,0},... | collective-permute-start | bytes 196616 | tf_op jit(solution)/shard_map/ppermute | solution.py:13
  4.7 19.6 %collective-permute-start.15 = (bf16[32,1024]{1,0:T(8,128)(2,1)}, bf16[32,1024]{1,0:T(8,128)(2,1)S(1)}, u32[]{:S(2)}, u32[]{:S(2)}) collective-permute-start(bf16[32,1024]{1,0:T(8,128)(2,1)} %bitcast.38), channel_id=1, source_target_pairs={{0,8},{2,10},{4,12},{6,14},{8,0},{10,2},{12,4},{14,6},{16,24},{18,... | collective-permute-start | bytes 196616 | tf_op jit(solution)/shard_map/ppermute | solution.py:13
  6.3 21.7 %collective-permute-start.18 = (bf16[32,1024]{1,0:T(8,128)(2,1)}, bf16[32,1024]{1,0:T(8,128)(2,1)S(1)}, u32[]{:S(2)}, u32[]{:S(2)}) collective-permute-start(bf16[32,1024]{1,0:T(8,128)(2,1)} %bitcast.39), channel_id=1, source_target_pairs={{0,2},{2,0},{4,6},{6,4},{8,10},{10,8},{12,14},{14,12},{16,18},{18,... | collective-permute-start | bytes 196616 | tf_op jit(solution)/shard_map/ppermute | solution.py:13
  6.3 17.9 %collective-permute-start.8 = (s32[2,1]{0,1:T(1,128)}, s32[2,1]{0,1:T(1,128)S(1)}, u32[]{:S(2)}, u32[]{:S(2)}) collective-permute-start(s32[2,1]{0,1:T(1,128)} %param.10), channel_id=1, source_target_pairs={{0,4},{2,6},{4,0},{6,2},{8,12},{10,14},{12,8},{14,10},{16,20},{18,... | collective-permute-start | bytes 32 | tf_op jit(solution)/shard_map/ppermute | solution.py:13
  7.8 27.5 %collective-permute-start.1 = (bf16[32,4096]{1,0:T(8,128)(2,1)}, bf16[32,4096]{1,0:T(8,128)(2,1)S(1)}, u32[]{:S(2)}, u32[]{:S(2)}) collective-permute-start(bf16[32,4096]{1,0:T(8,128)(2,1)} %bitcast.34), channel_id=1, source_target_pairs={{0,16},{2,18},{4,20},{6,22},{8,24},{10,26},{12,28},{14,30},{16,0},... | collective-permute-start | bytes 786440 | tf_op jit(solution)/shard_map/ppermute | solution.py:13
  8.1 14.2 %copy-start.5 = (s32[2,1]{0,1:T(1,128)S(1)}, s32[2,1]{0,1:T(1,128)}, u32[]{:S(2)}) copy-start(s32[2,1]{0,1:T(1,128)} %param.10) | copy-start | bytes 28
  8.1 19.9 %copy-start.1 = (bf16[1,4096,32]{1,2,0:T(8,128)(2,1)S(1)}, bf16[1,4096,32]{1,2,0:T(8,128)(2,1)}, u32[]{:S(2)}) copy-start(bf16[1,4096,32]{1,2,0:T(8,128)(2,1)} %param.8) | copy-start | bytes 786436
  8.1 20.7 %copy-start.3 = (bf16[128,2048]{1,0:T(8,128)(2,1)S(1)}, bf16[128,2048]{1,0:T(8,128)(2,1)}, u32[]{:S(2)}) copy-start(bf16[128,2048]{1,0:T(8,128)(2,1)} %param.11) | copy-start | bytes 1572868
  8.1 22.2 %copy-start.2 = (bf16[1,32,1024]{2,1,0:T(8,128)(2,1)S(1)}, bf16[1,32,1024]{2,1,0:T(8,128)(2,1)}, u32[]{:S(2)}) copy-start(bf16[1,32,1024]{2,1,0:T(8,128)(2,1)} %param.9) | copy-start | bytes 196612
  21.8 4.3 %collective-permute-start.13 = (bf16[32,1024]{1,0:T(8,128)(2,1)S(1)}, bf16[32,1024]{1,0:T(8,128)(2,1)S(1)}, u32[]{:S(2)}, u32[]{:S(2)}) collective-permute-start(bf16[32,1024]{1,0:T(8,128)(2,1)S(1)} %collective-permute-done.12), channel_id=1, source_target_pairs={{0,8},{2,10},{4,12},{6,14},{8,0},{10,2},{12,4},{14,6},{16,24},{18,... | collective-permute-start | bytes 196616 | tf_op jit(solution)/shard_map/ppermute | solution.py:13
  24.3 4.6 %collective-permute-start.17 = (bf16[32,1024]{1,0:T(8,128)(2,1)S(1)}, bf16[32,1024]{1,0:T(8,128)(2,1)S(1)}, u32[]{:S(2)}, u32[]{:S(2)}) collective-permute-start(bf16[32,1024]{1,0:T(8,128)(2,1)S(1)} %collective-permute-done.12), channel_id=1, source_target_pairs={{0,2},{2,0},{4,6},{6,4},{8,10},{10,8},{12,14},{14,12},{16,18},{18,... | collective-permute-start | bytes 196616 | tf_op jit(solution)/shard_map/ppermute | solution.py:13
  24.3 4.2 %collective-permute-start.16 = (bf16[32,1024]{1,0:T(8,128)(2,1)S(1)}, bf16[32,1024]{1,0:T(8,128)(2,1)S(1)}, u32[]{:S(2)}, u32[]{:S(2)}) collective-permute-start(bf16[32,1024]{1,0:T(8,128)(2,1)S(1)} %collective-permute-done.15), channel_id=1, source_target_pairs={{0,2},{2,0},{4,6},{6,4},{8,10},{10,8},{12,14},{14,12},{16,18},{18,... | collective-permute-start | bytes 196616 | tf_op jit(solution)/shard_map/ppermute | solution.py:13
  26.1 4.2 %collective-permute-start.14 = (bf16[32,1024]{1,0:T(8,128)(2,1)S(1)}, bf16[32,1024]{1,0:T(8,128)(2,1)S(1)}, u32[]{:S(2)}, u32[]{:S(2)}) collective-permute-start(bf16[32,1024]{1,0:T(8,128)(2,1)S(1)} %collective-permute-done.13), channel_id=1, source_target_pairs={{0,2},{2,0},{4,6},{6,4},{8,10},{10,8},{12,14},{14,12},{16,18},{18,... | collective-permute-start | bytes 196616 | tf_op jit(solution)/shard_map/ppermute | solution.py:13
  28.1 10.9 %collective-permute-start.4 = (bf16[32,4096]{1,0:T(8,128)(2,1)S(1)}, bf16[32,4096]{1,0:T(8,128)(2,1)S(1)}, u32[]{:S(2)}, u32[]{:S(2)}) collective-permute-start(bf16[32,4096]{1,0:T(8,128)(2,1)S(1)} %bitcast.35), channel_id=1, source_target_pairs={{0,8},{2,10},{4,12},{6,14},{8,0},{10,2},{12,4},{14,6},{16,24},{18,... | collective-permute-start | bytes 786440 | tf_op jit(solution)/shard_map/ppermute | solution.py:13
  28.6 16.3 %collective-permute-start.7 = (bf16[32,4096]{1,0:T(8,128)(2,1)S(1)}, bf16[32,4096]{1,0:T(8,128)(2,1)S(1)}, u32[]{:S(2)}, u32[]{:S(2)}) collective-permute-start(bf16[32,4096]{1,0:T(8,128)(2,1)S(1)} %bitcast.36), channel_id=1, source_target_pairs={{0,2},{2,0},{4,6},{6,4},{8,10},{10,8},{12,14},{14,12},{16,18},{18,... | collective-permute-start | bytes 786440 | tf_op jit(solution)/shard_map/ppermute | solution.py:13
  28.8 14.1 %collective-permute-start.21 = (bf16[128,2048]{1,0:T(8,128)(2,1)S(1)}, bf16[128,2048]{1,0:T(8,128)(2,1)S(1)}, u32[]{:S(2)}, u32[]{:S(2)}) collective-permute-start(bf16[128,2048]{1,0:T(8,128)(2,1)S(1)} %copy-done.3), channel_id=1, source_target_pairs={{0,1},{1,0},{2,3},{3,2},{4,5},{5,4},{6,7},{7,6},{8,9},{9,8},{10,11... | collective-permute-start | bytes 1572872 | tf_op jit(solution)/shard_map/ppermute | solution.py:96
  30.4 4.3 %collective-permute-start.20 = (bf16[32,1024]{1,0:T(8,128)(2,1)S(1)}, bf16[32,1024]{1,0:T(8,128)(2,1)S(1)}, u32[]{:S(2)}, u32[]{:S(2)}) collective-permute-start(bf16[32,1024]{1,0:T(8,128)(2,1)S(1)} %select_select_fusion.4), channel_id=1, source_target_pairs={{0,4},{2,6},{4,0},{6,2},{8,12},{10,14},{12,8},{14,10},{16,20},{18,... | collective-permute-start | bytes 196616 | tf_op jit(solution)/shard_map/ppermute | solution.py:13
  34.7 4.3 %collective-permute-start.19 = (bf16[32,1024]{1,0:T(8,128)(2,1)S(1)}, bf16[32,1024]{1,0:T(8,128)(2,1)S(1)}, u32[]{:S(2)}, u32[]{:S(2)}) collective-permute-start(bf16[32,1024]{1,0:T(8,128)(2,1)S(1)} %select_select_fusion.6), channel_id=1, source_target_pairs={{0,4},{2,6},{4,0},{6,2},{8,12},{10,14},{12,8},{14,10},{16,20},{18,... | collective-permute-start | bytes 196616 | tf_op jit(solution)/shard_map/ppermute | solution.py:13
  35.3 8.2 %copy-start = (bf16[256,4096]{1,0:T(8,128)(2,1)S(1)}, bf16[256,4096]{1,0:T(8,128)(2,1)}, u32[]{:S(2)}) copy-start(bf16[256,4096]{1,0:T(8,128)(2,1)} %param.6) | copy-start | bytes 6291460
  35.3 9.2 %collective-permute-start.2 = (bf16[32,4096]{1,0:T(8,128)(2,1)S(1)}, bf16[32,4096]{1,0:T(8,128)(2,1)S(1)}, u32[]{:S(2)}, u32[]{:S(2)}) collective-permute-start(bf16[32,4096]{1,0:T(8,128)(2,1)S(1)} %collective-permute-done.1), channel_id=1, source_target_pairs={{0,8},{2,10},{4,12},{6,14},{8,0},{10,2},{12,4},{14,6},{16,24},{18,... | collective-permute-start | bytes 786440 | tf_op jit(solution)/shard_map/ppermute | solution.py:13
  39.0 7.6 %collective-permute-start.6 = (bf16[32,4096]{1,0:T(8,128)(2,1)S(1)}, bf16[32,4096]{1,0:T(8,128)(2,1)S(1)}, u32[]{:S(2)}, u32[]{:S(2)}) collective-permute-start(bf16[32,4096]{1,0:T(8,128)(2,1)S(1)} %collective-permute-done.1), channel_id=1, source_target_pairs={{0,2},{2,0},{4,6},{6,4},{8,10},{10,8},{12,14},{14,12},{16,18},{18,... | collective-permute-start | bytes 786440 | tf_op jit(solution)/shard_map/ppermute | solution.py:13
  39.0 7.6 %collective-permute-start.5 = (bf16[32,4096]{1,0:T(8,128)(2,1)S(1)}, bf16[32,4096]{1,0:T(8,128)(2,1)S(1)}, u32[]{:S(2)}, u32[]{:S(2)}) collective-permute-start(bf16[32,4096]{1,0:T(8,128)(2,1)S(1)} %collective-permute-done.4), channel_id=1, source_target_pairs={{0,2},{2,0},{4,6},{6,4},{8,10},{10,8},{12,14},{14,12},{16,18},{18,... | collective-permute-start | bytes 786440 | tf_op jit(solution)/shard_map/ppermute | solution.py:13
  43.8 9.3 %collective-permute-start.22 = (bf16[32,4096]{1,0:T(8,128)(2,1)S(1)}, bf16[32,4096]{1,0:T(8,128)(2,1)S(1)}, u32[]{:S(2)}, u32[]{:S(2)}) collective-permute-start(bf16[32,4096]{1,0:T(8,128)(2,1)S(1)} %get-tuple-element.26), channel_id=1, source_target_pairs={{0,4},{2,6},{4,0},{6,2},{8,12},{10,14},{12,8},{14,10},{16,20},{18,... | collective-permute-start | bytes 786440 | tf_op jit(solution)/shard_map/ppermute | solution.py:13
  44.6 2.0 %collective-permute-start.3 = (bf16[32,4096]{1,0:T(8,128)(2,1)S(1)}, bf16[32,4096]{1,0:T(8,128)(2,1)S(1)}, u32[]{:S(2)}, u32[]{:S(2)}) collective-permute-start(bf16[32,4096]{1,0:T(8,128)(2,1)S(1)} %collective-permute-done.2), channel_id=1, source_target_pairs={{0,2},{2,0},{4,6},{6,4},{8,10},{10,8},{12,14},{14,12},{16,18},{18,... | collective-permute-start | bytes 786440 | tf_op jit(solution)/shard_map/ppermute | solution.py:13
  44.9 13.8 %collective-permute-start.23 = (bf16[32,4096]{1,0:T(8,128)(2,1)S(1)}, bf16[32,4096]{1,0:T(8,128)(2,1)S(1)}, u32[]{:S(2)}, u32[]{:S(2)}) collective-permute-start(bf16[32,4096]{1,0:T(8,128)(2,1)S(1)} %get-tuple-element.28), channel_id=1, source_target_pairs={{0,4},{2,6},{4,0},{6,2},{8,12},{10,14},{12,8},{14,10},{16,20},{18,... | collective-permute-start | bytes 786440 | tf_op jit(solution)/shard_map/ppermute | solution.py:13
  46.7 17.6 %collective-permute-start.10 = (bf16[32,4096]{1,0:T(8,128)(2,1)S(1)}, bf16[32,4096]{1,0:T(8,128)(2,1)S(1)}, u32[]{:S(2)}, u32[]{:S(2)}) collective-permute-start(bf16[32,4096]{1,0:T(8,128)(2,1)S(1)} %select_select_fusion), channel_id=1, source_target_pairs={{0,4},{2,6},{4,0},{6,2},{8,12},{10,14},{12,8},{14,10},{16,20},{18,... | collective-permute-start | bytes 786440 | tf_op jit(solution)/shard_map/ppermute | solution.py:13
  48.1 20.3 %collective-permute-start.9 = (bf16[32,4096]{1,0:T(8,128)(2,1)S(1)}, bf16[32,4096]{1,0:T(8,128)(2,1)S(1)}, u32[]{:S(2)}, u32[]{:S(2)}) collective-permute-start(bf16[32,4096]{1,0:T(8,128)(2,1)S(1)} %select_select_fusion.2), channel_id=1, source_target_pairs={{0,4},{2,6},{4,0},{6,2},{8,12},{10,14},{12,8},{14,10},{16,20},{18,... | collective-permute-start | bytes 786440 | tf_op jit(solution)/shard_map/ppermute | solution.py:13
  58.9 12.2 %collective-permute-start.28 = (bf16[32,4096]{1,0:T(8,128)(2,1)S(1)}, bf16[32,4096]{1,0:T(8,128)(2,1)S(1)}, u32[]{:S(2)}, u32[]{:S(2)}) collective-permute-start(bf16[32,4096]{1,0:T(8,128)(2,1)S(1)} %fusion.37), channel_id=1, source_target_pairs={{0,2},{2,0},{4,6},{6,4},{8,10},{10,8},{12,14},{14,12},{16,18},{18,... | collective-permute-start | bytes 786440 | tf_op jit(solution)/shard_map/ppermute | solution.py:13
  69.0 4.9 %collective-permute-start.11 = (f32[32,256]{1,0:T(8,128)S(1)}, f32[32,256]{1,0:T(8,128)S(1)}, u32[]{:S(2)}, u32[]{:S(2)}) collective-permute-start(f32[32,256]{1,0:T(8,128)S(1)} %pad_maximum_fusion.2), channel_id=1, source_target_pairs={{0,1},{1,0},{2,3},{3,2},{4,5},{5,4},{6,7},{7,6},{8,9},{9,8},{10,11... | collective-permute-start | bytes 98312 | tf_op jit(solution)/shard_map/ppermute | solution.py:135
  72.0 30.1 %collective-permute-start.25 = (bf16[32,4096]{1,0:T(8,128)(2,1)S(1)}, bf16[32,4096]{1,0:T(8,128)(2,1)S(1)}, u32[]{:S(2)}, u32[]{:S(2)}) collective-permute-start(bf16[32,4096]{1,0:T(8,128)(2,1)S(1)} %get-tuple-element.7), channel_id=1, source_target_pairs={{0,2},{2,0},{4,6},{6,4},{8,10},{10,8},{12,14},{14,12},{16,18},{18,... | collective-permute-start | bytes 786440 | tf_op jit(solution)/shard_map/ppermute | solution.py:13
  72.0 30.1 %collective-permute-start.29 = (bf16[32,4096]{1,0:T(8,128)(2,1)S(1)}, bf16[32,4096]{1,0:T(8,128)(2,1)S(1)}, u32[]{:S(2)}, u32[]{:S(2)}) collective-permute-start(bf16[32,4096]{1,0:T(8,128)(2,1)S(1)} %get-tuple-element.9), channel_id=1, source_target_pairs={{0,8},{2,10},{4,12},{6,14},{8,0},{10,2},{12,4},{14,6},{16,24},{18,... | collective-permute-start | bytes 786440 | tf_op jit(solution)/shard_map/ppermute | solution.py:13
  73.7 31.1 %collective-permute-start.27 = (bf16[32,4096]{1,0:T(8,128)(2,1)S(1)}, bf16[32,4096]{1,0:T(8,128)(2,1)S(1)}, u32[]{:S(2)}, u32[]{:S(2)}) collective-permute-start(bf16[32,4096]{1,0:T(8,128)(2,1)S(1)} %get-tuple-element.8), channel_id=1, source_target_pairs={{0,2},{2,0},{4,6},{6,4},{8,10},{10,8},{12,14},{14,12},{16,18},{18,... | collective-permute-start | bytes 786440 | tf_op jit(solution)/shard_map/ppermute | solution.py:13
  74.3 20.5 %collective-permute-start.31 = (bf16[32,512]{1,0:T(8,128)(2,1)S(1)}, bf16[32,512]{1,0:T(8,128)(2,1)S(1)}, u32[]{:S(2)}, u32[]{:S(2)}) collective-permute-start(bf16[32,512]{1,0:T(8,128)(2,1)S(1)} %fusion.102), channel_id=1, source_target_pairs={{0,4},{2,6},{4,0},{6,2},{8,12},{10,14},{12,8},{14,10},{16,20},{18,... | collective-permute-start | bytes 98312 | tf_op jit(solution)/shard_map/ppermute | solution.py:13
  75.0 19.8 %collective-permute-start.32 = (bf16[32,512]{1,0:T(8,128)(2,1)S(1)}, bf16[32,512]{1,0:T(8,128)(2,1)S(1)}, u32[]{:S(2)}, u32[]{:S(2)}) collective-permute-start(bf16[32,512]{1,0:T(8,128)(2,1)S(1)} %fusion.101), channel_id=1, source_target_pairs={{0,4},{2,6},{4,0},{6,2},{8,12},{10,14},{12,8},{14,10},{16,20},{18,... | collective-permute-start | bytes 98312 | tf_op jit(solution)/shard_map/ppermute | solution.py:13
  94.9 18.4 %copy-start.4 = (f32[256,2048]{1,0:T(8,128)S(1)}, f32[256,2048]{1,0:T(8,128)}, u32[]{:S(2)}) copy-start(f32[256,2048]{1,0:T(8,128)} %fusion.111) | copy-start | bytes 6291460
  94.9 1.3 %collective-permute-start.37 = (bf16[32,512]{1,0:T(8,128)(2,1)S(1)}, bf16[32,512]{1,0:T(8,128)(2,1)S(1)}, u32[]{:S(2)}, u32[]{:S(2)}) collective-permute-start(bf16[32,512]{1,0:T(8,128)(2,1)S(1)} %fusion.82), channel_id=1, source_target_pairs={{0,2},{2,0},{4,6},{6,4},{8,10},{10,8},{12,14},{14,12},{16,18},{18,... | collective-permute-start | bytes 98312 | tf_op jit(solution)/shard_map/ppermute | solution.py:13
  95.0 3.1 %collective-permute-start.36 = (bf16[32,512]{1,0:T(8,128)(2,1)S(1)}, bf16[32,512]{1,0:T(8,128)(2,1)S(1)}, u32[]{:S(2)}, u32[]{:S(2)}) collective-permute-start(bf16[32,512]{1,0:T(8,128)(2,1)S(1)} %get-tuple-element.17), channel_id=1, source_target_pairs={{0,2},{2,0},{4,6},{6,4},{8,10},{10,8},{12,14},{14,12},{16,18},{18,... | collective-permute-start | bytes 98312 | tf_op jit(solution)/shard_map/ppermute | solution.py:13
  96.1 1.2 collective-permute-start.34
  97.4 3.9 %collective-permute-start.38 = (bf16[32,512]{1,0:T(8,128)(2,1)S(1)}, bf16[32,512]{1,0:T(8,128)(2,1)S(1)}, u32[]{:S(2)}, u32[]{:S(2)}) collective-permute-start(bf16[32,512]{1,0:T(8,128)(2,1)S(1)} %fusion.79), channel_id=1, source_target_pairs={{0,8},{2,10},{4,12},{6,14},{8,0},{10,2},{12,4},{14,6},{16,24},{18,... | collective-permute-start | bytes 98312 | tf_op jit(solution)/shard_map/ppermute | solution.py:13
  98.1 13.8 %collective-permute-start = (bf16[128,2048]{1,0:T(8,128)(2,1)S(1)}, bf16[128,2048]{1,0:T(8,128)(2,1)S(1)}, u32[]{:S(2)}, u32[]{:S(2)}) collective-permute-start(bf16[128,2048]{1,0:T(8,128)(2,1)S(1)} %dynamic-slice_convert_fusion), channel_id=1, source_target_pairs={{0,1},{1,0},{2,3},{3,2},{4,5},{5,4},{6,7},{7,6},{8,9},{9,8},{10,11... | collective-permute-start | bytes 1572872 | tf_op jit(solution)/shard_map/ppermute | solution.py:123
  101.3 12.0 %collective-permute-start.35 = (bf16[32,512]{1,0:T(8,128)(2,1)S(1)}, bf16[32,512]{1,0:T(8,128)(2,1)S(1)}, u32[]{:S(2)}, u32[]{:S(2)}) collective-permute-start(bf16[32,512]{1,0:T(8,128)(2,1)S(1)} %get-tuple-element.15), channel_id=1, source_target_pairs={{0,8},{2,10},{4,12},{6,14},{8,0},{10,2},{12,4},{14,6},{16,24},{18,... | collective-permute-start | bytes 98312 | tf_op jit(solution)/shard_map/ppermute | solution.py:13
  102.0 12.4 %collective-permute-start.33 = (bf16[32,512]{1,0:T(8,128)(2,1)S(1)}, bf16[32,512]{1,0:T(8,128)(2,1)S(1)}, u32[]{:S(2)}, u32[]{:S(2)}) collective-permute-start(bf16[32,512]{1,0:T(8,128)(2,1)S(1)} %get-tuple-element.14), channel_id=1, source_target_pairs={{0,2},{2,0},{4,6},{6,4},{8,10},{10,8},{12,14},{14,12},{16,18},{18,... | collective-permute-start | bytes 98312 | tf_op jit(solution)/shard_map/ppermute | solution.py:13
  102.1 12.3 %collective-permute-start.39 = (bf16[32,512]{1,0:T(8,128)(2,1)S(1)}, bf16[32,512]{1,0:T(8,128)(2,1)S(1)}, u32[]{:S(2)}, u32[]{:S(2)}) collective-permute-start(bf16[32,512]{1,0:T(8,128)(2,1)S(1)} %fusion.72), channel_id=1, source_target_pairs={{0,16},{2,18},{4,20},{6,22},{8,24},{10,26},{12,28},{14,30},{16,0},... | collective-permute-start | bytes 98312 | tf_op jit(solution)/shard_map/ppermute | solution.py:13
  105.3 15.1 %collective-permute-start.30 = (bf16[32,4096]{1,0:T(8,128)(2,1)S(1)}, bf16[32,4096]{1,0:T(8,128)(2,1)S(1)}, u32[]{:S(2)}, u32[]{:S(2)}) collective-permute-start(bf16[32,4096]{1,0:T(8,128)(2,1)S(1)} %get-tuple-element.6), channel_id=1, source_target_pairs={{0,16},{2,18},{4,20},{6,22},{8,24},{10,26},{12,28},{14,30},{16,0},... | collective-permute-start | bytes 786440 | tf_op jit(solution)/shard_map/ppermute | solution.py:13
  111.9 12.0 %collective-permute-start.26 = (bf16[32,4096]{1,0:T(8,128)(2,1)S(1)}, bf16[32,4096]{1,0:T(8,128)(2,1)S(1)}, u32[]{:S(2)}, u32[]{:S(2)}) collective-permute-start(bf16[32,4096]{1,0:T(8,128)(2,1)S(1)} %get-tuple-element.5), channel_id=1, source_target_pairs={{0,8},{2,10},{4,12},{6,14},{8,0},{10,2},{12,4},{14,6},{16,24},{18,... | collective-permute-start | bytes 786440 | tf_op jit(solution)/shard_map/ppermute | solution.py:13
  113.2 10.6 %collective-permute-start.24 = (bf16[32,4096]{1,0:T(8,128)(2,1)S(1)}, bf16[32,4096]{1,0:T(8,128)(2,1)S(1)}, u32[]{:S(2)}, u32[]{:S(2)}) collective-permute-start(bf16[32,4096]{1,0:T(8,128)(2,1)S(1)} %get-tuple-element.4), channel_id=1, source_target_pairs={{0,2},{2,0},{4,6},{6,4},{8,10},{10,8},{12,14},{14,12},{16,18},{18,... | collective-permute-start | bytes 786440 | tf_op jit(solution)/shard_map/ppermute | solution.py:13

commit v2 on v1

v2 whole, which is shorter than its diff:
```python
import jax
import jax.numpy as jnp
from jax import lax
from jax.sharding import PartitionSpec as P

adapter_scale = 0.5
f32 = jnp.float32
bf16 = jnp.bfloat16
core, far = 1, 2


def swap(value, offset):
    count = lax.axis_size("blk")
    return lax.ppermute(value, "blk", [(i, i ^ offset) for i in range(count)])


def cross(value):
    return lax.ppermute(value, "tp", [(0, 1), (1, 0)])


def dot(a, b, contract):
    return lax.dot_general(a, b, ((contract[:1], contract[1:]), ((), ())), preferred_element_type=f32)


def pick(blocks, hits):
    out = jnp.where(hits[0], blocks[0], jnp.zeros_like(blocks[0]))
    for block, hit in zip(blocks[1:], hits[1:]):
        out = jnp.where(hit, block, out)
    return out


def blend(blocks, hits):
    out = jnp.zeros(blocks[0].shape, f32)
    for block, hit in zip(blocks, hits):
        out = out + jnp.where(hit, block.astype(f32), 0.0)
    return out


def after(value, *others):
    return lax.optimization_barrier((value,) + others)[0]


def plan(me, tile_map, map_far, places, rank):
    stacked = tile_map.shape[0] * rank
    shape = (stacked, len(places) * rank)
    tile, lane = lax.broadcasted_iota(jnp.int32, shape, 0), lax.broadcasted_iota(jnp.int32, shape, 1)
    same_row = tile % rank == lane % rank
    place = jnp.zeros(shape, jnp.int32)
    for i, o in enumerate(places):
        place = jnp.where(lane // rank == i, o, place)
    near, away = [
        jnp.broadcast_to((m ^ me)[:, :, None], (m.shape[0], rank, 1)).reshape(stacked, 1)
        for m in (tile_map, map_far)
    ]
    routes = [
        (same_row & (wanted == (place | side))).astype(bf16) for wanted in (near, away) for side in (0, core)
    ]
    square = (stacked, stacked)
    same = lax.broadcasted_iota(jnp.int32, square, 0) == lax.broadcasted_iota(jnp.int32, square, 1)
    return routes + [(same & ((near & far) != 0)).astype(bf16)]


def on_device(tokens, weight, bank_a, bank_b, tile_map, grad_out):
    blk_count = lax.axis_size("blk")
    tp_count = lax.axis_size("tp")
    me = lax.axis_index("blk")
    col = lax.axis_index("tp")
    offsets = list(range(0, blk_count, 4))
    bits = list(range(2, blk_count.bit_length() - 1))
    c_parts = 2

    rows = tokens.shape[0]
    features = tokens.shape[1]
    tile_count = tile_map.shape[0]
    tile_rows = rows // tile_count
    rank_two = bank_a.shape[2]
    rank_one = rank_two // 2
    kv_width = bank_b.shape[2]
    kv_dev = kv_width // tp_count
    local_rows = rows // tp_count
    stacked = tile_count * rank_two

    own_a = bank_a[0].T
    own_b = bank_b[0]
    map_far = swap(tile_map, far)
    keep = (
        lax.broadcasted_iota(jnp.int32, (stacked, rows), 0) // rank_two
        == lax.broadcasted_iota(jnp.int32, (stacked, rows), 1) // tile_rows
    )

    def split(value, count=rank_two):
        return [value[i : i + count] for i in range(0, value.shape[0], count)]

    places = [0]
    for bit in reversed(bits):
        places = places + [o | 1 << bit for o in places]

    def joined_hops(own):
        blocks, hops = own, []
        for bit in reversed(bits):
            more = swap(blocks, 1 << bit)
            hops.append(more)
            blocks = jnp.concatenate([blocks, more], axis=0)
        return blocks, hops

    def give_away(here, there):
        return (dot(far_here, here, (1, 0)) + dot(far_there, there, (1, 0))).astype(bf16)

    def take_in(here, there, got):
        return (
            dot(near_here, here, (1, 0)) + dot(near_there, there, (1, 0)) + dot(from_far, got, (1, 0))
        ).astype(bf16)

    def sums(sent, got, back):
        kept = dot(near_here, sent, (0, 0)) + dot(far_here, got, (0, 0)) + back.astype(f32)
        return dict(zip(places, split(kept)))

    def core_part(sent, got):
        return (dot(near_there, sent, (0, 0)) + dot(far_there, got, (0, 0))).astype(bf16)

    def leaving(total, bit):
        return jnp.concatenate([total[o].astype(bf16) for o in total if o >> bit & 1], axis=0)

    def add_hop(total, came, bit):
        gone = [o for o in total if o >> bit & 1]
        return {
            o ^ 1 << bit: total[o ^ 1 << bit] + c.astype(f32) for o, c in zip(gone, split(came))
        }

    if tp_count == 2:
        other = cross(grad_out)
        grad_rows = jnp.where(
            col == 0,
            jnp.concatenate([grad_out, other], axis=0),
            jnp.concatenate([other, grad_out], axis=0),
        )
    else:
        grad_rows = lax.all_gather(grad_out, "tp", axis=0, tiled=True)

    here_b, hops_b = joined_hops(own_b)
    near_here, near_there, far_here, far_there, from_far = plan(
        me, tile_map, after(map_far, hops_b[-1]), places, rank_two
    )
    there_b = swap(here_b, core)
    factor_b = take_in(here_b, there_b, swap(give_away(here_b, there_b), far))
    key_row = lax.broadcasted_iota(jnp.int32, factor_b.shape, 0) % rank_two < rank_one
    nothing = jnp.zeros_like(factor_b)
    wide_b = jnp.concatenate(
        [jnp.where(key_row, factor_b, nothing), jnp.where(key_row, nothing, factor_b)], axis=1
    )
    rank_grad = jnp.where(keep, dot(wide_b, grad_rows, (1, 1)), 0.0).astype(bf16)
    width_c = features // c_parts
    down = [
        (adapter_scale * dot(rank_grad, tokens[:, i * width_c : (i + 1) * width_c], (1, 0))).astype(bf16)
        for i in range(c_parts)
    ]

    blocks_a = [after(own_a, there_b)]
    late_hop = None
    for bit in reversed(bits):
        if len(blocks_a) > 1:
            blocks_a[-1] = late_hop = after(blocks_a[-1], down[0])
        blocks_a = blocks_a + [swap(block, 1 << bit) for block in blocks_a]
    here_a = jnp.concatenate(blocks_a, axis=0)
    if tp_count == 2:
        base = dot(after(tokens, late_hop), weight, (1, 0))
        near_base = lax.dynamic_slice_in_dim(base, col * local_rows, local_rows, 0)
        far_base = lax.dynamic_slice_in_dim(base, (1 - col) * local_rows, local_rows, 0).astype(bf16)
        base_rows = near_base + cross(far_base).astype(f32)
        here_a = after(here_a, far_base)
    else:
        far_base = dot(tokens, weight, (1, 0))
        base_rows = lax.psum_scatter(far_base, "tp", scatter_dimension=0, tiled=True)
    there_a = swap(here_a, core)
    sent_a = give_away(here_a, there_a)
    factor_a = take_in(here_a, there_a, swap(sent_a, far))

    got_c = [swap(d, far) for d in down]
    got_c[0] = after(got_c[0], here_a)
    back = swap(core_part(down[0], got_c[0]), core)
    total = sums(down[0], got_c[0], back)
    first_gone = after(leaving(total, bits[0]), sent_a)
    total = add_hop(total, swap(first_gone, 1 << bits[0]), bits[0])

    got_c[1] = after(got_c[1], first_gone)
    away = core_part(down[1], got_c[1])
    base_grad = dot(after(grad_rows, sent_a, away), weight, (1, 1))

    total_c = []
    first_came = None
    mark = base_grad
    for i in range(c_parts):
        if i:
            total = sums(down[i], got_c[i], swap(away, core))
            first_came = swap(after(leaving(total, bits[0]), mark), 1 << bits[0])
            total = add_hop(total, first_came, bits[0])
        for bit in bits[1:]:
            mark = after(leaving(total, bit), mark)
            total = add_hop(total, swap(mark, 1 << bit), bit)
        total_c.append(total)
    grad_a = jnp.concatenate([total[0] for total in total_c], axis=1)

    rank_part = jnp.where(keep, dot(factor_a, tokens, (1, 1)), 0.0)
    rank_part = sum(split(rank_part))
    if tp_count == 2:
        rank_sum = rank_part + cross(rank_part)
    else:
        rank_sum = lax.psum(rank_part, "tp")
    rank_act = rank_sum.astype(bf16)

    first = col * local_rows
    local_act = lax.dynamic_slice_in_dim(rank_act, first, local_rows, 1)
    local_b = pick(split(wide_b), [first // tile_rows == k for k in range(tile_count)])
    key_value_output = (base_rows + adapter_scale * dot(local_act, local_b, (0, 0))).astype(bf16)

    spread = jnp.where(keep, jnp.concatenate([rank_act] * tile_count, axis=0), jnp.zeros((), bf16))
    whole = adapter_scale * dot(spread, grad_rows, (1, 0))
    key_part = lax.dynamic_slice(whole, (0, col * kv_dev), (stacked, kv_dev))
    value_part = lax.dynamic_slice(whole, (0, kv_width + col * kv_dev), (stacked, kv_dev))
    up = jnp.where(key_row[:, :kv_dev], key_part, value_part).astype(bf16)
    got_up = after(swap(up, far), first_came)
    back_up = swap(core_part(up, got_up), core)
    total_up = sums(up, got_up, back_up)
    leave = [after(total_up[o].astype(bf16), mark) for o in places[1:]]
    came_up = [swap(t, o) for o, t in zip(places[1:], leave)]
    grad_b = sum([c.astype(f32) for c in came_up], total_up[0])

    lora_grad = dot(after(rank_grad, rank_act), factor_a, (0, 0))
    token_gradient = (after(base_grad, rank_act) + adapter_scale * lora_grad).astype(bf16)
    return key_value_output, token_gradient, grad_a.T[None], grad_b[None]


def solution(mesh):
    in_specs = (
        P("blk", "tp"),
        P("tp", None),
        P("blk", "tp", None),
        P("blk", None, None),
        P("blk", None),
        P(("blk", "tp"), None),
    )
    out_specs = (P(("blk", "tp"), None), P("blk", "tp"), P("blk", "tp", None), P("blk", None, "tp"))
    return jax.shard_map(
        on_device, mesh=mesh, in_specs=in_specs, out_specs=out_specs, check_vma=False
    )
```

time: 125 us -> 107 us (0.86)
  waiting for transfers between devices: 47.1 us -> 23.5 us
  other arithmetic: 4.07 us -> 11.2 us
  starting transfers between devices: 32.4 us -> 26.4 us
  matrix products: 35.1 us -> 39.9 us
  between operations: 3.68 us -> 1.63 us
    ppermute x40 -> x26, waiting for transfers between devices: 47.1 us -> 23.5 us  [the longest x23 21.7 us: swap(): return lax.ppermute(value, 'blk', [(i, i ^ offset) for i in range(count)])]
    ppermute x40 -> x26, starting transfers between devices: 32.4 us -> 26.4 us  [the longest x23 22.8 us: swap(): return lax.ppermute(value, 'blk', [(i, i ^ offset) for i in range(count)])]
    dot_general x13 -> x31, matrix products: 35.1 us -> 39.9 us  [dot(): lax.dot_general(a, b, ((contract[:1], contract[1:]), ((), ())), preferred...]
    concatenate x1 -> x3, other arithmetic: 0.02 us -> 1.83 us  [the longest x2 1.76 us: joined_hops(): blocks = jnp.concatenate([blocks, more], axis=0)]
    convert_element_type x10 -> x4, other arithmetic: 1.36 us -> 2.91 us  [the longest x1 1.83 us: on_device(): (after(base_grad, rank_act) + adapter_scale * lora_grad).astype(bf16)]
    unnamed x12 -> x104, local copies, waits for them, and re-layouts: 0.04 us -> 1.56 us
  transfers between devices with their start and end apart: 40 -> 26, of which waited for: 14 -> 9; matrix products, arithmetic and copies ran while one was open for 32% -> 49% of each run, Pallas kernels for 0% -> 0%
where the time goes in v2:
time: 107 us; the launch traced here: 106 us
  matrix products  39.9 us (37%)
  starting transfers between devices  26.4 us (25%)
  waiting for transfers between devices  23.5 us (22%)
  other arithmetic  11.2 us (10%)
  local copies, waits for them, and re-layouts  3.63 us (3%)
  between operations  1.63 us (2%)
    dot_general x31, matrix products, dot(): lax.dot_general(a, b, ((contract[:1], contract[1:]), ((), ())), preferred...  39.9 us
    ppermute x23, starting transfers between devices, swap(): return lax.ppermute(value, 'blk', [(i, i ^ offset) for i in range(count)])  22.8 us
    ppermute x23, waiting for transfers between devices, swap(): return lax.ppermute(value, 'blk', [(i, i ^ offset) for i in range(count)])  21.7 us
    ppermute x3, starting transfers between devices, cross(): return lax.ppermute(value, 'tp', [(0, 1), (1, 0)])  3.61 us
  transfers between devices with their start and end apart: 26, of which 9 were waited for; matrix products, arithmetic and copies ran while one was open for 49% of the time, Pallas kernels for 0%

profile of v2, /device:TPU:0, one launch (start us, length us, event | category | flops | bytes accessed | tf_op | source)
XLA Modules:
  0.0 106.2 jit_solution(3745928106574845604)
XLA Ops:
  0.6 3.0 %collective-permute-start.4 = (s32[2,1]{0,1:T(1,128)}, s32[2,1]{0,1:T(1,128)S(1)}, u32[]{:S(2)}, u32[]{:S(2)}) collective-permute-start(s32[2,1]{0,1:T(1,128)} %param.10), channel_id=1, source_target_pairs={{0,4},{2,6},{4,0},{6,2},{8,12},{10,14},{12,8},{14,10},{16,20},{18,... | collective-permute-start | bytes 32 | tf_op jit(solution)/shard_map/ppermute | solution.py:14
  3.6 2.6 %collective-permute-start = (bf16[32,1024]{1,0:T(8,128)(2,1)}, bf16[32,1024]{1,0:T(8,128)(2,1)S(1)}, u32[]{:S(2)}, u32[]{:S(2)}) collective-permute-start(bf16[32,1024]{1,0:T(8,128)(2,1)} %bitcast.46), channel_id=1, source_target_pairs={{0,16},{2,18},{4,20},{6,22},{8,24},{10,26},{12,28},{14,30},{16,0},... | collective-permute-start | bytes 196616 | tf_op jit(solution)/shard_map/ppermute | solution.py:14
  6.2 1.5 %collective-permute-start.6 = (bf16[128,2048]{1,0:T(8,128)(2,1)}, bf16[128,2048]{1,0:T(8,128)(2,1)S(1)}, u32[]{:S(2)}, u32[]{:S(2)}) collective-permute-start(bf16[128,2048]{1,0:T(8,128)(2,1)} %param.11), channel_id=1, source_target_pairs={{0,1},{1,0},{2,3},{3,2},{4,5},{5,4},{6,7},{7,6},{8,9},{9,8},{10,11... | collective-permute-start | bytes 1572872 | tf_op jit(solution)/shard_map/ppermute | solution.py:18
  8.4 0.7 xor_bitcast_fusion.1
  9.2 0.7 select_compare_fusion
  10.0 0.9 pad_maximum_fusion.4
  10.8 1.6 %collective-permute-start.1 = (bf16[64,1024]{1,0:T(8,128)(2,1)S(1)}, bf16[64,1024]{1,0:T(8,128)(2,1)S(1)}, u32[]{:S(2)}, u32[]{:S(2)}) collective-permute-start(bf16[64,1024]{1,0:T(8,128)(2,1)S(1)} %pad_maximum_fusion.4), channel_id=1, source_target_pairs={{0,8},{2,10},{4,12},{6,14},{8,0},{10,2},{12,4},{14,6},{16,24},{18,... | collective-permute-start | bytes 393224 | tf_op jit(solution)/shard_map/ppermute | solution.py:14
  13.5 2.3 %collective-permute-done.1 = bf16[64,1024]{1,0:T(8,128)(2,1)S(1)} collective-permute-done((bf16[64,1024]{1,0:T(8,128)(2,1)S(1)}, bf16[64,1024]{1,0:T(8,128)(2,1)S(1)}, u32[]{:S(2)}, u32[]{:S(2)}) %collective-permute-start.1) | collective-permute-done | bytes 131104 | tf_op jit(solution)/shard_map/ppermute | solution.py:14
  15.9 0.9 pad_maximum_fusion.3
  16.9 0.6 compare_and_fusion.7
  17.6 0.8 collective-permute-done.2
  18.4 1.6 %collective-permute-start.8 = (bf16[32,4096]{1,0:T(8,128)(2,1)}, bf16[32,4096]{1,0:T(8,128)(2,1)S(1)}, u32[]{:S(2)}, u32[]{:S(2)}) collective-permute-start(bf16[32,4096]{1,0:T(8,128)(2,1)} %bitcast.51), channel_id=1, source_target_pairs={{0,8},{2,10},{4,12},{6,14},{8,0},{10,2},{12,4},{14,6},{16,24},{18,... | collective-permute-start | bytes 786440 | tf_op jit(solution)/shard_map/ppermute | solution.py:14
  20.0 2.2 %collective-permute-start.3 = (bf16[32,4096]{1,0:T(8,128)(2,1)}, bf16[32,4096]{1,0:T(8,128)(2,1)S(1)}, u32[]{:S(2)}, u32[]{:S(2)}) collective-permute-start(bf16[32,4096]{1,0:T(8,128)(2,1)} %bitcast.52), channel_id=1, source_target_pairs={{0,16},{2,18},{4,20},{6,22},{8,24},{10,26},{12,28},{14,30},{16,0},... | collective-permute-start | bytes 786440 | tf_op jit(solution)/shard_map/ppermute | solution.py:14
  22.4 1.1 %fusion.11 = bf16[64,1024]{1,0:T(8,128)(2,1)S(1)} fusion(f32[64,1024]{1,0:T(8,128)S(1)} %fusion.66, s32[64]{0:T(128)S(1)} %broadcast_in_dim.60, s32[128]{0:T(128)S(1)} %get-tuple-element.51, s32[128]{0:T(128)S(1)} %get-tuple-element.53, pred[128]{0:T(512)(128)(4,1)S(1)} %get-tuple-element.47, s32[128]{0:T(128)S(1)} %get-tuple-element.52, ...), kind=kOutput, calls=%fused_computation.28 | convolution fusion | flops 17793024 | bytes 658496 | tf_op jit(solution)/shard_map/dot_general | solution.py:22
  23.6 0.6 collective-permute-start.5
  24.8 3.8 %collective-permute-done.5 = bf16[64,1024]{1,0:T(8,128)(2,1)S(1)} collective-permute-done((bf16[64,1024]{1,0:T(8,128)(2,1)S(1)}, bf16[64,1024]{1,0:T(8,128)(2,1)S(1)}, u32[]{:S(2)}, u32[]{:S(2)}) %collective-permute-start.5) | collective-permute-done | bytes 131104 | tf_op jit(solution)/shard_map/ppermute | solution.py:14
  28.9 0.9 broadcast_select_fusion.1
  31.3 0.6 collective-permute-start.13
  32.0 1.5 %fusion.58 = f32[128,2048]{1,0:T(8,128)} fusion(bf16[64,2048]{1,0:T(8,128)(2,1)S(1)} %fusion.7, s32[128]{0:T(128)S(1)} %copy-done.18, s32[128]{0:T(128)S(1)} %get-tuple-element.53, s32[64]{0:T(128)S(1)} %copy-done.33, pred[128]{0:T(512)(128)(4,1)S(1)} %copy-done.24, s32[128]{0:T(128)S(1)} %copy-done.21, s32[128]{0:T(128)S(1)} %copy-done.15, ...), kind=kOutput, calls=%fused_computation.130 | convolution fusion | flops 33652736 | bytes 1313856 | tf_op jit(solution)/shard_map/dot_general | solution.py:22
  33.9 1.6 %collective-permute-start.14 = (bf16[64,2048]{1,0:T(8,128)(2,1)S(1)}, bf16[64,2048]{1,0:T(8,128)(2,1)S(1)}, u32[]{:S(2)}, u32[]{:S(2)}) collective-permute-start(bf16[64,2048]{1,0:T(8,128)(2,1)S(1)} %fusion.6), channel_id=1, source_target_pairs={{0,4},{2,6},{4,0},{6,2},{8,12},{10,14},{12,8},{14,10},{16,20},{18,... | collective-permute-start | bytes 786440 | tf_op jit(solution)/shard_map/ppermute | solution.py:14
  36.7 8.1 %fusion.69 = f32[256,2048]{1,0:T(8,128)S(1)} fusion(bf16[256,4096]{1,0:T(8,128)(2,1)S(1)} %copy-done, bf16[4096,2048]{1,0:T(8,128)(2,1)} %param.7), kind=kOutput, calls=%fused_computation.141 | convolution fusion | flops 4294967296 | bytes 20971520 | tf_op jit(solution)/shard_map/dot_general | solution.py:22
  44.8 1.0 dynamic-slice_convert_fusion
  45.8 1.5 %collective-permute-start.7 = (bf16[128,2048]{1,0:T(8,128)(2,1)}, bf16[128,2048]{1,0:T(8,128)(2,1)}, u32[]{:S(2)}, u32[]{:S(2)}) collective-permute-start(bf16[128,2048]{1,0:T(8,128)(2,1)} %dynamic-slice_convert_fusion), channel_id=1, source_target_pairs={{0,1},{1,0},{2,3},{3,2},{4,5},{5,4},{6,7},{7,6},{8,9},{9,8},{10,11... | collective-permute-start | bytes 1572872 | tf_op jit(solution)/shard_map/ppermute | solution.py:18
  48.9 1.3 %fusion.60 = f32[64,4096]{1,0:T(8,128)} fusion(bf16[128,4096]{1,0:T(8,128)(2,1)S(1)} %pad_maximum_fusion, s32[128]{0:T(128)S(1)} %copy-done.18, s32[128]{0:T(128)S(1)} %get-tuple-element.53, s32[64]{0:T(128)S(1)} %copy-done.33, pred[128]{0:T(512)(128)(4,1)S(1)} %copy-done.24, s32[128]{0:T(128)S(1)} %copy-done.21, s32[128]{0:T(128)S(1)} %copy-done.15, ...), kind=kOutput, calls=%fused_computation.132 | convolution fusion | flops 67207168 | bytes 2100288 | tf_op jit(solution)/shard_map/dot_general | solution.py:22
  50.2 0.7 collective-permute-done.15
  51.3 1.0 copy-done.4
  52.4 0.8 slice.177
  53.1 1.1 %fusion.1 = bf16[64,4096]{1,0:T(8,128)(2,1)} fusion(f32[64,4096]{1,0:T(8,128)S(1)} %fusion.65, bf16[128,4096]{1,0:T(8,128)(2,1)S(1)} %collective-permute-done.10, s32[64]{0:T(128)S(1)} %copy-done.36, s32[128]{0:T(128)S(1)} %copy-done.18, s32[128]{0:T(128)S(1)} %get-tuple-element.53, pred[128]{0:T(512)(128)(4,1)S(1)} %copy-done.24, s32[128]{0:T(128)S(1)} %copy-done.21, ...), kind=kOutput, calls=%fused_computation.5 | convolution fusion | flops 67739648 | bytes 2624576 | tf_op jit(solution)/shard_map/dot_general | solution.py:22
  54.3 1.7 %collective-permute-start.16 = (bf16[64,2048]{1,0:T(8,128)(2,1)}, bf16[64,2048]{1,0:T(8,128)(2,1)}, u32[]{:S(2)}, u32[]{:S(2)}) collective-permute-start(bf16[64,2048]{1,0:T(8,128)(2,1)} %slice.177), channel_id=1, source_target_pairs={{0,8},{2,10},{4,12},{6,14},{8,0},{10,2},{12,4},{14,6},{16,24},{18,... | collective-permute-start | bytes 786440 | tf_op jit(solution)/shard_map/ppermute | solution.py:14
  56.0 1.2 %fusion.5 = bf16[128,2048]{1,0:T(8,128)(2,1)} fusion(f32[128,2048]{1,0:T(8,128)S(1)} %fusion.63, bf16[64,2048]{1,0:T(8,128)(2,1)S(1)} %collective-permute-done.13, s32[64]{0:T(128)S(1)} %copy-done.36, s32[128]{0:T(128)S(1)} %copy-done.18, s32[128]{0:T(128)S(1)} %get-tuple-element.53, pred[128]{0:T(512)(128)(4,1)S(1)} %copy-done.24, s32[128]{0:T(128)S(1)} %copy-done.21, ...), kind=kOutput, calls=%fused_computation.15 | convolution fusion | flops 34185216 | bytes 1838144 | tf_op jit(solution)/shard_map/dot_general | solution.py:22
  57.8 10.2 %fusion.70 = f32[256,4096]{1,0:T(8,128)} fusion(bf16[256,2048]{1,0:T(8,128)(2,1)S(1)} %maximum_select_fusion, bf16[4096,2048]{1,0:T(8,128)(2,1)} %param.7), kind=kOutput, calls=%fused_computation.142 | convolution fusion | flops 4294967296 | bytes 22020096 | tf_op jit(solution)/shard_map/dot_general | solution.py:22
  68.0 1.0 fusion.18
  69.3 1.9 %convolution_add_fusion.2 = f32[64,4096]{1,0:T(8,128)S(1)} fusion(f32[64,4096]{1,0:T(8,128)} %fusion.60, bf16[128,4096]{1,0:T(8,128)(2,1)} %copy-done.1, s32[128]{0:T(128)} %copy-done.17, s32[128]{0:T(128)S(1)} %get-tuple-element.53, s32[64]{0:T(128)} %copy-done.32, pred[128]{0:T(512)(128)(4,1)} %copy-done.23, s32[128]{0:T(128)} %copy-done.20, ...), kind=kOutput, calls=%fused_computation.3 | convolution fusion | flops 67477504 | bytes 3148864 | tf_op jit(solution)/shard_map/dot_general | solution.py:22
  71.3 6.8 %collective-permute-done.17 = bf16[32,2048]{1,0:T(8,128)(2,1)S(1)} collective-permute-done((bf16[32,2048]{1,0:T(8,128)(2,1)S(1)}, bf16[32,2048]{1,0:T(8,128)(2,1)S(1)}, u32[]{:S(2)}, u32[]{:S(2)}) %collective-permute-start.17) | collective-permute-done | bytes 131104 | tf_op jit(solution)/shard_map/ppermute | solution.py:14
  78.1 1.0 fusion.19
  79.2 1.4 %fusion = bf16[64,4096]{1,0:T(8,128)(2,1)S(1)} fusion(f32[64,4096]{1,0:T(8,128)S(1)} %convolution_add_fusion.2, bf16[64,4096]{1,0:T(8,128)(2,1)} %collective-permute-done.11, pred[64]{0:T(512)(128)(4,1)S(1)} %copy-done.51), kind=kOutput, calls=%fused_computation.4 | convolution fusion | flops 34086912 | bytes 2097216 | tf_op jit(solution)/shard_map/dot_general | solution.py:22
  80.7 0.8 convolution_select_fusion.1
  82.2 1.5 %fusion.2 = f32[128,2048]{1,0:T(8,128)S(1)} fusion(f32[128,2048]{1,0:T(8,128)S(1)} %copy-done.3, bf16[64,2048]{1,0:T(8,128)(2,1)S(1)} %collective-permute-done.13, bf16[128,2048]{1,0:T(8,128)(2,1)} %collective-permute-done.18, s32[64]{0:T(128)S(1)} %copy-done.37, s32[128]{0:T(128)S(1)} %copy-done.19, s32[128]{0:T(128)S(1)} %get-tuple-element.53, ...), kind=kOutput, calls=%fused_computation.8 | convolution fusion | flops 34439168 | bytes 2886720 | tf_op jit(solution)/shard_map/dot_general | solution.py:22
  83.8 1.7 %collective-permute-done.12 = f32[32,256]{1,0:T(8,128)S(1)} collective-permute-done((f32[32,256]{1,0:T(8,128)S(1)}, f32[32,256]{1,0:T(8,128)S(1)}, u32[]{:S(2)}, u32[]{:S(2)}) %collective-permute-start.12) | collective-permute-done | bytes 32800 | tf_op jit(solution)/shard_map/ppermute | solution.py:18
  85.9 1.6 %collective-permute-start.21 = (bf16[64,512]{1,0:T(8,128)(2,1)S(1)}, bf16[64,512]{1,0:T(8,128)(2,1)S(1)}, u32[]{:S(2)}, u32[]{:S(2)}) collective-permute-start(bf16[64,512]{1,0:T(8,128)(2,1)S(1)} %select_convert_fusion), channel_id=1, source_target_pairs={{0,4},{2,6},{4,0},{6,2},{8,12},{10,14},{12,8},{14,10},{16,20},{18,... | collective-permute-start | bytes 196616 | tf_op jit(solution)/shard_map/ppermute | solution.py:14
  87.5 0.7 convolution_multiply_fusion
  88.3 1.8 %add_convert_fusion = bf16[256,4096]{1,0:T(8,128)(2,1)} fusion(f32[256,4096]{1,0:T(8,128)S(1)} %copy-done.2, f32[256,4096]{1,0:T(8,128)S(1)} %convolution_multiply_fusion), kind=kLoop, calls=%fused_computation.6 | loop fusion | flops 2097152 | bytes 10485760 | tf_op jit(solution)/shard_map/convert_element_type | solution.py:229
  90.1 2.2 %add_convert_fusion.1 = bf16[128,2048]{1,0:T(8,128)(2,1)} fusion(bf16[128,2048]{1,0:T(8,128)(2,1)} %collective-permute-done.7, f32[256,2048]{1,0:T(8,128)S(1)} %copy-done.6, s32[]{:T(128)S(6)} %select_n.168, bf16[64,1024]{1,0:T(8,128)(2,1)S(1)} %get-tuple-element.40, bf16[64,1024]{1,0:T(8,128)(2,1)S(1)} %copy-done.9, pred[]{:T(512)S(6)} %eq.111, ...), kind=kOutput, calls=%fused_computation.36 | convolution fusion | flops 18743296 | bytes 2369536 | tf_op jit(solution)/shard_map/dot_general | solution.py:22
  93.5 1.2 %collective-permute-done.22 = bf16[128,512]{1,0:T(8,128)(2,1)S(1)} collective-permute-done((bf16[128,512]{1,0:T(8,128)(2,1)S(1)}, bf16[128,512]{1,0:T(8,128)(2,1)S(1)}, u32[]{:S(2)}, u32[]{:S(2)}) %collective-permute-start.22) | collective-permute-done | bytes 131104 | tf_op jit(solution)/shard_map/ppermute | solution.py:14
  95.4 2.9 %collective-permute-start.25 = (bf16[32,512]{1,0:T(8,128)(2,1)S(1)}, bf16[32,512]{1,0:T(8,128)(2,1)S(1)}, u32[]{:S(2)}, u32[]{:S(2)}) collective-permute-start(bf16[32,512]{1,0:T(8,128)(2,1)S(1)} %get-tuple-element.39), channel_id=1, source_target_pairs={{0,24},{2,26},{4,28},{6,30},{8,16},{10,18},{12,20},{14,22},{16,8},... | collective-permute-start | bytes 98312 | tf_op jit(solution)/shard_map/ppermute | solution.py:14
  98.6 5.6 %collective-permute-done.20 = bf16[32,2048]{1,0:T(8,128)(2,1)S(1)} collective-permute-done((bf16[32,2048]{1,0:T(8,128)(2,1)S(1)}, bf16[32,2048]{1,0:T(8,128)(2,1)S(1)}, u32[]{:S(2)}, u32[]{:S(2)}) %collective-permute-start.20) | collective-permute-done | bytes 131104 | tf_op jit(solution)/shard_map/ppermute | solution.py:14
  104.3 0.8 maximum_bitcast_fusion
  105.6 0.7 fusion.30
  (174 shorter events, 12.7 us)
Async XLA Ops:
  0.6 23.9 %copy-start.7 = (bf16[128,2048]{1,0:T(8,128)(2,1)S(1)}, bf16[128,2048]{1,0:T(8,128)(2,1)}, u32[]{:S(2)}) copy-start(bf16[128,2048]{1,0:T(8,128)(2,1)} %param.11) | copy-start | bytes 1572868
  0.6 16.8 %collective-permute-start.4 = (s32[2,1]{0,1:T(1,128)}, s32[2,1]{0,1:T(1,128)S(1)}, u32[]{:S(2)}, u32[]{:S(2)}) collective-permute-start(s32[2,1]{0,1:T(1,128)} %param.10), channel_id=1, source_target_pairs={{0,4},{2,6},{4,0},{6,2},{8,12},{10,14},{12,8},{14,10},{16,20},{18,... | collective-permute-start | bytes 32 | tf_op jit(solution)/shard_map/ppermute | solution.py:14
  3.6 6.3 %collective-permute-start = (bf16[32,1024]{1,0:T(8,128)(2,1)}, bf16[32,1024]{1,0:T(8,128)(2,1)S(1)}, u32[]{:S(2)}, u32[]{:S(2)}) collective-permute-start(bf16[32,1024]{1,0:T(8,128)(2,1)} %bitcast.46), channel_id=1, source_target_pairs={{0,16},{2,18},{4,20},{6,22},{8,24},{10,26},{12,28},{14,30},{16,0},... | collective-permute-start | bytes 196616 | tf_op jit(solution)/shard_map/ppermute | solution.py:14
  6.2 18.2 %collective-permute-start.6 = (bf16[128,2048]{1,0:T(8,128)(2,1)}, bf16[128,2048]{1,0:T(8,128)(2,1)S(1)}, u32[]{:S(2)}, u32[]{:S(2)}) collective-permute-start(bf16[128,2048]{1,0:T(8,128)(2,1)} %param.11), channel_id=1, source_target_pairs={{0,1},{1,0},{2,3},{3,2},{4,5},{5,4},{6,7},{7,6},{8,9},{9,8},{10,11... | collective-permute-start | bytes 1572872 | tf_op jit(solution)/shard_map/ppermute | solution.py:18
  7.8 20.9 %copy-start.14 = (s32[128]{0:T(128)}, s32[128]{0:T(128)S(1)}, u32[]{:S(2)}) copy-start(s32[128]{0:T(128)S(1)} %get-tuple-element.54) | copy-start | bytes 1540
  7.8 17.0 %copy-start.17 = (s32[128]{0:T(128)}, s32[128]{0:T(128)S(1)}, u32[]{:S(2)}) copy-start(s32[128]{0:T(128)S(1)} %get-tuple-element.51) | copy-start | bytes 1540
  7.8 17.0 %copy-start.20 = (s32[128]{0:T(128)}, s32[128]{0:T(128)S(1)}, u32[]{:S(2)}) copy-start(s32[128]{0:T(128)S(1)} %get-tuple-element.52) | copy-start | bytes 1540
  9.2 15.6 %copy-start.32 = (s32[64]{0:T(128)}, s32[64]{0:T(128)S(1)}, u32[]{:S(2)}) copy-start(s32[64]{0:T(128)S(1)} %broadcast_in_dim.54) | copy-start | bytes 772
  9.2 19.4 %copy-start.50 = (pred[64]{0:T(512)(128)(4,1)}, pred[64]{0:T(512)(128)(4,1)S(1)}, u32[]{:S(2)}) copy-start(pred[64]{0:T(512)(128)(4,1)S(1)} %and_compare_fusion) | copy-start | bytes 196
  10.0 14.8 %copy-start.23 = (pred[128]{0:T(512)(128)(4,1)}, pred[128]{0:T(512)(128)(4,1)S(1)}, u32[]{:S(2)}) copy-start(pred[128]{0:T(512)(128)(4,1)S(1)} %get-tuple-element.47) | copy-start | bytes 388
  10.0 14.8 %copy-start.26 = (pred[128]{0:T(512)(128)(4,1)}, pred[128]{0:T(512)(128)(4,1)S(1)}, u32[]{:S(2)}) copy-start(pred[128]{0:T(512)(128)(4,1)S(1)} %get-tuple-element.48) | copy-start | bytes 388
  10.8 5.0 %collective-permute-start.1 = (bf16[64,1024]{1,0:T(8,128)(2,1)S(1)}, bf16[64,1024]{1,0:T(8,128)(2,1)S(1)}, u32[]{:S(2)}, u32[]{:S(2)}) collective-permute-start(bf16[64,1024]{1,0:T(8,128)(2,1)S(1)} %pad_maximum_fusion.4), channel_id=1, source_target_pairs={{0,8},{2,10},{4,12},{6,14},{8,0},{10,2},{12,4},{14,6},{16,24},{18,... | collective-permute-start | bytes 393224 | tf_op jit(solution)/shard_map/ppermute | solution.py:14
  15.9 8.5 %copy-start.30 = (bf16[64,1024]{1,0:T(8,128)(2,1)}, bf16[64,1024]{1,0:T(8,128)(2,1)S(1)}, u32[]{:S(2)}) copy-start(bf16[64,1024]{1,0:T(8,128)(2,1)S(1)} %collective-permute-done.1) | copy-start | bytes 393220
  16.8 1.6 %collective-permute-start.2 = (bf16[128,1024]{1,0:T(8,128)(2,1)S(1)}, bf16[128,1024]{1,0:T(8,128)(2,1)S(1)}, u32[]{:S(2)}, u32[]{:S(2)}) collective-permute-start(bf16[128,1024]{1,0:T(8,128)(2,1)S(1)} %pad_maximum_fusion.3), channel_id=1, source_target_pairs={{0,2},{2,0},{4,6},{6,4},{8,10},{10,8},{12,14},{14,12},{16,18},{18,... | collective-permute-start | bytes 786440 | tf_op jit(solution)/shard_map/ppermute | solution.py:14
  17.6 11.0 %copy-start.35 = (s32[64]{0:T(128)}, s32[64]{0:T(128)S(1)}, u32[]{:S(2)}) copy-start(s32[64]{0:T(128)S(1)} %broadcast_in_dim.60) | copy-start | bytes 772
  18.4 28.9 %collective-permute-start.8 = (bf16[32,4096]{1,0:T(8,128)(2,1)}, bf16[32,4096]{1,0:T(8,128)(2,1)S(1)}, u32[]{:S(2)}, u32[]{:S(2)}) collective-permute-start(bf16[32,4096]{1,0:T(8,128)(2,1)} %bitcast.51), channel_id=1, source_target_pairs={{0,8},{2,10},{4,12},{6,14},{8,0},{10,2},{12,4},{14,6},{16,24},{18,... | collective-permute-start | bytes 786440 | tf_op jit(solution)/shard_map/ppermute | solution.py:14
  20.0 16.4 %collective-permute-start.3 = (bf16[32,4096]{1,0:T(8,128)(2,1)}, bf16[32,4096]{1,0:T(8,128)(2,1)S(1)}, u32[]{:S(2)}, u32[]{:S(2)}) collective-permute-start(bf16[32,4096]{1,0:T(8,128)(2,1)} %bitcast.52), channel_id=1, source_target_pairs={{0,16},{2,18},{4,20},{6,22},{8,24},{10,26},{12,28},{14,30},{16,0},... | collective-permute-start | bytes 786440 | tf_op jit(solution)/shard_map/ppermute | solution.py:14
  22.4 6.4 %copy-start.12 = (bf16[1,32,1024]{2,1,0:T(8,128)(2,1)S(1)}, bf16[1,32,1024]{2,1,0:T(8,128)(2,1)}, u32[]{:S(2)}) copy-start(bf16[1,32,1024]{2,1,0:T(8,128)(2,1)} %param.9) | copy-start | bytes 196612
  23.6 5.0 %collective-permute-start.5 = (bf16[64,1024]{1,0:T(8,128)(2,1)S(1)}, bf16[64,1024]{1,0:T(8,128)(2,1)S(1)}, u32[]{:S(2)}, u32[]{:S(2)}) collective-permute-start(bf16[64,1024]{1,0:T(8,128)(2,1)S(1)} %fusion.11), channel_id=1, source_target_pairs={{0,4},{2,6},{4,0},{6,2},{8,12},{10,14},{12,8},{14,10},{16,20},{18,... | collective-permute-start | bytes 393224 | tf_op jit(solution)/shard_map/ppermute | solution.py:14
  24.4 5.5 %copy-start.38 = (s32[256]{0:T(256)S(1)}, s32[256]{0:T(256)}, u32[]{:S(2)}) copy-start(s32[256]{0:T(256)} %get-tuple-element.55) | copy-start | bytes 3076
  24.8 5.6 %copy-start = (bf16[256,4096]{1,0:T(8,128)(2,1)S(1)}, bf16[256,4096]{1,0:T(8,128)(2,1)}, u32[]{:S(2)}) copy-start(bf16[256,4096]{1,0:T(8,128)(2,1)} %param.6) | copy-start | bytes 6291460
  31.3 24.7 %collective-permute-start.13 = (bf16[64,2048]{1,0:T(8,128)(2,1)S(1)}, bf16[64,2048]{1,0:T(8,128)(2,1)S(1)}, u32[]{:S(2)}, u32[]{:S(2)}) collective-permute-start(bf16[64,2048]{1,0:T(8,128)(2,1)S(1)} %fusion.7), channel_id=1, source_target_pairs={{0,4},{2,6},{4,0},{6,2},{8,12},{10,14},{12,8},{14,10},{16,20},{18,... | collective-permute-start | bytes 786440 | tf_op jit(solution)/shard_map/ppermute | solution.py:14
  33.9 13.6 %collective-permute-start.14 = (bf16[64,2048]{1,0:T(8,128)(2,1)S(1)}, bf16[64,2048]{1,0:T(8,128)(2,1)S(1)}, u32[]{:S(2)}, u32[]{:S(2)}) collective-permute-start(bf16[64,2048]{1,0:T(8,128)(2,1)S(1)} %fusion.6), channel_id=1, source_target_pairs={{0,4},{2,6},{4,0},{6,2},{8,12},{10,14},{12,8},{14,10},{16,20},{18,... | collective-permute-start | bytes 786440 | tf_op jit(solution)/shard_map/ppermute | solution.py:14
  36.3 11.0 %copy-start.13 = (bf16[1,4096,32]{1,2,0:T(8,128)(2,1)S(1)}, bf16[1,4096,32]{1,2,0:T(8,128)(2,1)}, u32[]{:S(2)}) copy-start(bf16[1,4096,32]{1,2,0:T(8,128)(2,1)} %param.8) | copy-start | bytes 786436
  36.3 11.0 %collective-permute-start.9 = (bf16[32,4096]{1,0:T(8,128)(2,1)S(1)}, bf16[32,4096]{1,0:T(8,128)(2,1)S(1)}, u32[]{:S(2)}, u32[]{:S(2)}) collective-permute-start(bf16[32,4096]{1,0:T(8,128)(2,1)S(1)} %collective-permute-done.3), channel_id=1, source_target_pairs={{0,8},{2,10},{4,12},{6,14},{8,0},{10,2},{12,4},{14,6},{16,24},{18,... | collective-permute-start | bytes 786440 | tf_op jit(solution)/shard_map/ppermute | solution.py:14
  45.8 44.3 %collective-permute-start.7 = (bf16[128,2048]{1,0:T(8,128)(2,1)}, bf16[128,2048]{1,0:T(8,128)(2,1)}, u32[]{:S(2)}, u32[]{:S(2)}) collective-permute-start(bf16[128,2048]{1,0:T(8,128)(2,1)} %dynamic-slice_convert_fusion), channel_id=1, source_target_pairs={{0,1},{1,0},{2,3},{3,2},{4,5},{5,4},{6,7},{7,6},{8,9},{9,8},{10,11... | collective-permute-start | bytes 1572872 | tf_op jit(solution)/shard_map/ppermute | solution.py:18
  47.4 5.7 %collective-permute-start.10 = (bf16[128,4096]{1,0:T(8,128)(2,1)S(1)}, bf16[128,4096]{1,0:T(8,128)(2,1)S(1)}, u32[]{:S(2)}, u32[]{:S(2)}) collective-permute-start(bf16[128,4096]{1,0:T(8,128)(2,1)S(1)} %pad_maximum_fusion), channel_id=1, source_target_pairs={{0,2},{2,0},{4,6},{6,4},{8,10},{10,8},{12,14},{14,12},{16,18},{18,... | collective-permute-start | bytes 3145736 | tf_op jit(solution)/shard_map/ppermute | solution.py:14
  48.0 2.9 %collective-permute-start.15 = (bf16[128,2048]{1,0:T(8,128)(2,1)S(1)}, bf16[128,2048]{1,0:T(8,128)(2,1)S(1)}, u32[]{:S(2)}, u32[]{:S(2)}) collective-permute-start(bf16[128,2048]{1,0:T(8,128)(2,1)S(1)} %fusion.4), channel_id=1, source_target_pairs={{0,2},{2,0},{4,6},{6,4},{8,10},{10,8},{12,14},{14,12},{16,18},{18,... | collective-permute-start | bytes 1572872 | tf_op jit(solution)/shard_map/ppermute | solution.py:14
  54.3 13.7 %collective-permute-start.16 = (bf16[64,2048]{1,0:T(8,128)(2,1)}, bf16[64,2048]{1,0:T(8,128)(2,1)}, u32[]{:S(2)}, u32[]{:S(2)}) collective-permute-start(bf16[64,2048]{1,0:T(8,128)(2,1)} %slice.177), channel_id=1, source_target_pairs={{0,8},{2,10},{4,12},{6,14},{8,0},{10,2},{12,4},{14,6},{16,24},{18,... | collective-permute-start | bytes 786440 | tf_op jit(solution)/shard_map/ppermute | solution.py:14
  57.3 24.9 %collective-permute-start.18 = (bf16[128,2048]{1,0:T(8,128)(2,1)}, bf16[128,2048]{1,0:T(8,128)(2,1)}, u32[]{:S(2)}, u32[]{:S(2)}) collective-permute-start(bf16[128,2048]{1,0:T(8,128)(2,1)} %fusion.5), channel_id=1, source_target_pairs={{0,2},{2,0},{4,6},{6,4},{8,10},{10,8},{12,14},{14,12},{16,18},{18,... | collective-permute-start | bytes 1572872 | tf_op jit(solution)/shard_map/ppermute | solution.py:14
  57.3 21.9 %collective-permute-start.11 = (bf16[64,4096]{1,0:T(8,128)(2,1)}, bf16[64,4096]{1,0:T(8,128)(2,1)}, u32[]{:S(2)}, u32[]{:S(2)}) collective-permute-start(bf16[64,4096]{1,0:T(8,128)(2,1)} %fusion.1), channel_id=1, source_target_pairs={{0,4},{2,6},{4,0},{6,2},{8,12},{10,14},{12,8},{14,10},{16,20},{18,... | collective-permute-start | bytes 1572872 | tf_op jit(solution)/shard_map/ppermute | solution.py:14
  69.0 10.2 %copy-start.51 = (pred[64]{0:T(512)(128)(4,1)S(1)}, pred[64]{0:T(512)(128)(4,1)}, u32[]{:S(2)}) copy-start(pred[64]{0:T(512)(128)(4,1)} %copy-done.50) | copy-start | bytes 196
  69.0 9.1 %collective-permute-start.17 = (bf16[32,2048]{1,0:T(8,128)(2,1)S(1)}, bf16[32,2048]{1,0:T(8,128)(2,1)S(1)}, u32[]{:S(2)}, u32[]{:S(2)}) collective-permute-start(bf16[32,2048]{1,0:T(8,128)(2,1)S(1)} %fusion.18), channel_id=1, source_target_pairs={{0,16},{2,18},{4,20},{6,22},{8,24},{10,26},{12,28},{14,30},{16,0},... | collective-permute-start | bytes 393224 | tf_op jit(solution)/shard_map/ppermute | solution.py:14
  71.3 9.4 %copy-start.39 = (s32[256]{0:T(256)S(1)}, s32[256]{0:T(256)}, u32[]{:S(2)}) copy-start(s32[256]{0:T(256)} %get-tuple-element.55) | copy-start | bytes 3076
  71.3 9.4 %copy-start.41 = (s32[256]{0:T(256)S(1)}, s32[256]{0:T(256)}, u32[]{:S(2)}) copy-start(s32[256]{0:T(256)} %get-tuple-element.56) | copy-start | bytes 3076
  71.3 9.4 %copy-start.43 = (s32[64]{0:T(128)S(1)}, s32[64]{0:T(128)}, u32[]{:S(2)}) copy-start(s32[64]{0:T(128)} %get-tuple-element.57) | copy-start | bytes 772
  71.3 9.4 %copy-start.45 = (s32[64]{0:T(128)S(1)}, s32[64]{0:T(128)}, u32[]{:S(2)}) copy-start(s32[64]{0:T(128)} %get-tuple-element.58) | copy-start | bytes 772
  71.3 9.4 %copy-start.47 = (pred[64]{0:T(512)(128)(4,1)S(1)}, pred[64]{0:T(512)(128)(4,1)}, u32[]{:S(2)}) copy-start(pred[64]{0:T(512)(128)(4,1)} %compare_and_fusion.8) | copy-start | bytes 196
  71.3 9.4 %copy-start.49 = (pred[256]{0:T(512)(128)(4,1)S(1)}, pred[256]{0:T(512)(128)(4,1)}, u32[]{:S(2)}) copy-start(pred[256]{0:T(512)(128)(4,1)} %compare_and_fusion.7) | copy-start | bytes 772
  81.5 6.0 %copy-start.11 = (bf16[64,256]{1,0:T(8,128)(2,1)S(1)}, bf16[64,256]{1,0:T(8,128)(2,1)}, u32[]{:S(2)}) copy-start(bf16[64,256]{1,0:T(8,128)(2,1)} %copy-done.10) | copy-start | bytes 98308
  81.5 4.0 %collective-permute-start.12 = (f32[32,256]{1,0:T(8,128)S(1)}, f32[32,256]{1,0:T(8,128)S(1)}, u32[]{:S(2)}, u32[]{:S(2)}) collective-permute-start(f32[32,256]{1,0:T(8,128)S(1)} %slice_add_fusion.5), channel_id=1, source_target_pairs={{0,1},{1,0},{2,3},{3,2},{4,5},{5,4},{6,7},{7,6},{8,9},{9,8},{10,11... | collective-permute-start | bytes 98312 | tf_op jit(solution)/shard_map/ppermute | solution.py:18
  83.7 9.2 %collective-permute-start.19 = (bf16[64,2048]{1,0:T(8,128)(2,1)S(1)}, bf16[64,2048]{1,0:T(8,128)(2,1)S(1)}, u32[]{:S(2)}, u32[]{:S(2)}) collective-permute-start(bf16[64,2048]{1,0:T(8,128)(2,1)S(1)} %slice.176), channel_id=1, source_target_pairs={{0,8},{2,10},{4,12},{6,14},{8,0},{10,2},{12,4},{14,6},{16,24},{18,... | collective-permute-start | bytes 786440 | tf_op jit(solution)/shard_map/ppermute | solution.py:14
  85.9 7.0 %collective-permute-start.21 = (bf16[64,512]{1,0:T(8,128)(2,1)S(1)}, bf16[64,512]{1,0:T(8,128)(2,1)S(1)}, u32[]{:S(2)}, u32[]{:S(2)}) collective-permute-start(bf16[64,512]{1,0:T(8,128)(2,1)S(1)} %select_convert_fusion), channel_id=1, source_target_pairs={{0,4},{2,6},{4,0},{6,2},{8,12},{10,14},{12,8},{14,10},{16,20},{18,... | collective-permute-start | bytes 196616 | tf_op jit(solution)/shard_map/ppermute | solution.py:14
  93.3 1.4 %collective-permute-start.22 = (bf16[128,512]{1,0:T(8,128)(2,1)S(1)}, bf16[128,512]{1,0:T(8,128)(2,1)S(1)}, u32[]{:S(2)}, u32[]{:S(2)}) collective-permute-start(bf16[128,512]{1,0:T(8,128)(2,1)S(1)} %fusion.12), channel_id=1, source_target_pairs={{0,2},{2,0},{4,6},{6,4},{8,10},{10,8},{12,14},{14,12},{16,18},{18,... | collective-permute-start | bytes 393224 | tf_op jit(solution)/shard_map/ppermute | solution.py:14
  93.4 10.8 %collective-permute-start.20 = (bf16[32,2048]{1,0:T(8,128)(2,1)S(1)}, bf16[32,2048]{1,0:T(8,128)(2,1)S(1)}, u32[]{:S(2)}, u32[]{:S(2)}) collective-permute-start(bf16[32,2048]{1,0:T(8,128)(2,1)S(1)} %fusion.16), channel_id=1, source_target_pairs={{0,16},{2,18},{4,20},{6,22},{8,24},{10,26},{12,28},{14,30},{16,0},... | collective-permute-start | bytes 393224 | tf_op jit(solution)/shard_map/ppermute | solution.py:14
  95.0 10.1 %collective-permute-start.24 = (bf16[32,512]{1,0:T(8,128)(2,1)S(1)}, bf16[32,512]{1,0:T(8,128)(2,1)S(1)}, u32[]{:S(2)}, u32[]{:S(2)}) collective-permute-start(bf16[32,512]{1,0:T(8,128)(2,1)S(1)} %get-tuple-element.38), channel_id=1, source_target_pairs={{0,8},{2,10},{4,12},{6,14},{8,0},{10,2},{12,4},{14,6},{16,24},{18,... | collective-permute-start | bytes 98312 | tf_op jit(solution)/shard_map/ppermute | solution.py:14
  95.4 9.7 %collective-permute-start.25 = (bf16[32,512]{1,0:T(8,128)(2,1)S(1)}, bf16[32,512]{1,0:T(8,128)(2,1)S(1)}, u32[]{:S(2)}, u32[]{:S(2)}) collective-permute-start(bf16[32,512]{1,0:T(8,128)(2,1)S(1)} %get-tuple-element.39), channel_id=1, source_target_pairs={{0,24},{2,26},{4,28},{6,30},{8,16},{10,18},{12,20},{14,22},{16,8},... | collective-permute-start | bytes 98312 | tf_op jit(solution)/shard_map/ppermute | solution.py:14
  98.2 7.3 %collective-permute-start.23 = (bf16[32,512]{1,0:T(8,128)(2,1)S(1)}, bf16[32,512]{1,0:T(8,128)(2,1)S(1)}, u32[]{:S(2)}, u32[]{:S(2)}) collective-permute-start(bf16[32,512]{1,0:T(8,128)(2,1)S(1)} %get-tuple-element.37), channel_id=1, source_target_pairs={{0,16},{2,18},{4,20},{6,22},{8,24},{10,26},{12,28},{14,30},{16,0},... | collective-permute-start | bytes 98312 | tf_op jit(solution)/shard_map/ppermute | solution.py:14
  (30 other events, 90.2 us)

commit v3 on v2

--- a/solution.py
+++ b/solution.py
@@ -139,10 +139,11 @@
 
     here_b, hops_b = joined_hops(own_b)
     near_here, near_there, far_here, far_there, from_far = plan(
-        me, tile_map, after(map_far, hops_b[-1]), places, rank_two
+        me, after(tile_map, hops_b[0]), after(map_far, hops_b[0]), places, rank_two
     )
     there_b = swap(here_b, core)
-    factor_b = take_in(here_b, there_b, swap(give_away(here_b, there_b), far))
+    sent_b = give_away(here_b, there_b)
+    factor_b = take_in(here_b, there_b, swap(sent_b, far))
     key_row = lax.broadcasted_iota(jnp.int32, factor_b.shape, 0) % rank_two < rank_one
     nothing = jnp.zeros_like(factor_b)
     wide_b = jnp.concatenate(
@@ -155,7 +156,7 @@
         for i in range(c_parts)
     ]
 
-    blocks_a = [after(own_a, there_b)]
+    blocks_a = [after(own_a, sent_b)]
     late_hop = None
     for bit in reversed(bits):
         if len(blocks_a) > 1:
@@ -173,11 +174,10 @@
         base_rows = lax.psum_scatter(far_base, "tp", scatter_dimension=0, tiled=True)
     there_a = swap(here_a, core)
     sent_a = give_away(here_a, there_a)
-    factor_a = take_in(here_a, there_a, swap(sent_a, far))
 
     got_c = [swap(d, far) for d in down]
     got_c[0] = after(got_c[0], here_a)
-    back = swap(core_part(down[0], got_c[0]), core)
+    back = after(swap(core_part(down[0], got_c[0]), core), sent_a)
     total = sums(down[0], got_c[0], back)
     first_gone = after(leaving(total, bits[0]), sent_a)
     total = add_hop(total, swap(first_gone, 1 << bits[0]), bits[0])
@@ -186,9 +186,13 @@
     away = core_part(down[1], got_c[1])
     base_grad = dot(after(grad_rows, sent_a, away), weight, (1, 1))
 
+    factor_a = take_in(here_a, there_a, after(swap(sent_a, far), base_grad))
+    rank_part = jnp.where(keep, dot(factor_a, tokens, (1, 1)), 0.0)
+    rank_part = sum(split(rank_part))
+
     total_c = []
     first_came = None
-    mark = base_grad
+    mark = rank_part
     for i in range(c_parts):
         if i:
             total = sums(down[i], got_c[i], swap(away, core))
@@ -200,8 +204,6 @@
         total_c.append(total)
     grad_a = jnp.concatenate([total[0] for total in total_c], axis=1)
 
-    rank_part = jnp.where(keep, dot(factor_a, tokens, (1, 1)), 0.0)
-    rank_part = sum(split(rank_part))
     if tp_count == 2:
         rank_sum = rank_part + cross(rank_part)
     else:

time: 107 us -> 101 us (0.944)
  waiting for transfers between devices: 23.5 us -> 14.5 us
  starting transfers between devices: 26.4 us -> 29.9 us
    ppermute x23, waiting for transfers between devices: 21.7 us -> 14.5 us  [swap(): return lax.ppermute(value, 'blk', [(i, i ^ offset) for i in range(count)])]
    ppermute x23, starting transfers between devices: 22.8 us -> 26.2 us  [swap(): return lax.ppermute(value, 'blk', [(i, i ^ offset) for i in range(count)])]
    ppermute x3, waiting for transfers between devices: 1.75 us -> 0.01 us  [cross(): return lax.ppermute(value, 'tp', [(0, 1), (1, 0)])]
  transfers between devices with their start and end apart: 26 -> 26, of which waited for: 9 -> 8; matrix products, arithmetic and copies ran while one was open for 49% -> 53% of each run, Pallas kernels for 0% -> 0%
where the time goes in v3:
time: 101 us
  matrix products  39.9 us (40%)
  starting transfers between devices  29.9 us (30%)
  waiting for transfers between devices  14.5 us (14%)
  other arithmetic  12 us (12%)
  local copies, waits for them, and re-layouts  2.71 us (3%)
  between operations  1.58 us (2%)
    dot_general x31, matrix products, dot(): lax.dot_general(a, b, ((contract[:1], contract[1:]), ((), ())), preferred...  39.9 us
    ppermute x23, starting transfers between devices, swap(): return lax.ppermute(value, 'blk', [(i, i ^ offset) for i in range(count)])  26.2 us
    ppermute x23, waiting for transfers between devices, swap(): return lax.ppermute(value, 'blk', [(i, i ^ offset) for i in range(count)])  14.5 us
    ppermute x3, starting transfers between devices, cross(): return lax.ppermute(value, 'tp', [(0, 1), (1, 0)])  3.78 us
  transfers between devices with their start and end apart: 26, of which 8 were waited for; matrix products, arithmetic and copies ran while one was open for 53% of the time, Pallas kernels for 0%

profile of v3, /device:TPU:0, one launch (start us, length us, event | category | flops | bytes accessed | tf_op | source)
XLA Modules:
  0.0 100.6 jit_solution(16510283857623904)
XLA Ops:
  0.6 3.0 %collective-permute-start = (s32[2,1]{0,1:T(1,128)}, s32[2,1]{0,1:T(1,128)S(1)}, u32[]{:S(2)}, u32[]{:S(2)}) collective-permute-start(s32[2,1]{0,1:T(1,128)} %param.10), channel_id=1, source_target_pairs={{0,4},{2,6},{4,0},{6,2},{8,12},{10,14},{12,8},{14,10},{16,20},{18,... | collective-permute-start | bytes 32 | tf_op jit(solution)/shard_map/ppermute | solution.py:14
  3.6 2.6 %collective-permute-start.1 = (bf16[32,1024]{1,0:T(8,128)(2,1)}, bf16[32,1024]{1,0:T(8,128)(2,1)S(1)}, u32[]{:S(2)}, u32[]{:S(2)}) collective-permute-start(bf16[32,1024]{1,0:T(8,128)(2,1)} %bitcast.46), channel_id=1, source_target_pairs={{0,16},{2,18},{4,20},{6,22},{8,24},{10,26},{12,28},{14,30},{16,0},... | collective-permute-start | bytes 196616 | tf_op jit(solution)/shard_map/ppermute | solution.py:14
  6.2 1.5 %collective-permute-start.6 = (bf16[128,2048]{1,0:T(8,128)(2,1)}, bf16[128,2048]{1,0:T(8,128)(2,1)S(1)}, u32[]{:S(2)}, u32[]{:S(2)}) collective-permute-start(bf16[128,2048]{1,0:T(8,128)(2,1)} %param.11), channel_id=1, source_target_pairs={{0,1},{1,0},{2,3},{3,2},{4,5},{5,4},{6,7},{7,6},{8,9},{9,8},{10,11... | collective-permute-start | bytes 1572872 | tf_op jit(solution)/shard_map/ppermute | solution.py:18
  8.4 0.7 select_compare_fusion
  9.7 0.8 pad_maximum_fusion.4
  10.6 1.6 %collective-permute-start.2 = (bf16[64,1024]{1,0:T(8,128)(2,1)S(1)}, bf16[64,1024]{1,0:T(8,128)(2,1)S(1)}, u32[]{:S(2)}, u32[]{:S(2)}) collective-permute-start(bf16[64,1024]{1,0:T(8,128)(2,1)S(1)} %pad_maximum_fusion.4), channel_id=1, source_target_pairs={{0,8},{2,10},{4,12},{6,14},{8,0},{10,2},{12,4},{14,6},{16,24},{18,... | collective-permute-start | bytes 393224 | tf_op jit(solution)/shard_map/ppermute | solution.py:14
  13.3 2.3 %collective-permute-done.2 = bf16[64,1024]{1,0:T(8,128)(2,1)S(1)} collective-permute-done((bf16[64,1024]{1,0:T(8,128)(2,1)S(1)}, bf16[64,1024]{1,0:T(8,128)(2,1)S(1)}, u32[]{:S(2)}, u32[]{:S(2)}) %collective-permute-start.2) | collective-permute-done | bytes 131104 | tf_op jit(solution)/shard_map/ppermute | solution.py:14
  15.6 0.9 pad_maximum_fusion.3
  16.6 0.7 xor_bitcast_fusion
  18.3 1.1 %fusion.10 = bf16[64,1024]{1,0:T(8,128)(2,1)S(1)} fusion(f32[64,1024]{1,0:T(8,128)S(1)} %fusion.58, s32[128]{0:T(128)S(1)} %get-tuple-element.57, s32[128]{0:T(128)S(1)} %get-tuple-element.61, s32[64]{0:T(128)S(1)} %broadcast_in_dim.54, pred[128]{0:T(512)(128)(4,1)S(1)} %get-tuple-element.55, s32[128]{0:T(128)S(1)} %get-tuple-element.58, ...), kind=kOutput, calls=%fused_computation.27 | convolution fusion | flops 17793024 | bytes 658496 | tf_op jit(solution)/shard_map/dot_general | solution.py:22
  20.1 1.6 %collective-permute-start.8 = (bf16[32,4096]{1,0:T(8,128)(2,1)}, bf16[32,4096]{1,0:T(8,128)(2,1)S(1)}, u32[]{:S(2)}, u32[]{:S(2)}) collective-permute-start(bf16[32,4096]{1,0:T(8,128)(2,1)} %bitcast.1), channel_id=1, source_target_pairs={{0,8},{2,10},{4,12},{6,14},{8,0},{10,2},{12,4},{14,6},{16,24},{18,... | collective-permute-start | bytes 786440 | tf_op jit(solution)/shard_map/ppermute | solution.py:14
  21.7 2.5 %collective-permute-start.4 = (bf16[32,4096]{1,0:T(8,128)(2,1)}, bf16[32,4096]{1,0:T(8,128)(2,1)S(1)}, u32[]{:S(2)}, u32[]{:S(2)}) collective-permute-start(bf16[32,4096]{1,0:T(8,128)(2,1)} %bitcast.1), channel_id=1, source_target_pairs={{0,16},{2,18},{4,20},{6,22},{8,24},{10,26},{12,28},{14,30},{16,0},... | collective-permute-start | bytes 786440 | tf_op jit(solution)/shard_map/ppermute | solution.py:14
  25.4 1.0 broadcast_select_fusion.1
  27.9 1.6 %collective-permute-start.12 = (bf16[64,2048]{1,0:T(8,128)(2,1)S(1)}, bf16[64,2048]{1,0:T(8,128)(2,1)S(1)}, u32[]{:S(2)}, u32[]{:S(2)}) collective-permute-start(bf16[64,2048]{1,0:T(8,128)(2,1)S(1)} %fusion.7), channel_id=1, source_target_pairs={{0,4},{2,6},{4,0},{6,2},{8,12},{10,14},{12,8},{14,10},{16,20},{18,... | collective-permute-start | bytes 786440 | tf_op jit(solution)/shard_map/ppermute | solution.py:14
  29.5 1.5 %fusion.60 = f32[128,2048]{1,0:T(8,128)} fusion(bf16[64,2048]{1,0:T(8,128)(2,1)S(1)} %fusion.7, s32[64]{0:T(128)S(1)} %copy-done.33, s32[128]{0:T(128)S(1)} %copy-done.18, s32[128]{0:T(128)S(1)} %get-tuple-element.61, pred[128]{0:T(512)(128)(4,1)S(1)} %copy-done.24, s32[128]{0:T(128)S(1)} %copy-done.21, s32[128]{0:T(128)S(1)} %copy-done.15, ...), kind=kOutput, calls=%fused_computation.132 | convolution fusion | flops 33652736 | bytes 1313856 | tf_op jit(solution)/shard_map/dot_general | solution.py:22
  31.4 0.6 collective-permute-start.13
  32.4 3.8 %collective-permute-done.4 = bf16[32,4096]{1,0:T(8,128)(2,1)S(1)} collective-permute-done((bf16[32,4096]{1,0:T(8,128)(2,1)}, bf16[32,4096]{1,0:T(8,128)(2,1)S(1)}, u32[]{:S(2)}, u32[]{:S(2)}) %collective-permute-start.4) | collective-permute-done | bytes 262176 | tf_op jit(solution)/shard_map/ppermute | solution.py:14
  36.4 8.1 %fusion.69 = f32[256,2048]{1,0:T(8,128)S(1)} fusion(bf16[256,4096]{1,0:T(8,128)(2,1)S(1)} %copy-done, bf16[4096,2048]{1,0:T(8,128)(2,1)} %param.7), kind=kOutput, calls=%fused_computation.141 | convolution fusion | flops 4294967296 | bytes 20971520 | tf_op jit(solution)/shard_map/dot_general | solution.py:22
  44.6 1.0 dynamic-slice_convert_fusion
  45.5 1.0 %pad_maximum_fusion = bf16[128,4096]{1,0:T(8,128)(2,1)S(1)} fusion(bf16[32,4096]{1,0:T(8,128)(2,1)S(1)} %collective-permute-done.9, bf16[32,4096]{1,0:T(8,128)(2,1)S(1)} %collective-permute-done.8, bf16[32,4096]{1,0:T(8,128)(2,1)S(1)} %collective-permute-done.4, bf16[32,4096]{1,0:T(8,128)(2,1)} %bitcast.1), kind=kLoop, calls=%fused_computation.34 | loop fusion | flops 4194304 | bytes 2097152 | tf_op jit(solution)/shard_map/concatenate | solution.py:165
  47.1 1.6 %collective-permute-start.7 = (bf16[128,2048]{1,0:T(8,128)(2,1)}, bf16[128,2048]{1,0:T(8,128)(2,1)}, u32[]{:S(2)}, u32[]{:S(2)}) collective-permute-start(bf16[128,2048]{1,0:T(8,128)(2,1)} %dynamic-slice_convert_fusion), channel_id=1, source_target_pairs={{0,1},{1,0},{2,3},{3,2},{4,5},{5,4},{6,7},{7,6},{8,9},{9,8},{10,11... | collective-permute-start | bytes 1572872 | tf_op jit(solution)/shard_map/ppermute | solution.py:18
  49.7 1.3 %fusion.62 = f32[64,4096]{1,0:T(8,128)} fusion(bf16[128,4096]{1,0:T(8,128)(2,1)S(1)} %pad_maximum_fusion, s32[64]{0:T(128)S(1)} %copy-done.33, s32[128]{0:T(128)S(1)} %copy-done.18, s32[128]{0:T(128)S(1)} %get-tuple-element.61, pred[128]{0:T(512)(128)(4,1)S(1)} %copy-done.24, s32[128]{0:T(128)S(1)} %copy-done.21, s32[128]{0:T(128)S(1)} %copy-done.15, ...), kind=kOutput, calls=%fused_computation.134 | convolution fusion | flops 67207168 | bytes 2100288 | tf_op jit(solution)/shard_map/dot_general | solution.py:22
  51.1 1.1 %fusion.1 = bf16[64,4096]{1,0:T(8,128)(2,1)} fusion(f32[64,4096]{1,0:T(8,128)S(1)} %fusion.57, bf16[128,4096]{1,0:T(8,128)(2,1)S(1)} %collective-permute-done.10, s32[128]{0:T(128)S(1)} %copy-done.18, s32[128]{0:T(128)S(1)} %get-tuple-element.61, s32[64]{0:T(128)S(1)} %copy-done.36, pred[128]{0:T(512)(128)(4,1)S(1)} %copy-done.24, s32[128]{0:T(128)S(1)} %copy-done.21, ...), kind=kOutput, calls=%fused_computation.5 | convolution fusion | flops 67739648 | bytes 2624576 | tf_op jit(solution)/shard_map/dot_general | solution.py:22
  52.7 0.8 slice.177
  53.5 1.7 %collective-permute-start.16 = (bf16[64,2048]{1,0:T(8,128)(2,1)}, bf16[64,2048]{1,0:T(8,128)(2,1)}, u32[]{:S(2)}, u32[]{:S(2)}) collective-permute-start(bf16[64,2048]{1,0:T(8,128)(2,1)} %slice.177), channel_id=1, source_target_pairs={{0,8},{2,10},{4,12},{6,14},{8,0},{10,2},{12,4},{14,6},{16,24},{18,... | collective-permute-start | bytes 786440 | tf_op jit(solution)/shard_map/ppermute | solution.py:14
  55.2 1.2 %fusion.5 = bf16[128,2048]{1,0:T(8,128)(2,1)} fusion(f32[128,2048]{1,0:T(8,128)S(1)} %fusion.65, bf16[64,2048]{1,0:T(8,128)(2,1)S(1)} %collective-permute-done.12, s32[128]{0:T(128)S(1)} %copy-done.18, s32[128]{0:T(128)S(1)} %get-tuple-element.61, s32[64]{0:T(128)S(1)} %copy-done.36, pred[128]{0:T(512)(128)(4,1)S(1)} %copy-done.24, s32[128]{0:T(128)S(1)} %copy-done.21, ...), kind=kOutput, calls=%fused_computation.15 | convolution fusion | flops 34185216 | bytes 1838144 | tf_op jit(solution)/shard_map/dot_general | solution.py:22
  56.4 1.5 %collective-permute-start.11 = (bf16[64,4096]{1,0:T(8,128)(2,1)}, bf16[64,4096]{1,0:T(8,128)(2,1)}, u32[]{:S(2)}, u32[]{:S(2)}) collective-permute-start(bf16[64,4096]{1,0:T(8,128)(2,1)} %fusion.1), channel_id=1, source_target_pairs={{0,4},{2,6},{4,0},{6,2},{8,12},{10,14},{12,8},{14,10},{16,20},{18,... | collective-permute-start | bytes 1572872 | tf_op jit(solution)/shard_map/ppermute | solution.py:14
  57.9 10.2 %fusion.70 = f32[256,4096]{1,0:T(8,128)} fusion(bf16[256,2048]{1,0:T(8,128)(2,1)S(1)} %maximum_select_fusion, bf16[4096,2048]{1,0:T(8,128)(2,1)} %param.7), kind=kOutput, calls=%fused_computation.142 | convolution fusion | flops 4294967296 | bytes 22020096 | tf_op jit(solution)/shard_map/dot_general | solution.py:22
  68.1 2.0 %convolution_add_fusion.2 = f32[64,4096]{1,0:T(8,128)S(1)} fusion(f32[64,4096]{1,0:T(8,128)} %fusion.62, bf16[128,4096]{1,0:T(8,128)(2,1)} %copy-done.1, s32[64]{0:T(128)} %copy-done.32, s32[128]{0:T(128)} %copy-done.17, s32[128]{0:T(128)S(1)} %get-tuple-element.61, pred[128]{0:T(512)(128)(4,1)} %copy-done.23, s32[128]{0:T(128)} %copy-done.20, ...), kind=kOutput, calls=%fused_computation.3 | convolution fusion | flops 67477504 | bytes 3148864 | tf_op jit(solution)/shard_map/dot_general | solution.py:22
  70.2 0.9 fusion.18
  71.2 1.5 %fusion = bf16[64,4096]{1,0:T(8,128)(2,1)S(1)} fusion(f32[64,4096]{1,0:T(8,128)S(1)} %convolution_add_fusion.2, bf16[64,4096]{1,0:T(8,128)(2,1)} %collective-permute-done.11, pred[64]{0:T(512)(128)(4,1)S(1)} %copy-done.51), kind=kOutput, calls=%fused_computation.4 | convolution fusion | flops 34086912 | bytes 2097216 | tf_op jit(solution)/shard_map/dot_general | solution.py:22
  72.7 0.8 convolution_select_fusion.1
  73.5 0.7 collective-permute-start.15
  74.3 1.5 %fusion.2 = f32[128,2048]{1,0:T(8,128)S(1)} fusion(f32[128,2048]{1,0:T(8,128)S(1)} %copy-done.3, bf16[64,2048]{1,0:T(8,128)(2,1)S(1)} %collective-permute-done.12, bf16[128,2048]{1,0:T(8,128)(2,1)} %collective-permute-done.18, s32[128]{0:T(128)S(1)} %copy-done.19, s32[128]{0:T(128)S(1)} %get-tuple-element.61, s32[64]{0:T(128)S(1)} %copy-done.37, ...), kind=kOutput, calls=%fused_computation.8 | convolution fusion | flops 34439168 | bytes 2886720 | tf_op jit(solution)/shard_map/dot_general | solution.py:22
  75.8 1.2 %collective-permute-start.17 = (bf16[32,2048]{1,0:T(8,128)(2,1)S(1)}, bf16[32,2048]{1,0:T(8,128)(2,1)S(1)}, u32[]{:S(2)}, u32[]{:S(2)}) collective-permute-start(bf16[32,2048]{1,0:T(8,128)(2,1)S(1)} %fusion.18), channel_id=1, source_target_pairs={{0,16},{2,18},{4,20},{6,22},{8,24},{10,26},{12,28},{14,30},{16,0},... | collective-permute-start | bytes 393224 | tf_op jit(solution)/shard_map/ppermute | solution.py:14
  77.0 1.7 %collective-permute-start.19 = (bf16[64,2048]{1,0:T(8,128)(2,1)S(1)}, bf16[64,2048]{1,0:T(8,128)(2,1)S(1)}, u32[]{:S(2)}, u32[]{:S(2)}) collective-permute-start(bf16[64,2048]{1,0:T(8,128)(2,1)S(1)} %slice.176), channel_id=1, source_target_pairs={{0,8},{2,10},{4,12},{6,14},{8,0},{10,2},{12,4},{14,6},{16,24},{18,... | collective-permute-start | bytes 786440 | tf_op jit(solution)/shard_map/ppermute | solution.py:14
  79.1 1.4 %collective-permute-start.21 = (bf16[64,512]{1,0:T(8,128)(2,1)S(1)}, bf16[64,512]{1,0:T(8,128)(2,1)S(1)}, u32[]{:S(2)}, u32[]{:S(2)}) collective-permute-start(bf16[64,512]{1,0:T(8,128)(2,1)S(1)} %select_convert_fusion), channel_id=1, source_target_pairs={{0,4},{2,6},{4,0},{6,2},{8,12},{10,14},{12,8},{14,10},{16,20},{18,... | collective-permute-start | bytes 196616 | tf_op jit(solution)/shard_map/ppermute | solution.py:14
  80.5 0.7 convolution_multiply_fusion
  81.3 1.8 %add_convert_fusion = bf16[256,4096]{1,0:T(8,128)(2,1)} fusion(f32[256,4096]{1,0:T(8,128)S(1)} %copy-done.2, f32[256,4096]{1,0:T(8,128)S(1)} %convolution_multiply_fusion), kind=kLoop, calls=%fused_computation.6 | loop fusion | flops 2097152 | bytes 10485760 | tf_op jit(solution)/shard_map/convert_element_type | solution.py:231
  83.5 2.2 %add_convert_fusion.1 = bf16[128,2048]{1,0:T(8,128)(2,1)} fusion(bf16[128,2048]{1,0:T(8,128)(2,1)} %collective-permute-done.7, f32[256,2048]{1,0:T(8,128)S(1)} %copy-done.7, s32[]{:T(128)S(6)} %select_n.168, bf16[64,1024]{1,0:T(8,128)(2,1)S(1)} %get-tuple-element.46, bf16[64,1024]{1,0:T(8,128)(2,1)S(1)} %copy-done.10, pred[]{:T(512)S(6)} %eq.111, ...), kind=kOutput, calls=%fused_computation.35 | convolution fusion | flops 18743296 | bytes 2369536 | tf_op jit(solution)/shard_map/dot_general | solution.py:22
  86.0 1.0 fusion.19
  87.0 0.7 collective-permute-done.19
  88.4 0.9 collective-permute-done.22
  89.7 0.9 collective-permute-start.24
  90.6 2.3 %collective-permute-start.25 = (bf16[32,512]{1,0:T(8,128)(2,1)S(1)}, bf16[32,512]{1,0:T(8,128)(2,1)S(1)}, u32[]{:S(2)}, u32[]{:S(2)}) collective-permute-start(bf16[32,512]{1,0:T(8,128)(2,1)S(1)} %get-tuple-element.45), channel_id=1, source_target_pairs={{0,24},{2,26},{4,28},{6,30},{8,16},{10,18},{12,20},{14,22},{16,8},... | collective-permute-start | bytes 98312 | tf_op jit(solution)/shard_map/ppermute | solution.py:14
  93.3 5.4 %collective-permute-done.20 = bf16[32,2048]{1,0:T(8,128)(2,1)S(1)} collective-permute-done((bf16[32,2048]{1,0:T(8,128)(2,1)S(1)}, bf16[32,2048]{1,0:T(8,128)(2,1)S(1)}, u32[]{:S(2)}, u32[]{:S(2)}) %collective-permute-start.20) | collective-permute-done | bytes 131104 | tf_op jit(solution)/shard_map/ppermute | solution.py:14
  98.7 0.8 maximum_bitcast_fusion
  100.0 0.6 fusion.30
  (173 shorter events, 12.7 us)
Async XLA Ops:
  0.6 23.9 %copy-start.8 = (bf16[128,2048]{1,0:T(8,128)(2,1)S(1)}, bf16[128,2048]{1,0:T(8,128)(2,1)}, u32[]{:S(2)}) copy-start(bf16[128,2048]{1,0:T(8,128)(2,1)} %param.11) | copy-start | bytes 1572868
  0.6 12.6 %collective-permute-start = (s32[2,1]{0,1:T(1,128)}, s32[2,1]{0,1:T(1,128)S(1)}, u32[]{:S(2)}, u32[]{:S(2)}) collective-permute-start(s32[2,1]{0,1:T(1,128)} %param.10), channel_id=1, source_target_pairs={{0,4},{2,6},{4,0},{6,2},{8,12},{10,14},{12,8},{14,10},{16,20},{18,... | collective-permute-start | bytes 32 | tf_op jit(solution)/shard_map/ppermute | solution.py:14
  3.6 6.1 %collective-permute-start.1 = (bf16[32,1024]{1,0:T(8,128)(2,1)}, bf16[32,1024]{1,0:T(8,128)(2,1)S(1)}, u32[]{:S(2)}, u32[]{:S(2)}) collective-permute-start(bf16[32,1024]{1,0:T(8,128)(2,1)} %bitcast.46), channel_id=1, source_target_pairs={{0,16},{2,18},{4,20},{6,22},{8,24},{10,26},{12,28},{14,30},{16,0},... | collective-permute-start | bytes 196616 | tf_op jit(solution)/shard_map/ppermute | solution.py:14
  6.2 18.2 %collective-permute-start.6 = (bf16[128,2048]{1,0:T(8,128)(2,1)}, bf16[128,2048]{1,0:T(8,128)(2,1)S(1)}, u32[]{:S(2)}, u32[]{:S(2)}) collective-permute-start(bf16[128,2048]{1,0:T(8,128)(2,1)} %param.11), channel_id=1, source_target_pairs={{0,1},{1,0},{2,3},{3,2},{4,5},{5,4},{6,7},{7,6},{8,9},{9,8},{10,11... | collective-permute-start | bytes 1572872 | tf_op jit(solution)/shard_map/ppermute | solution.py:18
  7.8 17.3 %copy-start.14 = (s32[128]{0:T(128)}, s32[128]{0:T(128)S(1)}, u32[]{:S(2)}) copy-start(s32[128]{0:T(128)S(1)} %get-tuple-element.62) | copy-start | bytes 1540
  7.8 17.0 %copy-start.20 = (s32[128]{0:T(128)}, s32[128]{0:T(128)S(1)}, u32[]{:S(2)}) copy-start(s32[128]{0:T(128)S(1)} %get-tuple-element.58) | copy-start | bytes 1540
  7.8 17.3 %copy-start.17 = (s32[128]{0:T(128)}, s32[128]{0:T(128)S(1)}, u32[]{:S(2)}) copy-start(s32[128]{0:T(128)S(1)} %get-tuple-element.57) | copy-start | bytes 1540
  8.4 16.4 %copy-start.23 = (pred[128]{0:T(512)(128)(4,1)}, pred[128]{0:T(512)(128)(4,1)S(1)}, u32[]{:S(2)}) copy-start(pred[128]{0:T(512)(128)(4,1)S(1)} %get-tuple-element.55) | copy-start | bytes 388
  8.4 16.4 %copy-start.26 = (pred[128]{0:T(512)(128)(4,1)}, pred[128]{0:T(512)(128)(4,1)S(1)}, u32[]{:S(2)}) copy-start(pred[128]{0:T(512)(128)(4,1)S(1)} %get-tuple-element.56) | copy-start | bytes 388
  10.6 5.0 %collective-permute-start.2 = (bf16[64,1024]{1,0:T(8,128)(2,1)S(1)}, bf16[64,1024]{1,0:T(8,128)(2,1)S(1)}, u32[]{:S(2)}, u32[]{:S(2)}) collective-permute-start(bf16[64,1024]{1,0:T(8,128)(2,1)S(1)} %pad_maximum_fusion.4), channel_id=1, source_target_pairs={{0,8},{2,10},{4,12},{6,14},{8,0},{10,2},{12,4},{14,6},{16,24},{18,... | collective-permute-start | bytes 393224 | tf_op jit(solution)/shard_map/ppermute | solution.py:14
  15.6 8.8 %copy-start.30 = (bf16[64,1024]{1,0:T(8,128)(2,1)}, bf16[64,1024]{1,0:T(8,128)(2,1)S(1)}, u32[]{:S(2)}) copy-start(bf16[64,1024]{1,0:T(8,128)(2,1)S(1)} %collective-permute-done.2) | copy-start | bytes 393220
  16.5 1.6 %collective-permute-start.3 = (bf16[128,1024]{1,0:T(8,128)(2,1)S(1)}, bf16[128,1024]{1,0:T(8,128)(2,1)S(1)}, u32[]{:S(2)}, u32[]{:S(2)}) collective-permute-start(bf16[128,1024]{1,0:T(8,128)(2,1)S(1)} %pad_maximum_fusion.3), channel_id=1, source_target_pairs={{0,2},{2,0},{4,6},{6,4},{8,10},{10,8},{12,14},{14,12},{16,18},{18,... | collective-permute-start | bytes 786440 | tf_op jit(solution)/shard_map/ppermute | solution.py:14
  17.4 7.7 %copy-start.32 = (s32[64]{0:T(128)}, s32[64]{0:T(128)S(1)}, u32[]{:S(2)}) copy-start(s32[64]{0:T(128)S(1)} %broadcast_in_dim.60) | copy-start | bytes 772
  17.6 7.6 %copy-start.35 = (s32[64]{0:T(128)}, s32[64]{0:T(128)S(1)}, u32[]{:S(2)}) copy-start(s32[64]{0:T(128)S(1)} %broadcast_in_dim.54) | copy-start | bytes 772
  17.6 7.6 %copy-start.50 = (pred[64]{0:T(512)(128)(4,1)}, pred[64]{0:T(512)(128)(4,1)S(1)}, u32[]{:S(2)}) copy-start(pred[64]{0:T(512)(128)(4,1)S(1)} %and_compare_fusion) | copy-start | bytes 196
  18.3 7.0 %copy-start.13 = (bf16[1,32,1024]{2,1,0:T(8,128)(2,1)S(1)}, bf16[1,32,1024]{2,1,0:T(8,128)(2,1)}, u32[]{:S(2)}) copy-start(bf16[1,32,1024]{2,1,0:T(8,128)(2,1)} %param.9) | copy-start | bytes 196612
  19.5 5.6 %collective-permute-start.5 = (bf16[64,1024]{1,0:T(8,128)(2,1)S(1)}, bf16[64,1024]{1,0:T(8,128)(2,1)S(1)}, u32[]{:S(2)}, u32[]{:S(2)}) collective-permute-start(bf16[64,1024]{1,0:T(8,128)(2,1)S(1)} %fusion.10), channel_id=1, source_target_pairs={{0,4},{2,6},{4,0},{6,2},{8,12},{10,14},{12,8},{14,10},{16,20},{18,... | collective-permute-start | bytes 393224 | tf_op jit(solution)/shard_map/ppermute | solution.py:14
  20.1 25.4 %collective-permute-start.8 = (bf16[32,4096]{1,0:T(8,128)(2,1)}, bf16[32,4096]{1,0:T(8,128)(2,1)S(1)}, u32[]{:S(2)}, u32[]{:S(2)}) collective-permute-start(bf16[32,4096]{1,0:T(8,128)(2,1)} %bitcast.1), channel_id=1, source_target_pairs={{0,8},{2,10},{4,12},{6,14},{8,0},{10,2},{12,4},{14,6},{16,24},{18,... | collective-permute-start | bytes 786440 | tf_op jit(solution)/shard_map/ppermute | solution.py:14
  21.7 14.6 %collective-permute-start.4 = (bf16[32,4096]{1,0:T(8,128)(2,1)}, bf16[32,4096]{1,0:T(8,128)(2,1)S(1)}, u32[]{:S(2)}, u32[]{:S(2)}) collective-permute-start(bf16[32,4096]{1,0:T(8,128)(2,1)} %bitcast.1), channel_id=1, source_target_pairs={{0,16},{2,18},{4,20},{6,22},{8,24},{10,26},{12,28},{14,30},{16,0},... | collective-permute-start | bytes 786440 | tf_op jit(solution)/shard_map/ppermute | solution.py:14
  27.9 27.3 %collective-permute-start.12 = (bf16[64,2048]{1,0:T(8,128)(2,1)S(1)}, bf16[64,2048]{1,0:T(8,128)(2,1)S(1)}, u32[]{:S(2)}, u32[]{:S(2)}) collective-permute-start(bf16[64,2048]{1,0:T(8,128)(2,1)S(1)} %fusion.7), channel_id=1, source_target_pairs={{0,4},{2,6},{4,0},{6,2},{8,12},{10,14},{12,8},{14,10},{16,20},{18,... | collective-permute-start | bytes 786440 | tf_op jit(solution)/shard_map/ppermute | solution.py:14
  31.4 17.3 %collective-permute-start.13 = (bf16[64,2048]{1,0:T(8,128)(2,1)S(1)}, bf16[64,2048]{1,0:T(8,128)(2,1)S(1)}, u32[]{:S(2)}, u32[]{:S(2)}) collective-permute-start(bf16[64,2048]{1,0:T(8,128)(2,1)S(1)} %fusion.6), channel_id=1, source_target_pairs={{0,4},{2,6},{4,0},{6,2},{8,12},{10,14},{12,8},{14,10},{16,20},{18,... | collective-permute-start | bytes 786440 | tf_op jit(solution)/shard_map/ppermute | solution.py:14
  36.2 9.3 %collective-permute-start.9 = (bf16[32,4096]{1,0:T(8,128)(2,1)S(1)}, bf16[32,4096]{1,0:T(8,128)(2,1)S(1)}, u32[]{:S(2)}, u32[]{:S(2)}) collective-permute-start(bf16[32,4096]{1,0:T(8,128)(2,1)S(1)} %collective-permute-done.4), channel_id=1, source_target_pairs={{0,8},{2,10},{4,12},{6,14},{8,0},{10,2},{12,4},{14,6},{16,24},{18,... | collective-permute-start | bytes 786440 | tf_op jit(solution)/shard_map/ppermute | solution.py:14
  44.6 4.1 %copy-start.36 = (s32[64]{0:T(128)S(1)}, s32[64]{0:T(128)}, u32[]{:S(2)}) copy-start(s32[64]{0:T(128)} %copy-done.35) | copy-start | bytes 772
  46.6 4.5 %collective-permute-start.10 = (bf16[128,4096]{1,0:T(8,128)(2,1)S(1)}, bf16[128,4096]{1,0:T(8,128)(2,1)S(1)}, u32[]{:S(2)}, u32[]{:S(2)}) collective-permute-start(bf16[128,4096]{1,0:T(8,128)(2,1)S(1)} %pad_maximum_fusion), channel_id=1, source_target_pairs={{0,2},{2,0},{4,6},{6,4},{8,10},{10,8},{12,14},{14,12},{16,18},{18,... | collective-permute-start | bytes 3145736 | tf_op jit(solution)/shard_map/ppermute | solution.py:14
  47.1 36.4 %collective-permute-start.7 = (bf16[128,2048]{1,0:T(8,128)(2,1)}, bf16[128,2048]{1,0:T(8,128)(2,1)}, u32[]{:S(2)}, u32[]{:S(2)}) collective-permute-start(bf16[128,2048]{1,0:T(8,128)(2,1)} %dynamic-slice_convert_fusion), channel_id=1, source_target_pairs={{0,1},{1,0},{2,3},{3,2},{4,5},{5,4},{6,7},{7,6},{8,9},{9,8},{10,11... | collective-permute-start | bytes 1572872 | tf_op jit(solution)/shard_map/ppermute | solution.py:18
  49.1 3.1 %collective-permute-start.14 = (bf16[128,2048]{1,0:T(8,128)(2,1)S(1)}, bf16[128,2048]{1,0:T(8,128)(2,1)S(1)}, u32[]{:S(2)}, u32[]{:S(2)}) collective-permute-start(bf16[128,2048]{1,0:T(8,128)(2,1)S(1)} %fusion.4), channel_id=1, source_target_pairs={{0,2},{2,0},{4,6},{6,4},{8,10},{10,8},{12,14},{14,12},{16,18},{18,... | collective-permute-start | bytes 1572872 | tf_op jit(solution)/shard_map/ppermute | solution.py:14
  52.7 3.7 %copy-start.4 = (f32[128,2048]{1,0:T(8,128)}, f32[128,2048]{1,0:T(8,128)S(1)}, u32[]{:S(2)}) copy-start(f32[128,2048]{1,0:T(8,128)S(1)} %fusion.3) | copy-start | bytes 3145732
  53.5 16.7 %collective-permute-start.16 = (bf16[64,2048]{1,0:T(8,128)(2,1)}, bf16[64,2048]{1,0:T(8,128)(2,1)}, u32[]{:S(2)}, u32[]{:S(2)}) collective-permute-start(bf16[64,2048]{1,0:T(8,128)(2,1)} %slice.177), channel_id=1, source_target_pairs={{0,8},{2,10},{4,12},{6,14},{8,0},{10,2},{12,4},{14,6},{16,24},{18,... | collective-permute-start | bytes 786440 | tf_op jit(solution)/shard_map/ppermute | solution.py:14
  56.4 17.8 %collective-permute-start.18 = (bf16[128,2048]{1,0:T(8,128)(2,1)}, bf16[128,2048]{1,0:T(8,128)(2,1)}, u32[]{:S(2)}, u32[]{:S(2)}) collective-permute-start(bf16[128,2048]{1,0:T(8,128)(2,1)} %fusion.5), channel_id=1, source_target_pairs={{0,2},{2,0},{4,6},{6,4},{8,10},{10,8},{12,14},{14,12},{16,18},{18,... | collective-permute-start | bytes 1572872 | tf_op jit(solution)/shard_map/ppermute | solution.py:14
  56.4 14.7 %collective-permute-start.11 = (bf16[64,4096]{1,0:T(8,128)(2,1)}, bf16[64,4096]{1,0:T(8,128)(2,1)}, u32[]{:S(2)}, u32[]{:S(2)}) collective-permute-start(bf16[64,4096]{1,0:T(8,128)(2,1)} %fusion.1), channel_id=1, source_target_pairs={{0,4},{2,6},{4,0},{6,2},{8,12},{10,14},{12,8},{14,10},{16,20},{18,... | collective-permute-start | bytes 1572872 | tf_op jit(solution)/shard_map/ppermute | solution.py:14
  68.1 3.1 %copy-start.51 = (pred[64]{0:T(512)(128)(4,1)S(1)}, pred[64]{0:T(512)(128)(4,1)}, u32[]{:S(2)}) copy-start(pred[64]{0:T(512)(128)(4,1)} %copy-done.50) | copy-start | bytes 196
  71.1 3.1 %copy-start.3 = (f32[128,2048]{1,0:T(8,128)S(1)}, f32[128,2048]{1,0:T(8,128)}, u32[]{:S(2)}) copy-start(f32[128,2048]{1,0:T(8,128)} %fusion.60) | copy-start | bytes 3145732
  71.1 3.1 %copy-start.16 = (s32[128]{0:T(128)S(1)}, s32[128]{0:T(128)}, u32[]{:S(2)}) copy-start(s32[128]{0:T(128)} %copy-done.14) | copy-start | bytes 1540
  71.1 3.1 %copy-start.19 = (s32[128]{0:T(128)S(1)}, s32[128]{0:T(128)}, u32[]{:S(2)}) copy-start(s32[128]{0:T(128)} %copy-done.17) | copy-start | bytes 1540
  71.1 3.1 %copy-start.22 = (s32[128]{0:T(128)S(1)}, s32[128]{0:T(128)}, u32[]{:S(2)}) copy-start(s32[128]{0:T(128)} %copy-done.20) | copy-start | bytes 1540
  71.1 3.1 %copy-start.25 = (pred[128]{0:T(512)(128)(4,1)S(1)}, pred[128]{0:T(512)(128)(4,1)}, u32[]{:S(2)}) copy-start(pred[128]{0:T(512)(128)(4,1)} %copy-done.23) | copy-start | bytes 388
  71.2 3.1 %copy-start.28 = (pred[128]{0:T(512)(128)(4,1)S(1)}, pred[128]{0:T(512)(128)(4,1)}, u32[]{:S(2)}) copy-start(pred[128]{0:T(512)(128)(4,1)} %copy-done.26) | copy-start | bytes 388
  73.5 5.6 %copy-start.29 = (pred[64,1024]{1,0:T(8,128)(4,1)S(1)}, pred[64,1024]{1,0:T(8,128)(4,1)}, u32[]{:S(2)}) copy-start(pred[64,1024]{1,0:T(8,128)(4,1)} %select_compare_fusion) | copy-start | bytes 196612
  73.5 7.0 %copy-start.12 = (bf16[64,256]{1,0:T(8,128)(2,1)S(1)}, bf16[64,256]{1,0:T(8,128)(2,1)}, u32[]{:S(2)}) copy-start(bf16[64,256]{1,0:T(8,128)(2,1)} %copy-done.11) | copy-start | bytes 98308
  73.5 5.2 %collective-permute-start.15 = (f32[32,256]{1,0:T(8,128)S(1)}, f32[32,256]{1,0:T(8,128)S(1)}, u32[]{:S(2)}, u32[]{:S(2)}) collective-permute-start(f32[32,256]{1,0:T(8,128)S(1)} %slice_add_fusion.5), channel_id=1, source_target_pairs={{0,1},{1,0},{2,3},{3,2},{4,5},{5,4},{6,7},{7,6},{8,9},{9,8},{10,11... | collective-permute-start | bytes 98312 | tf_op jit(solution)/shard_map/ppermute | solution.py:18
  75.8 10.2 %collective-permute-start.17 = (bf16[32,2048]{1,0:T(8,128)(2,1)S(1)}, bf16[32,2048]{1,0:T(8,128)(2,1)S(1)}, u32[]{:S(2)}, u32[]{:S(2)}) collective-permute-start(bf16[32,2048]{1,0:T(8,128)(2,1)S(1)} %fusion.18), channel_id=1, source_target_pairs={{0,16},{2,18},{4,20},{6,22},{8,24},{10,26},{12,28},{14,30},{16,0},... | collective-permute-start | bytes 393224 | tf_op jit(solution)/shard_map/ppermute | solution.py:14
  77.0 10.7 %collective-permute-start.19 = (bf16[64,2048]{1,0:T(8,128)(2,1)S(1)}, bf16[64,2048]{1,0:T(8,128)(2,1)S(1)}, u32[]{:S(2)}, u32[]{:S(2)}) collective-permute-start(bf16[64,2048]{1,0:T(8,128)(2,1)S(1)} %slice.176), channel_id=1, source_target_pairs={{0,8},{2,10},{4,12},{6,14},{8,0},{10,2},{12,4},{14,6},{16,24},{18,... | collective-permute-start | bytes 786440 | tf_op jit(solution)/shard_map/ppermute | solution.py:14
  79.1 7.8 %collective-permute-start.21 = (bf16[64,512]{1,0:T(8,128)(2,1)S(1)}, bf16[64,512]{1,0:T(8,128)(2,1)S(1)}, u32[]{:S(2)}, u32[]{:S(2)}) collective-permute-start(bf16[64,512]{1,0:T(8,128)(2,1)S(1)} %select_convert_fusion), channel_id=1, source_target_pairs={{0,4},{2,6},{4,0},{6,2},{8,12},{10,14},{12,8},{14,10},{16,20},{18,... | collective-permute-start | bytes 196616 | tf_op jit(solution)/shard_map/ppermute | solution.py:14
  87.9 1.4 %collective-permute-start.22 = (bf16[128,512]{1,0:T(8,128)(2,1)S(1)}, bf16[128,512]{1,0:T(8,128)(2,1)S(1)}, u32[]{:S(2)}, u32[]{:S(2)}) collective-permute-start(bf16[128,512]{1,0:T(8,128)(2,1)S(1)} %fusion.12), channel_id=1, source_target_pairs={{0,2},{2,0},{4,6},{6,4},{8,10},{10,8},{12,14},{14,12},{16,18},{18,... | collective-permute-start | bytes 393224 | tf_op jit(solution)/shard_map/ppermute | solution.py:14
  88.1 10.6 %collective-permute-start.20 = (bf16[32,2048]{1,0:T(8,128)(2,1)S(1)}, bf16[32,2048]{1,0:T(8,128)(2,1)S(1)}, u32[]{:S(2)}, u32[]{:S(2)}) collective-permute-start(bf16[32,2048]{1,0:T(8,128)(2,1)S(1)} %fusion.16), channel_id=1, source_target_pairs={{0,16},{2,18},{4,20},{6,22},{8,24},{10,26},{12,28},{14,30},{16,0},... | collective-permute-start | bytes 393224 | tf_op jit(solution)/shard_map/ppermute | solution.py:14
  89.7 9.8 %collective-permute-start.24 = (bf16[32,512]{1,0:T(8,128)(2,1)S(1)}, bf16[32,512]{1,0:T(8,128)(2,1)S(1)}, u32[]{:S(2)}, u32[]{:S(2)}) collective-permute-start(bf16[32,512]{1,0:T(8,128)(2,1)S(1)} %get-tuple-element.44), channel_id=1, source_target_pairs={{0,8},{2,10},{4,12},{6,14},{8,0},{10,2},{12,4},{14,6},{16,24},{18,... | collective-permute-start | bytes 98312 | tf_op jit(solution)/shard_map/ppermute | solution.py:14
  90.6 8.9 %collective-permute-start.25 = (bf16[32,512]{1,0:T(8,128)(2,1)S(1)}, bf16[32,512]{1,0:T(8,128)(2,1)S(1)}, u32[]{:S(2)}, u32[]{:S(2)}) collective-permute-start(bf16[32,512]{1,0:T(8,128)(2,1)S(1)} %get-tuple-element.45), channel_id=1, source_target_pairs={{0,24},{2,26},{4,28},{6,30},{8,16},{10,18},{12,20},{14,22},{16,8},... | collective-permute-start | bytes 98312 | tf_op jit(solution)/shard_map/ppermute | solution.py:14
  92.9 7.1 %collective-permute-start.23 = (bf16[32,512]{1,0:T(8,128)(2,1)S(1)}, bf16[32,512]{1,0:T(8,128)(2,1)S(1)}, u32[]{:S(2)}, u32[]{:S(2)}) collective-permute-start(bf16[32,512]{1,0:T(8,128)(2,1)S(1)} %get-tuple-element.43), channel_id=1, source_target_pairs={{0,16},{2,18},{4,20},{6,22},{8,24},{10,26},{12,28},{14,30},{16,0},... | collective-permute-start | bytes 98312 | tf_op jit(solution)/shard_map/ppermute | solution.py:14
  (30 other events, 68.1 us)

commit v4 on v3

--- a/solution.py
+++ b/solution.py
@@ -164,14 +164,16 @@
         blocks_a = blocks_a + [swap(block, 1 << bit) for block in blocks_a]
     here_a = jnp.concatenate(blocks_a, axis=0)
     if tp_count == 2:
-        base = dot(after(tokens, late_hop), weight, (1, 0))
+        base = dot(after(tokens, sent_b), weight, (1, 0))
         near_base = lax.dynamic_slice_in_dim(base, col * local_rows, local_rows, 0)
         far_base = lax.dynamic_slice_in_dim(base, (1 - col) * local_rows, local_rows, 0).astype(bf16)
         base_rows = near_base + cross(far_base).astype(f32)
-        here_a = after(here_a, far_base)
     else:
         far_base = dot(tokens, weight, (1, 0))
         base_rows = lax.psum_scatter(far_base, "tp", scatter_dimension=0, tiled=True)
+    half = features // 2
+    base_low = dot(after(grad_rows, late_hop), weight[:half], (1, 1))
+    here_a = after(here_a, base_low)
     there_a = swap(here_a, core)
     sent_a = give_away(here_a, there_a)
 
@@ -184,9 +186,9 @@
 
     got_c[1] = after(got_c[1], first_gone)
     away = core_part(down[1], got_c[1])
-    base_grad = dot(after(grad_rows, sent_a, away), weight, (1, 1))
-
-    factor_a = take_in(here_a, there_a, after(swap(sent_a, far), base_grad))
+    base_high = dot(after(grad_rows, sent_a, away), weight[half:], (1, 1))
+
+    factor_a = take_in(here_a, there_a, after(swap(sent_a, far), base_high))
     rank_part = jnp.where(keep, dot(factor_a, tokens, (1, 1)), 0.0)
     rank_part = sum(split(rank_part))
 
@@ -227,8 +229,14 @@
     came_up = [swap(t, o) for o, t in zip(places[1:], leave)]
     grad_b = sum([c.astype(f32) for c in came_up], total_up[0])
 
-    lora_grad = dot(after(rank_grad, rank_act), factor_a, (0, 0))
-    token_gradient = (after(base_grad, rank_act) + adapter_scale * lora_grad).astype(bf16)
+    late_grad = after(rank_grad, rank_act)
+    token_gradient = jnp.concatenate(
+        [
+            (after(base, rank_act) + adapter_scale * dot(late_grad, factor, (0, 0))).astype(bf16)
+            for base, factor in ((base_low, factor_a[:, :half]), (base_high, factor_a[:, half:]))
+        ],
+        axis=1,
+    )
     return key_value_output, token_gradient, grad_a.T[None], grad_b[None]
 
 

time: 101 us -> 90.3 us (0.89)
  matrix products: 39.9 us -> 32.8 us
  other arithmetic: 12 us -> 7.4 us
  waiting for transfers between devices: 14.5 us -> 17.1 us
  local copies, waits for them, and re-layouts: 2.71 us -> 1.13 us
    dot_general x31 -> x33, matrix products: 39.9 us -> 32.8 us  [dot(): lax.dot_general(a, b, ((contract[:1], contract[1:]), ((), ())), preferred...]
    concatenate x0 -> x1, other arithmetic: none -> 1.54 us  [on_device(): jnp.concatenate([(after(base, rank_act) + adapter_scale * dot(late_grad,...]
    ppermute x3, waiting for transfers between devices: 0.01 us -> 1.55 us  [cross(): return lax.ppermute(value, 'tp', [(0, 1), (1, 0)])]
    convert_element_type x1 -> x2, other arithmetic: 1.83 us -> 0.69 us  [on_device(): (after(base, rank_act) + adapter_scale * dot(late_grad, factor, (0, 0)))....]
    ppermute x23, waiting for transfers between devices: 14.5 us -> 15.6 us  [swap(): return lax.ppermute(value, 'blk', [(i, i ^ offset) for i in range(count)])]
  transfers between devices with their start and end apart: 26 -> 26, of which waited for: 8 -> 10; matrix products, arithmetic and copies ran while one was open for 53% -> 44% of each run, Pallas kernels for 0% -> 0%
where the time goes in v4:
time: 90.3 us; the launch traced here: 90 us
  matrix products  32.8 us (36%)
  starting transfers between devices  30.3 us (34%)
  waiting for transfers between devices  17.1 us (19%)
  other arithmetic  7.4 us (8%)
  between operations  1.14 us (1%)
  local copies, waits for them, and re-layouts  1.13 us (1%)
    dot_general x33, matrix products, dot(): lax.dot_general(a, b, ((contract[:1], contract[1:]), ((), ())), preferred...  32.8 us
    ppermute x23, starting transfers between devices, swap(): return lax.ppermute(value, 'blk', [(i, i ^ offset) for i in range(count)])  26.6 us
    ppermute x23, waiting for transfers between devices, swap(): return lax.ppermute(value, 'blk', [(i, i ^ offset) for i in range(count)])  15.6 us
    ppermute x3, starting transfers between devices, cross(): return lax.ppermute(value, 'tp', [(0, 1), (1, 0)])  3.68 us
  transfers between devices with their start and end apart: 26, of which 10 were waited for; matrix products, arithmetic and copies ran while one was open for 44% of the time, Pallas kernels for 0%

profile of v4, /device:TPU:0, one launch (start us, length us, event | category | flops | bytes accessed | tf_op | source)
XLA Modules:
  0.0 90.0 jit_solution(10480532725829245920)
XLA Ops:
  0.7 4.1 %collective-permute-start.1 = (bf16[32,1024]{1,0:T(8,128)(2,1)}, bf16[32,1024]{1,0:T(8,128)(2,1)S(1)}, u32[]{:S(2)}, u32[]{:S(2)}) collective-permute-start(bf16[32,1024]{1,0:T(8,128)(2,1)} %bitcast.46), channel_id=1, source_target_pairs={{0,16},{2,18},{4,20},{6,22},{8,24},{10,26},{12,28},{14,30},{16,0},... | collective-permute-start | bytes 196616 | tf_op jit(solution)/shard_map/ppermute | solution.py:14
  4.8 1.5 %collective-permute-start = (s32[2,1]{0,1:T(1,128)}, s32[2,1]{0,1:T(1,128)S(1)}, u32[]{:S(2)}, u32[]{:S(2)}) collective-permute-start(s32[2,1]{0,1:T(1,128)} %param.10), channel_id=1, source_target_pairs={{0,4},{2,6},{4,0},{6,2},{8,12},{10,14},{12,8},{14,10},{16,20},{18,... | collective-permute-start | bytes 32 | tf_op jit(solution)/shard_map/ppermute | solution.py:14
  6.2 1.5 %collective-permute-start.7 = (bf16[128,2048]{1,0:T(8,128)(2,1)}, bf16[128,2048]{1,0:T(8,128)(2,1)S(1)}, u32[]{:S(2)}, u32[]{:S(2)}) collective-permute-start(bf16[128,2048]{1,0:T(8,128)(2,1)} %param.11), channel_id=1, source_target_pairs={{0,1},{1,0},{2,3},{3,2},{4,5},{5,4},{6,7},{7,6},{8,9},{9,8},{10,11... | collective-permute-start | bytes 1572872 | tf_op jit(solution)/shard_map/ppermute | solution.py:18
  7.8 0.7 select_compare_fusion
  8.6 0.9 pad_maximum_fusion.5
  9.5 1.6 %collective-permute-start.2 = (bf16[64,1024]{1,0:T(8,128)(2,1)S(1)}, bf16[64,1024]{1,0:T(8,128)(2,1)S(1)}, u32[]{:S(2)}, u32[]{:S(2)}) collective-permute-start(bf16[64,1024]{1,0:T(8,128)(2,1)S(1)} %pad_maximum_fusion.5), channel_id=1, source_target_pairs={{0,8},{2,10},{4,12},{6,14},{8,0},{10,2},{12,4},{14,6},{16,24},{18,... | collective-permute-start | bytes 393224 | tf_op jit(solution)/shard_map/ppermute | solution.py:14
  11.1 3.4 %collective-permute-done.2 = bf16[64,1024]{1,0:T(8,128)(2,1)S(1)} collective-permute-done((bf16[64,1024]{1,0:T(8,128)(2,1)S(1)}, bf16[64,1024]{1,0:T(8,128)(2,1)S(1)}, u32[]{:S(2)}, u32[]{:S(2)}) %collective-permute-start.2) | collective-permute-done | bytes 131104 | tf_op jit(solution)/shard_map/ppermute | solution.py:14
  14.5 0.7 copy-done.5
  15.2 0.9 pad_maximum_fusion.4
  16.1 0.7 xor_bitcast_fusion
  17.1 0.5 collective-permute-done.3
  17.9 1.2 %fusion.14 = bf16[64,1024]{1,0:T(8,128)(2,1)S(1)} fusion(f32[64,1024]{1,0:T(8,128)S(1)} %fusion.64, s32[128]{0:T(128)S(1)} %get-tuple-element.61, s32[128]{0:T(128)S(1)} %get-tuple-element.65, s32[64]{0:T(128)S(1)} %broadcast_in_dim.54, pred[128]{0:T(512)(128)(4,1)S(1)} %get-tuple-element.59, s32[128]{0:T(128)S(1)} %get-tuple-element.62, ...), kind=kOutput, calls=%fused_computation.34 | convolution fusion | flops 17793024 | bytes 658496 | tf_op jit(solution)/shard_map/dot_general | solution.py:22
  19.0 1.8 %collective-permute-start.6 = (bf16[64,1024]{1,0:T(8,128)(2,1)S(1)}, bf16[64,1024]{1,0:T(8,128)(2,1)S(1)}, u32[]{:S(2)}, u32[]{:S(2)}) collective-permute-start(bf16[64,1024]{1,0:T(8,128)(2,1)S(1)} %fusion.14), channel_id=1, source_target_pairs={{0,4},{2,6},{4,0},{6,2},{8,12},{10,14},{12,8},{14,10},{16,20},{18,... | collective-permute-start | bytes 393224 | tf_op jit(solution)/shard_map/ppermute | solution.py:14
  20.8 2.1 %collective-permute-start.5 = (bf16[32,4096]{1,0:T(8,128)(2,1)S(1)}, bf16[32,4096]{1,0:T(8,128)(2,1)S(1)}, u32[]{:S(2)}, u32[]{:S(2)}) collective-permute-start(bf16[32,4096]{1,0:T(8,128)(2,1)S(1)} %bitcast.51), channel_id=1, source_target_pairs={{0,16},{2,18},{4,20},{6,22},{8,24},{10,26},{12,28},{14,30},{16,0},... | collective-permute-start | bytes 786440 | tf_op jit(solution)/shard_map/ppermute | solution.py:14
  22.9 1.7 %collective-permute-start.8 = (bf16[32,4096]{1,0:T(8,128)(2,1)S(1)}, bf16[32,4096]{1,0:T(8,128)(2,1)S(1)}, u32[]{:S(2)}, u32[]{:S(2)}) collective-permute-start(bf16[32,4096]{1,0:T(8,128)(2,1)S(1)} %bitcast.52), channel_id=1, source_target_pairs={{0,8},{2,10},{4,12},{6,14},{8,0},{10,2},{12,4},{14,6},{16,24},{18,... | collective-permute-start | bytes 786440 | tf_op jit(solution)/shard_map/ppermute | solution.py:14
  24.6 8.4 %fusion.75 = f32[256,2048]{1,0:T(8,128)S(1)} fusion(bf16[256,4096]{1,0:T(8,128)(2,1)S(1)} %copy-done, bf16[4096,2048]{1,0:T(8,128)(2,1)} %param.7), kind=kOutput, calls=%fused_computation.150 | convolution fusion | flops 4294967296 | bytes 20971520 | tf_op jit(solution)/shard_map/dot_general | solution.py:22
  33.1 1.6 %collective-permute-start.4 = (bf16[128,2048]{1,0:T(8,128)(2,1)S(1)}, bf16[128,2048]{1,0:T(8,128)(2,1)S(1)}, u32[]{:S(2)}, u32[]{:S(2)}) collective-permute-start(bf16[128,2048]{1,0:T(8,128)(2,1)S(1)} %dynamic-slice_convert_fusion), channel_id=1, source_target_pairs={{0,1},{1,0},{2,3},{3,2},{4,5},{5,4},{6,7},{7,6},{8,9},{9,8},{10,11... | collective-permute-start | bytes 1572872 | tf_op jit(solution)/shard_map/ppermute | solution.py:18
  35.8 0.5 fusion.17
  36.5 0.6 collective-permute-start.13
  37.9 0.4 fusion.67
  38.3 1.6 %collective-permute-start.12 = (bf16[64,2048]{1,0:T(8,128)(2,1)S(1)}, bf16[64,2048]{1,0:T(8,128)(2,1)S(1)}, u32[]{:S(2)}, u32[]{:S(2)}) collective-permute-start(bf16[64,2048]{1,0:T(8,128)(2,1)S(1)} %fusion.11), channel_id=1, source_target_pairs={{0,4},{2,6},{4,0},{6,2},{8,12},{10,14},{12,8},{14,10},{16,20},{18,... | collective-permute-start | bytes 786440 | tf_op jit(solution)/shard_map/ppermute | solution.py:14
  40.6 5.9 %fusion.2 = f32[256,2048]{1,0:T(8,128)S(1)} fusion(bf16[256,2048]{1,0:T(8,128)(2,1)S(1)} %maximum_select_fusion, bf16[4096,2048]{1,0:T(8,128)(2,1)} %param.7), kind=kOutput, calls=%fused_computation.2 | convolution fusion | flops 2147483648 | bytes 11534336 | tf_op jit(solution)/shard_map/dot_general | solution.py:22
  46.5 0.5 collective-permute-done.9
  47.2 0.4 fusion.66
  47.6 0.4 fusion.8
  48.1 0.6 collective-permute-start.14
  49.3 0.5 collective-permute-done.10
  50.2 0.6 collective-permute-start.11
  51.3 1.3 %collective-permute-start.16 = (bf16[64,2048]{1,0:T(8,128)(2,1)S(1)}, bf16[64,2048]{1,0:T(8,128)(2,1)S(1)}, u32[]{:S(2)}, u32[]{:S(2)}) collective-permute-start(bf16[64,2048]{1,0:T(8,128)(2,1)S(1)} %slice.203), channel_id=1, source_target_pairs={{0,8},{2,10},{4,12},{6,14},{8,0},{10,2},{12,4},{14,6},{16,24},{18,... | collective-permute-start | bytes 786440 | tf_op jit(solution)/shard_map/ppermute | solution.py:14
  53.1 5.9 %fusion = f32[256,2048]{1,0:T(8,128)S(1)} fusion(bf16[256,2048]{1,0:T(8,128)(2,1)S(1)} %maximum_select_fusion, bf16[4096,2048]{1,0:T(8,128)(2,1)} %param.7), kind=kOutput, calls=%fused_computation | convolution fusion | flops 2147483648 | bytes 11534336 | tf_op jit(solution)/shard_map/dot_general | solution.py:22
  59.5 4.7 %collective-permute-done.11 = bf16[64,4096]{1,0:T(8,128)(2,1)S(1)} collective-permute-done((bf16[64,4096]{1,0:T(8,128)(2,1)S(1)}, bf16[64,4096]{1,0:T(8,128)(2,1)S(1)}, u32[]{:S(2)}, u32[]{:S(2)}) %collective-permute-start.11) | collective-permute-done | bytes 524320 | tf_op jit(solution)/shard_map/ppermute | solution.py:14
  64.6 0.8 convolution_select_fusion.1
  65.4 0.6 collective-permute-start.15
  66.8 1.0 %collective-permute-start.19 = (bf16[64,2048]{1,0:T(8,128)(2,1)S(1)}, bf16[64,2048]{1,0:T(8,128)(2,1)S(1)}, u32[]{:S(2)}, u32[]{:S(2)}) collective-permute-start(bf16[64,2048]{1,0:T(8,128)(2,1)S(1)} %slice.202), channel_id=1, source_target_pairs={{0,8},{2,10},{4,12},{6,14},{8,0},{10,2},{12,4},{14,6},{16,24},{18,... | collective-permute-start | bytes 786440 | tf_op jit(solution)/shard_map/ppermute | solution.py:14
  67.8 1.5 %collective-permute-done.15 = f32[32,256]{1,0:T(8,128)S(1)} collective-permute-done((f32[32,256]{1,0:T(8,128)S(1)}, f32[32,256]{1,0:T(8,128)S(1)}, u32[]{:S(2)}, u32[]{:S(2)}) %collective-permute-start.15) | collective-permute-done | bytes 32800 | tf_op jit(solution)/shard_map/ppermute | solution.py:18
  69.7 0.5 convolution_multiply_fusion.1
  70.2 0.5 convolution_multiply_fusion
  70.7 0.6 collective-permute-start.21
  72.3 1.5 %pad_maximum_fusion = bf16[256,4096]{1,0:T(8,128)(2,1)} fusion(bf16[256,2048]{1,0:T(8,128)(2,1)S(1)} %add_convert_fusion, bf16[256,2048]{1,0:T(8,128)(2,1)S(1)} %add_convert_fusion.1), kind=kLoop, calls=%fused_computation.25 | loop fusion | flops 4194304 | bytes 4194304 | tf_op jit(solution)/shard_map/concatenate | solution.py:233
  73.8 1.1 %add_convert_fusion.2 = bf16[128,2048]{1,0:T(8,128)(2,1)} fusion(bf16[128,2048]{1,0:T(8,128)(2,1)S(1)} %collective-permute-done.4, f32[256,2048]{1,0:T(8,128)S(1)} %fusion.75, s32[]{:T(128)S(6)} %select_n.160, bf16[64,1024]{1,0:T(8,128)(2,1)S(1)} %get-tuple-element.51, bf16[64,1024]{1,0:T(8,128)(2,1)S(1)} %get-tuple-element.50, pred[]{:T(512)S(6)} %eq.111, ...), kind=kOutput, calls=%fused_computation.42 | convolution fusion | flops 18743296 | bytes 2369536 | tf_op jit(solution)/shard_map/dot_general | solution.py:22
  75.4 1.2 %collective-permute-done.19 = bf16[64,2048]{1,0:T(8,128)(2,1)S(1)} collective-permute-done((bf16[64,2048]{1,0:T(8,128)(2,1)S(1)}, bf16[64,2048]{1,0:T(8,128)(2,1)S(1)}, u32[]{:S(2)}, u32[]{:S(2)}) %collective-permute-start.19) | collective-permute-done | bytes 262176 | tf_op jit(solution)/shard_map/ppermute | solution.py:14
  77.0 2.2 %collective-permute-start.20 = (bf16[32,2048]{1,0:T(8,128)(2,1)S(1)}, bf16[32,2048]{1,0:T(8,128)(2,1)S(1)}, u32[]{:S(2)}, u32[]{:S(2)}) collective-permute-start(bf16[32,2048]{1,0:T(8,128)(2,1)S(1)} %fusion.20), channel_id=1, source_target_pairs={{0,16},{2,18},{4,20},{6,22},{8,24},{10,26},{12,28},{14,30},{16,0},... | collective-permute-start | bytes 393224 | tf_op jit(solution)/shard_map/ppermute | solution.py:14
  79.6 1.3 %collective-permute-start.23 = (bf16[32,512]{1,0:T(8,128)(2,1)S(1)}, bf16[32,512]{1,0:T(8,128)(2,1)S(1)}, u32[]{:S(2)}, u32[]{:S(2)}) collective-permute-start(bf16[32,512]{1,0:T(8,128)(2,1)S(1)} %get-tuple-element.47), channel_id=1, source_target_pairs={{0,16},{2,18},{4,20},{6,22},{8,24},{10,26},{12,28},{14,30},{16,0},... | collective-permute-start | bytes 98312 | tf_op jit(solution)/shard_map/ppermute | solution.py:14
  80.8 1.3 %collective-permute-start.24 = (bf16[32,512]{1,0:T(8,128)(2,1)S(1)}, bf16[32,512]{1,0:T(8,128)(2,1)S(1)}, u32[]{:S(2)}, u32[]{:S(2)}) collective-permute-start(bf16[32,512]{1,0:T(8,128)(2,1)S(1)} %get-tuple-element.48), channel_id=1, source_target_pairs={{0,8},{2,10},{4,12},{6,14},{8,0},{10,2},{12,4},{14,6},{16,24},{18,... | collective-permute-start | bytes 98312 | tf_op jit(solution)/shard_map/ppermute | solution.py:14
  82.2 1.8 %collective-permute-start.25 = (bf16[32,512]{1,0:T(8,128)(2,1)S(1)}, bf16[32,512]{1,0:T(8,128)(2,1)S(1)}, u32[]{:S(2)}, u32[]{:S(2)}) collective-permute-start(bf16[32,512]{1,0:T(8,128)(2,1)S(1)} %get-tuple-element.49), channel_id=1, source_target_pairs={{0,24},{2,26},{4,28},{6,30},{8,16},{10,18},{12,20},{14,22},{16,8},... | collective-permute-start | bytes 98312 | tf_op jit(solution)/shard_map/ppermute | solution.py:14
  84.0 4.4 %collective-permute-done.20 = bf16[32,2048]{1,0:T(8,128)(2,1)S(1)} collective-permute-done((bf16[32,2048]{1,0:T(8,128)(2,1)S(1)}, bf16[32,2048]{1,0:T(8,128)(2,1)S(1)}, u32[]{:S(2)}, u32[]{:S(2)}) %collective-permute-start.20) | collective-permute-done | bytes 131104 | tf_op jit(solution)/shard_map/ppermute | solution.py:14
  88.5 0.8 maximum_bitcast_fusion
  89.3 0.7 fusion.36
  (87 shorter events, 10.1 us)
Async XLA Ops:
  0.6 20.1 %copy-start.3 = (bf16[1,4096,32]{1,2,0:T(8,128)(2,1)S(1)}, bf16[1,4096,32]{1,2,0:T(8,128)(2,1)}, u32[]{:S(2)}) copy-start(bf16[1,4096,32]{1,2,0:T(8,128)(2,1)} %param.8) | copy-start | bytes 786436
  0.6 24.0 %copy-start = (bf16[256,4096]{1,0:T(8,128)(2,1)S(1)}, bf16[256,4096]{1,0:T(8,128)(2,1)}, u32[]{:S(2)}) copy-start(bf16[256,4096]{1,0:T(8,128)(2,1)} %param.6) | copy-start | bytes 6291460
  0.7 8.0 %collective-permute-start.1 = (bf16[32,1024]{1,0:T(8,128)(2,1)}, bf16[32,1024]{1,0:T(8,128)(2,1)S(1)}, u32[]{:S(2)}, u32[]{:S(2)}) collective-permute-start(bf16[32,1024]{1,0:T(8,128)(2,1)} %bitcast.46), channel_id=1, source_target_pairs={{0,16},{2,18},{4,20},{6,22},{8,24},{10,26},{12,28},{14,30},{16,0},... | collective-permute-start | bytes 196616 | tf_op jit(solution)/shard_map/ppermute | solution.py:14
  4.8 6.3 %collective-permute-start = (s32[2,1]{0,1:T(1,128)}, s32[2,1]{0,1:T(1,128)S(1)}, u32[]{:S(2)}, u32[]{:S(2)}) collective-permute-start(s32[2,1]{0,1:T(1,128)} %param.10), channel_id=1, source_target_pairs={{0,4},{2,6},{4,0},{6,2},{8,12},{10,14},{12,8},{14,10},{16,20},{18,... | collective-permute-start | bytes 32 | tf_op jit(solution)/shard_map/ppermute | solution.py:14
  6.2 28.7 %collective-permute-start.7 = (bf16[128,2048]{1,0:T(8,128)(2,1)}, bf16[128,2048]{1,0:T(8,128)(2,1)S(1)}, u32[]{:S(2)}, u32[]{:S(2)}) collective-permute-start(bf16[128,2048]{1,0:T(8,128)(2,1)} %param.11), channel_id=1, source_target_pairs={{0,1},{1,0},{2,3},{3,2},{4,5},{5,4},{6,7},{7,6},{8,9},{9,8},{10,11... | collective-permute-start | bytes 1572872 | tf_op jit(solution)/shard_map/ppermute | solution.py:18
  9.5 5.0 %collective-permute-start.2 = (bf16[64,1024]{1,0:T(8,128)(2,1)S(1)}, bf16[64,1024]{1,0:T(8,128)(2,1)S(1)}, u32[]{:S(2)}, u32[]{:S(2)}) collective-permute-start(bf16[64,1024]{1,0:T(8,128)(2,1)S(1)} %pad_maximum_fusion.5), channel_id=1, source_target_pairs={{0,8},{2,10},{4,12},{6,14},{8,0},{10,2},{12,4},{14,6},{16,24},{18,... | collective-permute-start | bytes 393224 | tf_op jit(solution)/shard_map/ppermute | solution.py:14
  14.5 0.7 copy-start.5
  16.0 1.6 %collective-permute-start.3 = (bf16[128,1024]{1,0:T(8,128)(2,1)S(1)}, bf16[128,1024]{1,0:T(8,128)(2,1)S(1)}, u32[]{:S(2)}, u32[]{:S(2)}) collective-permute-start(bf16[128,1024]{1,0:T(8,128)(2,1)S(1)} %pad_maximum_fusion.4), channel_id=1, source_target_pairs={{0,2},{2,0},{4,6},{6,4},{8,10},{10,8},{12,14},{14,12},{16,18},{18,... | collective-permute-start | bytes 786440 | tf_op jit(solution)/shard_map/ppermute | solution.py:14
  19.0 16.2 %collective-permute-start.6 = (bf16[64,1024]{1,0:T(8,128)(2,1)S(1)}, bf16[64,1024]{1,0:T(8,128)(2,1)S(1)}, u32[]{:S(2)}, u32[]{:S(2)}) collective-permute-start(bf16[64,1024]{1,0:T(8,128)(2,1)S(1)} %fusion.14), channel_id=1, source_target_pairs={{0,4},{2,6},{4,0},{6,2},{8,12},{10,14},{12,8},{14,10},{16,20},{18,... | collective-permute-start | bytes 393224 | tf_op jit(solution)/shard_map/ppermute | solution.py:14
  20.8 14.2 %copy-start.1 = (bf16[128,2048]{1,0:T(8,128)(2,1)S(1)}, bf16[128,2048]{1,0:T(8,128)(2,1)}, u32[]{:S(2)}) copy-start(bf16[128,2048]{1,0:T(8,128)(2,1)} %param.11) | copy-start | bytes 1572868
  20.8 19.5 %collective-permute-start.5 = (bf16[32,4096]{1,0:T(8,128)(2,1)S(1)}, bf16[32,4096]{1,0:T(8,128)(2,1)S(1)}, u32[]{:S(2)}, u32[]{:S(2)}) collective-permute-start(bf16[32,4096]{1,0:T(8,128)(2,1)S(1)} %bitcast.51), channel_id=1, source_target_pairs={{0,16},{2,18},{4,20},{6,22},{8,24},{10,26},{12,28},{14,30},{16,0},... | collective-permute-start | bytes 786440 | tf_op jit(solution)/shard_map/ppermute | solution.py:14
  22.9 23.6 %collective-permute-start.8 = (bf16[32,4096]{1,0:T(8,128)(2,1)S(1)}, bf16[32,4096]{1,0:T(8,128)(2,1)S(1)}, u32[]{:S(2)}, u32[]{:S(2)}) collective-permute-start(bf16[32,4096]{1,0:T(8,128)(2,1)S(1)} %bitcast.52), channel_id=1, source_target_pairs={{0,8},{2,10},{4,12},{6,14},{8,0},{10,2},{12,4},{14,6},{16,24},{18,... | collective-permute-start | bytes 786440 | tf_op jit(solution)/shard_map/ppermute | solution.py:14
  33.0 2.5 %copy-start.2 = (bf16[1,32,1024]{2,1,0:T(8,128)(2,1)S(1)}, bf16[1,32,1024]{2,1,0:T(8,128)(2,1)}, u32[]{:S(2)}) copy-start(bf16[1,32,1024]{2,1,0:T(8,128)(2,1)} %param.9) | copy-start | bytes 196612
  33.0 2.4 %copy-start.6 = (bf16[64,1024]{1,0:T(8,128)(2,1)S(1)}, bf16[64,1024]{1,0:T(8,128)(2,1)}, u32[]{:S(2)}) copy-start(bf16[64,1024]{1,0:T(8,128)(2,1)} %copy-done.5) | copy-start | bytes 393220
  33.1 40.7 %collective-permute-start.4 = (bf16[128,2048]{1,0:T(8,128)(2,1)S(1)}, bf16[128,2048]{1,0:T(8,128)(2,1)S(1)}, u32[]{:S(2)}, u32[]{:S(2)}) collective-permute-start(bf16[128,2048]{1,0:T(8,128)(2,1)S(1)} %dynamic-slice_convert_fusion), channel_id=1, source_target_pairs={{0,1},{1,0},{2,3},{3,2},{4,5},{5,4},{6,7},{7,6},{8,9},{9,8},{10,11... | collective-permute-start | bytes 1572872 | tf_op jit(solution)/shard_map/ppermute | solution.py:18
  36.5 11.1 %collective-permute-start.13 = (bf16[64,2048]{1,0:T(8,128)(2,1)S(1)}, bf16[64,2048]{1,0:T(8,128)(2,1)S(1)}, u32[]{:S(2)}, u32[]{:S(2)}) collective-permute-start(bf16[64,2048]{1,0:T(8,128)(2,1)S(1)} %fusion.10), channel_id=1, source_target_pairs={{0,4},{2,6},{4,0},{6,2},{8,12},{10,14},{12,8},{14,10},{16,20},{18,... | collective-permute-start | bytes 786440 | tf_op jit(solution)/shard_map/ppermute | solution.py:14
  38.3 14.3 %collective-permute-start.12 = (bf16[64,2048]{1,0:T(8,128)(2,1)S(1)}, bf16[64,2048]{1,0:T(8,128)(2,1)S(1)}, u32[]{:S(2)}, u32[]{:S(2)}) collective-permute-start(bf16[64,2048]{1,0:T(8,128)(2,1)S(1)} %fusion.11), channel_id=1, source_target_pairs={{0,4},{2,6},{4,0},{6,2},{8,12},{10,14},{12,8},{14,10},{16,20},{18,... | collective-permute-start | bytes 786440 | tf_op jit(solution)/shard_map/ppermute | solution.py:14
  40.3 6.7 %collective-permute-start.9 = (bf16[32,4096]{1,0:T(8,128)(2,1)S(1)}, bf16[32,4096]{1,0:T(8,128)(2,1)S(1)}, u32[]{:S(2)}, u32[]{:S(2)}) collective-permute-start(bf16[32,4096]{1,0:T(8,128)(2,1)S(1)} %collective-permute-done.5), channel_id=1, source_target_pairs={{0,8},{2,10},{4,12},{6,14},{8,0},{10,2},{12,4},{14,6},{16,24},{18,... | collective-permute-start | bytes 786440 | tf_op jit(solution)/shard_map/ppermute | solution.py:14
  47.1 2.7 %collective-permute-start.10 = (bf16[128,4096]{1,0:T(8,128)(2,1)S(1)}, bf16[128,4096]{1,0:T(8,128)(2,1)S(1)}, u32[]{:S(2)}, u32[]{:S(2)}) collective-permute-start(bf16[128,4096]{1,0:T(8,128)(2,1)S(1)} %pad_maximum_fusion.1), channel_id=1, source_target_pairs={{0,2},{2,0},{4,6},{6,4},{8,10},{10,8},{12,14},{14,12},{16,18},{18,... | collective-permute-start | bytes 3145736 | tf_op jit(solution)/shard_map/ppermute | solution.py:14
  48.1 2.7 %collective-permute-start.14 = (bf16[128,2048]{1,0:T(8,128)(2,1)S(1)}, bf16[128,2048]{1,0:T(8,128)(2,1)S(1)}, u32[]{:S(2)}, u32[]{:S(2)}) collective-permute-start(bf16[128,2048]{1,0:T(8,128)(2,1)S(1)} %fusion.8), channel_id=1, source_target_pairs={{0,2},{2,0},{4,6},{6,4},{8,10},{10,8},{12,14},{14,12},{16,18},{18,... | collective-permute-start | bytes 1572872 | tf_op jit(solution)/shard_map/ppermute | solution.py:14
  50.2 14.0 %collective-permute-start.11 = (bf16[64,4096]{1,0:T(8,128)(2,1)S(1)}, bf16[64,4096]{1,0:T(8,128)(2,1)S(1)}, u32[]{:S(2)}, u32[]{:S(2)}) collective-permute-start(bf16[64,4096]{1,0:T(8,128)(2,1)S(1)} %fusion.5), channel_id=1, source_target_pairs={{0,4},{2,6},{4,0},{6,2},{8,12},{10,14},{12,8},{14,10},{16,20},{18,... | collective-permute-start | bytes 1572872 | tf_op jit(solution)/shard_map/ppermute | solution.py:14
  51.3 8.2 %collective-permute-start.16 = (bf16[64,2048]{1,0:T(8,128)(2,1)S(1)}, bf16[64,2048]{1,0:T(8,128)(2,1)S(1)}, u32[]{:S(2)}, u32[]{:S(2)}) collective-permute-start(bf16[64,2048]{1,0:T(8,128)(2,1)S(1)} %slice.203), channel_id=1, source_target_pairs={{0,8},{2,10},{4,12},{6,14},{8,0},{10,2},{12,4},{14,6},{16,24},{18,... | collective-permute-start | bytes 786440 | tf_op jit(solution)/shard_map/ppermute | solution.py:14
  53.0 12.9 %collective-permute-start.18 = (bf16[128,2048]{1,0:T(8,128)(2,1)S(1)}, bf16[128,2048]{1,0:T(8,128)(2,1)S(1)}, u32[]{:S(2)}, u32[]{:S(2)}) collective-permute-start(bf16[128,2048]{1,0:T(8,128)(2,1)S(1)} %fusion.9), channel_id=1, source_target_pairs={{0,2},{2,0},{4,6},{6,4},{8,10},{10,8},{12,14},{14,12},{16,18},{18,... | collective-permute-start | bytes 1572872 | tf_op jit(solution)/shard_map/ppermute | solution.py:14
  65.4 4.0 %collective-permute-start.15 = (f32[32,256]{1,0:T(8,128)S(1)}, f32[32,256]{1,0:T(8,128)S(1)}, u32[]{:S(2)}, u32[]{:S(2)}) collective-permute-start(f32[32,256]{1,0:T(8,128)S(1)} %slice_add_fusion.5), channel_id=1, source_target_pairs={{0,1},{1,0},{2,3},{3,2},{4,5},{5,4},{6,7},{7,6},{8,9},{9,8},{10,11... | collective-permute-start | bytes 98312 | tf_op jit(solution)/shard_map/ppermute | solution.py:18
  66.4 8.9 %collective-permute-start.17 = (bf16[32,2048]{1,0:T(8,128)(2,1)S(1)}, bf16[32,2048]{1,0:T(8,128)(2,1)S(1)}, u32[]{:S(2)}, u32[]{:S(2)}) collective-permute-start(bf16[32,2048]{1,0:T(8,128)(2,1)S(1)} %fusion.22), channel_id=1, source_target_pairs={{0,16},{2,18},{4,20},{6,22},{8,24},{10,26},{12,28},{14,30},{16,0},... | collective-permute-start | bytes 393224 | tf_op jit(solution)/shard_map/ppermute | solution.py:14
  66.8 9.8 %collective-permute-start.19 = (bf16[64,2048]{1,0:T(8,128)(2,1)S(1)}, bf16[64,2048]{1,0:T(8,128)(2,1)S(1)}, u32[]{:S(2)}, u32[]{:S(2)}) collective-permute-start(bf16[64,2048]{1,0:T(8,128)(2,1)S(1)} %slice.202), channel_id=1, source_target_pairs={{0,8},{2,10},{4,12},{6,14},{8,0},{10,2},{12,4},{14,6},{16,24},{18,... | collective-permute-start | bytes 786440 | tf_op jit(solution)/shard_map/ppermute | solution.py:14
  69.7 0.9 %copy-start.4 = (pred[64,1024]{1,0:T(8,128)(4,1)S(1)}, pred[64,1024]{1,0:T(8,128)(4,1)}, u32[]{:S(2)}) copy-start(pred[64,1024]{1,0:T(8,128)(4,1)} %select_compare_fusion) | copy-start | bytes 196612
  70.7 4.7 %collective-permute-start.21 = (bf16[64,512]{1,0:T(8,128)(2,1)S(1)}, bf16[64,512]{1,0:T(8,128)(2,1)S(1)}, u32[]{:S(2)}, u32[]{:S(2)}) collective-permute-start(bf16[64,512]{1,0:T(8,128)(2,1)S(1)} %select_convert_fusion), channel_id=1, source_target_pairs={{0,4},{2,6},{4,0},{6,2},{8,12},{10,14},{12,8},{14,10},{16,20},{18,... | collective-permute-start | bytes 196616 | tf_op jit(solution)/shard_map/ppermute | solution.py:14
  76.9 2.3 %collective-permute-start.22 = (bf16[128,512]{1,0:T(8,128)(2,1)S(1)}, bf16[128,512]{1,0:T(8,128)(2,1)S(1)}, u32[]{:S(2)}, u32[]{:S(2)}) collective-permute-start(bf16[128,512]{1,0:T(8,128)(2,1)S(1)} %fusion.16), channel_id=1, source_target_pairs={{0,2},{2,0},{4,6},{6,4},{8,10},{10,8},{12,14},{14,12},{16,18},{18,... | collective-permute-start | bytes 393224 | tf_op jit(solution)/shard_map/ppermute | solution.py:14
  77.0 11.4 %collective-permute-start.20 = (bf16[32,2048]{1,0:T(8,128)(2,1)S(1)}, bf16[32,2048]{1,0:T(8,128)(2,1)S(1)}, u32[]{:S(2)}, u32[]{:S(2)}) collective-permute-start(bf16[32,2048]{1,0:T(8,128)(2,1)S(1)} %fusion.20), channel_id=1, source_target_pairs={{0,16},{2,18},{4,20},{6,22},{8,24},{10,26},{12,28},{14,30},{16,0},... | collective-permute-start | bytes 393224 | tf_op jit(solution)/shard_map/ppermute | solution.py:14
  79.6 9.8 %collective-permute-start.23 = (bf16[32,512]{1,0:T(8,128)(2,1)S(1)}, bf16[32,512]{1,0:T(8,128)(2,1)S(1)}, u32[]{:S(2)}, u32[]{:S(2)}) collective-permute-start(bf16[32,512]{1,0:T(8,128)(2,1)S(1)} %get-tuple-element.47), channel_id=1, source_target_pairs={{0,16},{2,18},{4,20},{6,22},{8,24},{10,26},{12,28},{14,30},{16,0},... | collective-permute-start | bytes 98312 | tf_op jit(solution)/shard_map/ppermute | solution.py:14
  80.8 8.5 %collective-permute-start.24 = (bf16[32,512]{1,0:T(8,128)(2,1)S(1)}, bf16[32,512]{1,0:T(8,128)(2,1)S(1)}, u32[]{:S(2)}, u32[]{:S(2)}) collective-permute-start(bf16[32,512]{1,0:T(8,128)(2,1)S(1)} %get-tuple-element.48), channel_id=1, source_target_pairs={{0,8},{2,10},{4,12},{6,14},{8,0},{10,2},{12,4},{14,6},{16,24},{18,... | collective-permute-start | bytes 98312 | tf_op jit(solution)/shard_map/ppermute | solution.py:14
  82.2 7.1 %collective-permute-start.25 = (bf16[32,512]{1,0:T(8,128)(2,1)S(1)}, bf16[32,512]{1,0:T(8,128)(2,1)S(1)}, u32[]{:S(2)}, u32[]{:S(2)}) collective-permute-start(bf16[32,512]{1,0:T(8,128)(2,1)S(1)} %get-tuple-element.49), channel_id=1, source_target_pairs={{0,24},{2,26},{4,28},{6,30},{8,16},{10,18},{12,20},{14,22},{16,8},... | collective-permute-start | bytes 98312 | tf_op jit(solution)/shard_map/ppermute | solution.py:14

commit v5 on v4

--- a/solution.py
+++ b/solution.py
@@ -164,7 +164,7 @@
         blocks_a = blocks_a + [swap(block, 1 << bit) for block in blocks_a]
     here_a = jnp.concatenate(blocks_a, axis=0)
     if tp_count == 2:
-        base = dot(after(tokens, sent_b), weight, (1, 0))
+        base = dot(after(tokens, down[-1]), weight, (1, 0))
         near_base = lax.dynamic_slice_in_dim(base, col * local_rows, local_rows, 0)
         far_base = lax.dynamic_slice_in_dim(base, (1 - col) * local_rows, local_rows, 0).astype(bf16)
         base_rows = near_base + cross(far_base).astype(f32)
@@ -177,34 +177,31 @@
     there_a = swap(here_a, core)
     sent_a = give_away(here_a, there_a)
 
-    got_c = [swap(d, far) for d in down]
-    got_c[0] = after(got_c[0], here_a)
-    back = after(swap(core_part(down[0], got_c[0]), core), sent_a)
-    total = sums(down[0], got_c[0], back)
-    first_gone = after(leaving(total, bits[0]), sent_a)
-    total = add_hop(total, swap(first_gone, 1 << bits[0]), bits[0])
-
-    got_c[1] = after(got_c[1], first_gone)
-    away = core_part(down[1], got_c[1])
-    base_high = dot(after(grad_rows, sent_a, away), weight[half:], (1, 1))
+    got_c = [after(swap(d, far), far_base) for d in down]
+    back_c = [swap(core_part(d, g), core) for d, g in zip(down, got_c)]
+    mark = sent_a
+    total_c, came_c = [], []
+    for sent, got, back in zip(down, got_c, back_c):
+        total = sums(sent, got, after(back, sent_a))
+        mark = after(leaving(total, bits[0]), mark)
+        came_c.append(swap(mark, 1 << bits[0]))
+        total_c.append(total)
+    base_high = dot(after(grad_rows, mark), weight[half:], (1, 1))
 
     factor_a = take_in(here_a, there_a, after(swap(sent_a, far), base_high))
     rank_part = jnp.where(keep, dot(factor_a, tokens, (1, 1)), 0.0)
     rank_part = sum(split(rank_part))
 
-    total_c = []
-    first_came = None
     mark = rank_part
-    for i in range(c_parts):
-        if i:
-            total = sums(down[i], got_c[i], swap(away, core))
-            first_came = swap(after(leaving(total, bits[0]), mark), 1 << bits[0])
-            total = add_hop(total, first_came, bits[0])
+    ends = []
+    for i, came in enumerate(came_c):
+        total = add_hop(total_c[i], came, bits[0])
         for bit in bits[1:]:
             mark = after(leaving(total, bit), mark)
-            total = add_hop(total, swap(mark, 1 << bit), bit)
-        total_c.append(total)
-    grad_a = jnp.concatenate([total[0] for total in total_c], axis=1)
+            came = swap(mark, 1 << bit)
+            if bit == bits[-1]:
+                ends.append((total, came))
+            total = add_hop(total, came, bit)
 
     if tp_count == 2:
         rank_sum = rank_part + cross(rank_part)
@@ -222,12 +219,15 @@
     key_part = lax.dynamic_slice(whole, (0, col * kv_dev), (stacked, kv_dev))
     value_part = lax.dynamic_slice(whole, (0, kv_width + col * kv_dev), (stacked, kv_dev))
     up = jnp.where(key_row[:, :kv_dev], key_part, value_part).astype(bf16)
-    got_up = after(swap(up, far), first_came)
+    got_up = after(swap(up, far), mark)
     back_up = swap(core_part(up, got_up), core)
     total_up = sums(up, got_up, back_up)
-    leave = [after(total_up[o].astype(bf16), mark) for o in places[1:]]
+    leave = [total_up[o].astype(bf16) for o in places[1:]]
     came_up = [swap(t, o) for o, t in zip(places[1:], leave)]
     grad_b = sum([c.astype(f32) for c in came_up], total_up[0])
+    grad_a = jnp.concatenate(
+        [add_hop(total, after(came, came_up[0]), bits[-1])[0] for total, came in ends], axis=1
+    )
 
     late_grad = after(rank_grad, rank_act)
     token_gradient = jnp.concatenate(

time: 90.3 us -> 88.3 us (0.978)
    ppermute x23, starting transfers between devices: 26.6 us -> 24.7 us  [swap(): return lax.ppermute(value, 'blk', [(i, i ^ offset) for i in range(count)])]
    ppermute x3, waiting for transfers between devices: 1.55 us -> 0.01 us  [cross(): return lax.ppermute(value, 'tp', [(0, 1), (1, 0)])]
    ppermute x3, starting transfers between devices: 3.68 us -> 5.19 us  [cross(): return lax.ppermute(value, 'tp', [(0, 1), (1, 0)])]
  transfers between devices with their start and end apart: 26 -> 26, of which waited for: 10 -> 12; matrix products, arithmetic and copies ran while one was open for 44% -> 45% of each run, Pallas kernels for 0% -> 0%
where the time goes in v5:
time: 88.3 us; the launch traced here: 88 us
  matrix products  32.8 us (37%)
  starting transfers between devices  29.9 us (34%)
  waiting for transfers between devices  16.4 us (19%)
  other arithmetic  6.74 us (8%)
  between operations  1.12 us (1%)
  local copies, waits for them, and re-layouts  1.08 us (1%)
    dot_general x33, matrix products, dot(): lax.dot_general(a, b, ((contract[:1], contract[1:]), ((), ())), preferred...  32.8 us
    ppermute x23, starting transfers between devices, swap(): return lax.ppermute(value, 'blk', [(i, i ^ offset) for i in range(count)])  24.7 us
    ppermute x23, waiting for transfers between devices, swap(): return lax.ppermute(value, 'blk', [(i, i ^ offset) for i in range(count)])  16.4 us
    ppermute x3, starting transfers between devices, cross(): return lax.ppermute(value, 'tp', [(0, 1), (1, 0)])  5.19 us
  transfers between devices with their start and end apart: 26, of which 12 were waited for; matrix products, arithmetic and copies ran while one was open for 45% of the time, Pallas kernels for 0%

profile of v5, /device:TPU:0, one launch (start us, length us, event | category | flops | bytes accessed | tf_op | source)
XLA Modules:
  0.0 88.0 jit_solution(6709276208547106105)
XLA Ops:
  0.7 3.0 %collective-permute-start.5 = (bf16[128,2048]{1,0:T(8,128)(2,1)}, bf16[128,2048]{1,0:T(8,128)(2,1)S(1)}, u32[]{:S(2)}, u32[]{:S(2)}) collective-permute-start(bf16[128,2048]{1,0:T(8,128)(2,1)} %param.11), channel_id=1, source_target_pairs={{0,1},{1,0},{2,3},{3,2},{4,5},{5,4},{6,7},{7,6},{8,9},{9,8},{10,11... | collective-permute-start | bytes 1572872 | tf_op jit(solution)/shard_map/ppermute | solution.py:18
  3.7 2.6 %collective-permute-start = (bf16[32,1024]{1,0:T(8,128)(2,1)}, bf16[32,1024]{1,0:T(8,128)(2,1)S(1)}, u32[]{:S(2)}, u32[]{:S(2)}) collective-permute-start(bf16[32,1024]{1,0:T(8,128)(2,1)} %bitcast.46), channel_id=1, source_target_pairs={{0,16},{2,18},{4,20},{6,22},{8,24},{10,26},{12,28},{14,30},{16,0},... | collective-permute-start | bytes 196616 | tf_op jit(solution)/shard_map/ppermute | solution.py:14
  6.3 1.5 %collective-permute-start.3 = (s32[2,1]{0,1:T(1,128)}, s32[2,1]{0,1:T(1,128)S(1)}, u32[]{:S(2)}, u32[]{:S(2)}) collective-permute-start(s32[2,1]{0,1:T(1,128)} %param.10), channel_id=1, source_target_pairs={{0,4},{2,6},{4,0},{6,2},{8,12},{10,14},{12,8},{14,10},{16,20},{18,... | collective-permute-start | bytes 32 | tf_op jit(solution)/shard_map/ppermute | solution.py:14
  7.9 1.4 %collective-permute-done = bf16[32,1024]{1,0:T(8,128)(2,1)S(1)} collective-permute-done((bf16[32,1024]{1,0:T(8,128)(2,1)}, bf16[32,1024]{1,0:T(8,128)(2,1)S(1)}, u32[]{:S(2)}, u32[]{:S(2)}) %collective-permute-start) | collective-permute-done | bytes 65568 | tf_op jit(solution)/shard_map/ppermute | solution.py:14
  9.4 0.9 pad_maximum_fusion.5
  10.2 1.3 %collective-permute-start.1 = (bf16[64,1024]{1,0:T(8,128)(2,1)S(1)}, bf16[64,1024]{1,0:T(8,128)(2,1)S(1)}, u32[]{:S(2)}, u32[]{:S(2)}) collective-permute-start(bf16[64,1024]{1,0:T(8,128)(2,1)S(1)} %pad_maximum_fusion.5), channel_id=1, source_target_pairs={{0,8},{2,10},{4,12},{6,14},{8,0},{10,2},{12,4},{14,6},{16,24},{18,... | collective-permute-start | bytes 393224 | tf_op jit(solution)/shard_map/ppermute | solution.py:14
  11.6 3.7 %collective-permute-done.1 = bf16[64,1024]{1,0:T(8,128)(2,1)S(1)} collective-permute-done((bf16[64,1024]{1,0:T(8,128)(2,1)S(1)}, bf16[64,1024]{1,0:T(8,128)(2,1)S(1)}, u32[]{:S(2)}, u32[]{:S(2)}) %collective-permute-start.1) | collective-permute-done | bytes 131104 | tf_op jit(solution)/shard_map/ppermute | solution.py:14
  15.2 0.9 pad_maximum_fusion.4
  16.2 0.7 xor_bitcast_fusion
  17.2 0.5 collective-permute-done.2
  18.0 1.1 %fusion.15 = bf16[64,1024]{1,0:T(8,128)(2,1)S(1)} fusion(f32[64,1024]{1,0:T(8,128)S(1)} %fusion.72, s32[64]{0:T(128)S(1)} %broadcast_in_dim.60, s32[128]{0:T(128)S(1)} %get-tuple-element.63, s32[128]{0:T(128)S(1)} %get-tuple-element.65, pred[128]{0:T(512)(128)(4,1)S(1)} %get-tuple-element.57, s32[128]{0:T(128)S(1)} %get-tuple-element.64, ...), kind=kOutput, calls=%fused_computation.35 | convolution fusion | flops 17793024 | bytes 658496 | tf_op jit(solution)/shard_map/dot_general | solution.py:22
  19.1 1.6 %collective-permute-start.4 = (bf16[64,1024]{1,0:T(8,128)(2,1)S(1)}, bf16[64,1024]{1,0:T(8,128)(2,1)S(1)}, u32[]{:S(2)}, u32[]{:S(2)}) collective-permute-start(bf16[64,1024]{1,0:T(8,128)(2,1)S(1)} %fusion.15), channel_id=1, source_target_pairs={{0,4},{2,6},{4,0},{6,2},{8,12},{10,14},{12,8},{14,10},{16,20},{18,... | collective-permute-start | bytes 393224 | tf_op jit(solution)/shard_map/ppermute | solution.py:14
  20.7 2.4 %collective-permute-start.7 = (bf16[32,4096]{1,0:T(8,128)(2,1)S(1)}, bf16[32,4096]{1,0:T(8,128)(2,1)S(1)}, u32[]{:S(2)}, u32[]{:S(2)}) collective-permute-start(bf16[32,4096]{1,0:T(8,128)(2,1)S(1)} %bitcast.51), channel_id=1, source_target_pairs={{0,16},{2,18},{4,20},{6,22},{8,24},{10,26},{12,28},{14,30},{16,0},... | collective-permute-start | bytes 786440 | tf_op jit(solution)/shard_map/ppermute | solution.py:14
  23.1 2.0 %collective-permute-start.8 = (bf16[32,4096]{1,0:T(8,128)(2,1)S(1)}, bf16[32,4096]{1,0:T(8,128)(2,1)S(1)}, u32[]{:S(2)}, u32[]{:S(2)}) collective-permute-start(bf16[32,4096]{1,0:T(8,128)(2,1)S(1)} %bitcast.52), channel_id=1, source_target_pairs={{0,8},{2,10},{4,12},{6,14},{8,0},{10,2},{12,4},{14,6},{16,24},{18,... | collective-permute-start | bytes 786440 | tf_op jit(solution)/shard_map/ppermute | solution.py:14
  26.2 0.4 fusion.17
  26.7 0.6 copy-done
  28.3 0.6 collective-permute-start.12
  29.4 0.4 fusion.64
  29.8 1.6 %collective-permute-start.14 = (bf16[64,2048]{1,0:T(8,128)(2,1)S(1)}, bf16[64,2048]{1,0:T(8,128)(2,1)S(1)}, u32[]{:S(2)}, u32[]{:S(2)}) collective-permute-start(bf16[64,2048]{1,0:T(8,128)(2,1)S(1)} %fusion.11), channel_id=1, source_target_pairs={{0,4},{2,6},{4,0},{6,2},{8,12},{10,14},{12,8},{14,10},{16,20},{18,... | collective-permute-start | bytes 786440 | tf_op jit(solution)/shard_map/ppermute | solution.py:14
  31.4 8.3 %fusion.75 = f32[256,2048]{1,0:T(8,128)S(1)} fusion(bf16[256,4096]{1,0:T(8,128)(2,1)S(1)} %copy-done, bf16[4096,2048]{1,0:T(8,128)(2,1)} %param.7), kind=kOutput, calls=%fused_computation.150 | convolution fusion | flops 4294967296 | bytes 20971520 | tf_op jit(solution)/shard_map/dot_general | solution.py:22
  39.8 0.6 collective-permute-start.6
  40.9 5.9 %fusion.2 = f32[256,2048]{1,0:T(8,128)S(1)} fusion(bf16[256,2048]{1,0:T(8,128)(2,1)S(1)} %maximum_select_fusion, bf16[4096,2048]{1,0:T(8,128)(2,1)} %param.7), kind=kOutput, calls=%fused_computation.2 | convolution fusion | flops 2147483648 | bytes 11534336 | tf_op jit(solution)/shard_map/dot_general | solution.py:22
  46.8 0.8 collective-permute-done.9
  47.7 0.4 fusion.8
  48.1 0.6 collective-permute-start.13
  50.7 0.6 collective-permute-start.11
  51.9 0.4 fusion.6
  52.3 1.3 %collective-permute-start.20 = (bf16[64,2048]{1,0:T(8,128)(2,1)S(1)}, bf16[64,2048]{1,0:T(8,128)(2,1)S(1)}, u32[]{:S(2)}, u32[]{:S(2)}) collective-permute-start(bf16[64,2048]{1,0:T(8,128)(2,1)S(1)} %slice.203), channel_id=1, source_target_pairs={{0,8},{2,10},{4,12},{6,14},{8,0},{10,2},{12,4},{14,6},{16,24},{18,... | collective-permute-start | bytes 786440 | tf_op jit(solution)/shard_map/ppermute | solution.py:14
  53.7 0.8 collective-permute-start.17
  54.4 5.9 %fusion = f32[256,2048]{1,0:T(8,128)S(1)} fusion(bf16[256,2048]{1,0:T(8,128)(2,1)S(1)} %maximum_select_fusion, bf16[4096,2048]{1,0:T(8,128)(2,1)} %param.7), kind=kOutput, calls=%fused_computation | convolution fusion | flops 2147483648 | bytes 11534336 | tf_op jit(solution)/shard_map/dot_general | solution.py:22
  60.7 0.9 %collective-permute-done.20 = bf16[64,2048]{1,0:T(8,128)(2,1)S(1)} collective-permute-done((bf16[64,2048]{1,0:T(8,128)(2,1)S(1)}, bf16[64,2048]{1,0:T(8,128)(2,1)S(1)}, u32[]{:S(2)}, u32[]{:S(2)}) %collective-permute-start.20) | collective-permute-done | bytes 262176 | tf_op jit(solution)/shard_map/ppermute | solution.py:14
  61.6 3.2 %collective-permute-done.11 = bf16[64,4096]{1,0:T(8,128)(2,1)S(1)} collective-permute-done((bf16[64,4096]{1,0:T(8,128)(2,1)S(1)}, bf16[64,4096]{1,0:T(8,128)(2,1)S(1)}, u32[]{:S(2)}, u32[]{:S(2)}) %collective-permute-start.11) | collective-permute-done | bytes 524320 | tf_op jit(solution)/shard_map/ppermute | solution.py:14
  65.1 0.8 convolution_select_fusion.1
  65.9 1.6 %collective-permute-start.16 = (f32[32,256]{1,0:T(8,128)S(1)}, f32[32,256]{1,0:T(8,128)S(1)}, u32[]{:S(2)}, u32[]{:S(2)}) collective-permute-start(f32[32,256]{1,0:T(8,128)S(1)} %slice_add_fusion.5), channel_id=1, source_target_pairs={{0,1},{1,0},{2,3},{3,2},{4,5},{5,4},{6,7},{7,6},{8,9},{9,8},{10,11... | collective-permute-start | bytes 98312 | tf_op jit(solution)/shard_map/ppermute | solution.py:18
  67.5 2.1 %collective-permute-start.18 = (bf16[32,2048]{1,0:T(8,128)(2,1)S(1)}, bf16[32,2048]{1,0:T(8,128)(2,1)S(1)}, u32[]{:S(2)}, u32[]{:S(2)}) collective-permute-start(bf16[32,2048]{1,0:T(8,128)(2,1)S(1)} %fusion.22), channel_id=1, source_target_pairs={{0,16},{2,18},{4,20},{6,22},{8,24},{10,26},{12,28},{14,30},{16,0},... | collective-permute-start | bytes 393224 | tf_op jit(solution)/shard_map/ppermute | solution.py:14
  69.6 0.8 collective-permute-start.23
  70.5 0.5 convolution_multiply_fusion
  71.0 0.5 convolution_multiply_fusion.1
  71.8 0.8 collective-permute-start.19
  73.2 1.5 %pad_maximum_fusion = bf16[256,4096]{1,0:T(8,128)(2,1)} fusion(bf16[256,2048]{1,0:T(8,128)(2,1)S(1)} %add_convert_fusion, bf16[256,2048]{1,0:T(8,128)(2,1)S(1)} %add_convert_fusion.1), kind=kLoop, calls=%fused_computation.25 | loop fusion | flops 4194304 | bytes 4194304 | tf_op jit(solution)/shard_map/concatenate | solution.py:233
  75.1 1.1 %collective-permute-done.19 = bf16[64,512]{1,0:T(8,128)(2,1)S(1)} collective-permute-done((bf16[64,512]{1,0:T(8,128)(2,1)S(1)}, bf16[64,512]{1,0:T(8,128)(2,1)S(1)}, u32[]{:S(2)}, u32[]{:S(2)}) %collective-permute-start.19) | collective-permute-done | bytes 65568 | tf_op jit(solution)/shard_map/ppermute | solution.py:14
  76.8 1.0 %collective-permute-done.21 = bf16[128,512]{1,0:T(8,128)(2,1)S(1)} collective-permute-done((bf16[128,512]{1,0:T(8,128)(2,1)S(1)}, bf16[128,512]{1,0:T(8,128)(2,1)S(1)}, u32[]{:S(2)}, u32[]{:S(2)}) %collective-permute-start.21) | collective-permute-done | bytes 131104 | tf_op jit(solution)/shard_map/ppermute | solution.py:14
  78.2 2.1 %collective-permute-start.22 = (bf16[32,512]{1,0:T(8,128)(2,1)S(1)}, bf16[32,512]{1,0:T(8,128)(2,1)S(1)}, u32[]{:S(2)}, u32[]{:S(2)}) collective-permute-start(bf16[32,512]{1,0:T(8,128)(2,1)S(1)} %get-tuple-element.54), channel_id=1, source_target_pairs={{0,16},{2,18},{4,20},{6,22},{8,24},{10,26},{12,28},{14,30},{16,0},... | collective-permute-start | bytes 98312 | tf_op jit(solution)/shard_map/ppermute | solution.py:14
  80.3 1.1 %add_convert_fusion.2 = bf16[128,2048]{1,0:T(8,128)(2,1)} fusion(bf16[128,2048]{1,0:T(8,128)(2,1)S(1)} %collective-permute-done.6, f32[256,2048]{1,0:T(8,128)S(1)} %fusion.75, s32[]{:T(128)S(6)} %select_n.168, bf16[64,1024]{1,0:T(8,128)(2,1)S(1)} %get-tuple-element.50, bf16[64,1024]{1,0:T(8,128)(2,1)S(1)} %get-tuple-element.51, pred[]{:T(512)S(6)} %eq.111, ...), kind=kOutput, calls=%fused_computation.42 | convolution fusion | flops 18743296 | bytes 2369536 | tf_op jit(solution)/shard_map/dot_general | solution.py:22
  81.5 1.6 %collective-permute-start.25 = (bf16[32,512]{1,0:T(8,128)(2,1)S(1)}, bf16[32,512]{1,0:T(8,128)(2,1)S(1)}, u32[]{:S(2)}, u32[]{:S(2)}) collective-permute-start(bf16[32,512]{1,0:T(8,128)(2,1)S(1)} %get-tuple-element.53), channel_id=1, source_target_pairs={{0,24},{2,26},{4,28},{6,30},{8,16},{10,18},{12,20},{14,22},{16,8},... | collective-permute-start | bytes 98312 | tf_op jit(solution)/shard_map/ppermute | solution.py:14
  83.4 0.8 maximum_bitcast_fusion
  84.2 3.1 %collective-permute-done.25 = bf16[32,512]{1,0:T(8,128)(2,1)S(1)} collective-permute-done((bf16[32,512]{1,0:T(8,128)(2,1)S(1)}, bf16[32,512]{1,0:T(8,128)(2,1)S(1)}, u32[]{:S(2)}, u32[]{:S(2)}) %collective-permute-start.25) | collective-permute-done | bytes 32800 | tf_op jit(solution)/shard_map/ppermute | solution.py:14
  87.3 0.7 fusion.36
  (81 shorter events, 10.0 us)
Async XLA Ops:
  0.6 24.7 %copy-start.1 = (bf16[128,2048]{1,0:T(8,128)(2,1)S(1)}, bf16[128,2048]{1,0:T(8,128)(2,1)}, u32[]{:S(2)}) copy-start(bf16[128,2048]{1,0:T(8,128)(2,1)} %param.11) | copy-start | bytes 1572868
  0.6 20.0 %copy-start.3 = (bf16[1,4096,32]{1,2,0:T(8,128)(2,1)S(1)}, bf16[1,4096,32]{1,2,0:T(8,128)(2,1)}, u32[]{:S(2)}) copy-start(bf16[1,4096,32]{1,2,0:T(8,128)(2,1)} %param.8) | copy-start | bytes 786436
  0.7 24.7 %collective-permute-start.5 = (bf16[128,2048]{1,0:T(8,128)(2,1)}, bf16[128,2048]{1,0:T(8,128)(2,1)S(1)}, u32[]{:S(2)}, u32[]{:S(2)}) collective-permute-start(bf16[128,2048]{1,0:T(8,128)(2,1)} %param.11), channel_id=1, source_target_pairs={{0,1},{1,0},{2,3},{3,2},{4,5},{5,4},{6,7},{7,6},{8,9},{9,8},{10,11... | collective-permute-start | bytes 1572872 | tf_op jit(solution)/shard_map/ppermute | solution.py:18
  3.7 5.7 %collective-permute-start = (bf16[32,1024]{1,0:T(8,128)(2,1)}, bf16[32,1024]{1,0:T(8,128)(2,1)S(1)}, u32[]{:S(2)}, u32[]{:S(2)}) collective-permute-start(bf16[32,1024]{1,0:T(8,128)(2,1)} %bitcast.46), channel_id=1, source_target_pairs={{0,16},{2,18},{4,20},{6,22},{8,24},{10,26},{12,28},{14,30},{16,0},... | collective-permute-start | bytes 196616 | tf_op jit(solution)/shard_map/ppermute | solution.py:14
  6.3 5.3 %collective-permute-start.3 = (s32[2,1]{0,1:T(1,128)}, s32[2,1]{0,1:T(1,128)S(1)}, u32[]{:S(2)}, u32[]{:S(2)}) collective-permute-start(s32[2,1]{0,1:T(1,128)} %param.10), channel_id=1, source_target_pairs={{0,4},{2,6},{4,0},{6,2},{8,12},{10,14},{12,8},{14,10},{16,20},{18,... | collective-permute-start | bytes 32 | tf_op jit(solution)/shard_map/ppermute | solution.py:14
  10.2 5.0 %collective-permute-start.1 = (bf16[64,1024]{1,0:T(8,128)(2,1)S(1)}, bf16[64,1024]{1,0:T(8,128)(2,1)S(1)}, u32[]{:S(2)}, u32[]{:S(2)}) collective-permute-start(bf16[64,1024]{1,0:T(8,128)(2,1)S(1)} %pad_maximum_fusion.5), channel_id=1, source_target_pairs={{0,8},{2,10},{4,12},{6,14},{8,0},{10,2},{12,4},{14,6},{16,24},{18,... | collective-permute-start | bytes 393224 | tf_op jit(solution)/shard_map/ppermute | solution.py:14
  16.1 1.6 %collective-permute-start.2 = (bf16[128,1024]{1,0:T(8,128)(2,1)S(1)}, bf16[128,1024]{1,0:T(8,128)(2,1)S(1)}, u32[]{:S(2)}, u32[]{:S(2)}) collective-permute-start(bf16[128,1024]{1,0:T(8,128)(2,1)S(1)} %pad_maximum_fusion.4), channel_id=1, source_target_pairs={{0,2},{2,0},{4,6},{6,4},{8,10},{10,8},{12,14},{14,12},{16,18},{18,... | collective-permute-start | bytes 786440 | tf_op jit(solution)/shard_map/ppermute | solution.py:14
  17.9 8.0 %copy-start.2 = (bf16[1,32,1024]{2,1,0:T(8,128)(2,1)S(1)}, bf16[1,32,1024]{2,1,0:T(8,128)(2,1)}, u32[]{:S(2)}) copy-start(bf16[1,32,1024]{2,1,0:T(8,128)(2,1)} %param.9) | copy-start | bytes 196612
  19.1 6.6 %collective-permute-start.4 = (bf16[64,1024]{1,0:T(8,128)(2,1)S(1)}, bf16[64,1024]{1,0:T(8,128)(2,1)S(1)}, u32[]{:S(2)}, u32[]{:S(2)}) collective-permute-start(bf16[64,1024]{1,0:T(8,128)(2,1)S(1)} %fusion.15), channel_id=1, source_target_pairs={{0,4},{2,6},{4,0},{6,2},{8,12},{10,14},{12,8},{14,10},{16,20},{18,... | collective-permute-start | bytes 393224 | tf_op jit(solution)/shard_map/ppermute | solution.py:14
  20.7 20.1 %collective-permute-start.7 = (bf16[32,4096]{1,0:T(8,128)(2,1)S(1)}, bf16[32,4096]{1,0:T(8,128)(2,1)S(1)}, u32[]{:S(2)}, u32[]{:S(2)}) collective-permute-start(bf16[32,4096]{1,0:T(8,128)(2,1)S(1)} %bitcast.51), channel_id=1, source_target_pairs={{0,16},{2,18},{4,20},{6,22},{8,24},{10,26},{12,28},{14,30},{16,0},... | collective-permute-start | bytes 786440 | tf_op jit(solution)/shard_map/ppermute | solution.py:14
  23.1 23.7 %collective-permute-start.8 = (bf16[32,4096]{1,0:T(8,128)(2,1)S(1)}, bf16[32,4096]{1,0:T(8,128)(2,1)S(1)}, u32[]{:S(2)}, u32[]{:S(2)}) collective-permute-start(bf16[32,4096]{1,0:T(8,128)(2,1)S(1)} %bitcast.52), channel_id=1, source_target_pairs={{0,8},{2,10},{4,12},{6,14},{8,0},{10,2},{12,4},{14,6},{16,24},{18,... | collective-permute-start | bytes 786440 | tf_op jit(solution)/shard_map/ppermute | solution.py:14
  25.7 1.6 %copy-start = (bf16[256,4096]{1,0:T(8,128)(2,1)S(1)}, bf16[256,4096]{1,0:T(8,128)(2,1)}, u32[]{:S(2)}) copy-start(bf16[256,4096]{1,0:T(8,128)(2,1)} %param.6) | copy-start | bytes 6291460
  28.3 18.4 %collective-permute-start.12 = (bf16[64,2048]{1,0:T(8,128)(2,1)S(1)}, bf16[64,2048]{1,0:T(8,128)(2,1)S(1)}, u32[]{:S(2)}, u32[]{:S(2)}) collective-permute-start(bf16[64,2048]{1,0:T(8,128)(2,1)S(1)} %fusion.10), channel_id=1, source_target_pairs={{0,4},{2,6},{4,0},{6,2},{8,12},{10,14},{12,8},{14,10},{16,20},{18,... | collective-permute-start | bytes 786440 | tf_op jit(solution)/shard_map/ppermute | solution.py:14
  29.8 18.9 %collective-permute-start.14 = (bf16[64,2048]{1,0:T(8,128)(2,1)S(1)}, bf16[64,2048]{1,0:T(8,128)(2,1)S(1)}, u32[]{:S(2)}, u32[]{:S(2)}) collective-permute-start(bf16[64,2048]{1,0:T(8,128)(2,1)S(1)} %fusion.11), channel_id=1, source_target_pairs={{0,4},{2,6},{4,0},{6,2},{8,12},{10,14},{12,8},{14,10},{16,20},{18,... | collective-permute-start | bytes 786440 | tf_op jit(solution)/shard_map/ppermute | solution.py:14
  39.8 40.6 %collective-permute-start.6 = (bf16[128,2048]{1,0:T(8,128)(2,1)S(1)}, bf16[128,2048]{1,0:T(8,128)(2,1)S(1)}, u32[]{:S(2)}, u32[]{:S(2)}) collective-permute-start(bf16[128,2048]{1,0:T(8,128)(2,1)S(1)} %dynamic-slice_convert_fusion), channel_id=1, source_target_pairs={{0,1},{1,0},{2,3},{3,2},{4,5},{5,4},{6,7},{7,6},{8,9},{9,8},{10,11... | collective-permute-start | bytes 1572872 | tf_op jit(solution)/shard_map/ppermute | solution.py:18
  40.8 6.7 %collective-permute-start.9 = (bf16[32,4096]{1,0:T(8,128)(2,1)S(1)}, bf16[32,4096]{1,0:T(8,128)(2,1)S(1)}, u32[]{:S(2)}, u32[]{:S(2)}) collective-permute-start(bf16[32,4096]{1,0:T(8,128)(2,1)S(1)} %collective-permute-done.7), channel_id=1, source_target_pairs={{0,8},{2,10},{4,12},{6,14},{8,0},{10,2},{12,4},{14,6},{16,24},{18,... | collective-permute-start | bytes 786440 | tf_op jit(solution)/shard_map/ppermute | solution.py:14
  47.6 2.7 %collective-permute-start.10 = (bf16[128,4096]{1,0:T(8,128)(2,1)S(1)}, bf16[128,4096]{1,0:T(8,128)(2,1)S(1)}, u32[]{:S(2)}, u32[]{:S(2)}) collective-permute-start(bf16[128,4096]{1,0:T(8,128)(2,1)S(1)} %pad_maximum_fusion.1), channel_id=1, source_target_pairs={{0,2},{2,0},{4,6},{6,4},{8,10},{10,8},{12,14},{14,12},{16,18},{18,... | collective-permute-start | bytes 3145736 | tf_op jit(solution)/shard_map/ppermute | solution.py:14
  48.1 3.2 %collective-permute-start.13 = (bf16[128,2048]{1,0:T(8,128)(2,1)S(1)}, bf16[128,2048]{1,0:T(8,128)(2,1)S(1)}, u32[]{:S(2)}, u32[]{:S(2)}) collective-permute-start(bf16[128,2048]{1,0:T(8,128)(2,1)S(1)} %fusion.8), channel_id=1, source_target_pairs={{0,2},{2,0},{4,6},{6,4},{8,10},{10,8},{12,14},{14,12},{16,18},{18,... | collective-permute-start | bytes 1572872 | tf_op jit(solution)/shard_map/ppermute | solution.py:14
  49.1 2.7 %collective-permute-start.15 = (bf16[128,2048]{1,0:T(8,128)(2,1)S(1)}, bf16[128,2048]{1,0:T(8,128)(2,1)S(1)}, u32[]{:S(2)}, u32[]{:S(2)}) collective-permute-start(bf16[128,2048]{1,0:T(8,128)(2,1)S(1)} %fusion.9), channel_id=1, source_target_pairs={{0,2},{2,0},{4,6},{6,4},{8,10},{10,8},{12,14},{14,12},{16,18},{18,... | collective-permute-start | bytes 1572872 | tf_op jit(solution)/shard_map/ppermute | solution.py:14
  50.7 14.0 %collective-permute-start.11 = (bf16[64,4096]{1,0:T(8,128)(2,1)S(1)}, bf16[64,4096]{1,0:T(8,128)(2,1)S(1)}, u32[]{:S(2)}, u32[]{:S(2)}) collective-permute-start(bf16[64,4096]{1,0:T(8,128)(2,1)S(1)} %fusion.5), channel_id=1, source_target_pairs={{0,4},{2,6},{4,0},{6,2},{8,12},{10,14},{12,8},{14,10},{16,20},{18,... | collective-permute-start | bytes 1572872 | tf_op jit(solution)/shard_map/ppermute | solution.py:14
  52.3 9.2 %collective-permute-start.20 = (bf16[64,2048]{1,0:T(8,128)(2,1)S(1)}, bf16[64,2048]{1,0:T(8,128)(2,1)S(1)}, u32[]{:S(2)}, u32[]{:S(2)}) collective-permute-start(bf16[64,2048]{1,0:T(8,128)(2,1)S(1)} %slice.203), channel_id=1, source_target_pairs={{0,8},{2,10},{4,12},{6,14},{8,0},{10,2},{12,4},{14,6},{16,24},{18,... | collective-permute-start | bytes 786440 | tf_op jit(solution)/shard_map/ppermute | solution.py:14
  53.7 13.8 %collective-permute-start.17 = (bf16[64,2048]{1,0:T(8,128)(2,1)S(1)}, bf16[64,2048]{1,0:T(8,128)(2,1)S(1)}, u32[]{:S(2)}, u32[]{:S(2)}) collective-permute-start(bf16[64,2048]{1,0:T(8,128)(2,1)S(1)} %slice.202), channel_id=1, source_target_pairs={{0,8},{2,10},{4,12},{6,14},{8,0},{10,2},{12,4},{14,6},{16,24},{18,... | collective-permute-start | bytes 786440 | tf_op jit(solution)/shard_map/ppermute | solution.py:14
  65.9 4.6 %collective-permute-start.16 = (f32[32,256]{1,0:T(8,128)S(1)}, f32[32,256]{1,0:T(8,128)S(1)}, u32[]{:S(2)}, u32[]{:S(2)}) collective-permute-start(f32[32,256]{1,0:T(8,128)S(1)} %slice_add_fusion.5), channel_id=1, source_target_pairs={{0,1},{1,0},{2,3},{3,2},{4,5},{5,4},{6,7},{7,6},{8,9},{9,8},{10,11... | collective-permute-start | bytes 98312 | tf_op jit(solution)/shard_map/ppermute | solution.py:18
  67.5 15.8 %collective-permute-start.18 = (bf16[32,2048]{1,0:T(8,128)(2,1)S(1)}, bf16[32,2048]{1,0:T(8,128)(2,1)S(1)}, u32[]{:S(2)}, u32[]{:S(2)}) collective-permute-start(bf16[32,2048]{1,0:T(8,128)(2,1)S(1)} %fusion.22), channel_id=1, source_target_pairs={{0,16},{2,18},{4,20},{6,22},{8,24},{10,26},{12,28},{14,30},{16,0},... | collective-permute-start | bytes 393224 | tf_op jit(solution)/shard_map/ppermute | solution.py:14
  69.6 13.4 %collective-permute-start.23 = (bf16[32,2048]{1,0:T(8,128)(2,1)S(1)}, bf16[32,2048]{1,0:T(8,128)(2,1)S(1)}, u32[]{:S(2)}, u32[]{:S(2)}) collective-permute-start(bf16[32,2048]{1,0:T(8,128)(2,1)S(1)} %fusion.21), channel_id=1, source_target_pairs={{0,16},{2,18},{4,20},{6,22},{8,24},{10,26},{12,28},{14,30},{16,0},... | collective-permute-start | bytes 393224 | tf_op jit(solution)/shard_map/ppermute | solution.py:14
  71.8 4.3 %collective-permute-start.19 = (bf16[64,512]{1,0:T(8,128)(2,1)S(1)}, bf16[64,512]{1,0:T(8,128)(2,1)S(1)}, u32[]{:S(2)}, u32[]{:S(2)}) collective-permute-start(bf16[64,512]{1,0:T(8,128)(2,1)S(1)} %select_convert_fusion), channel_id=1, source_target_pairs={{0,4},{2,6},{4,0},{6,2},{8,12},{10,14},{12,8},{14,10},{16,20},{18,... | collective-permute-start | bytes 196616 | tf_op jit(solution)/shard_map/ppermute | solution.py:14
  76.4 1.4 %collective-permute-start.21 = (bf16[128,512]{1,0:T(8,128)(2,1)S(1)}, bf16[128,512]{1,0:T(8,128)(2,1)S(1)}, u32[]{:S(2)}, u32[]{:S(2)}) collective-permute-start(bf16[128,512]{1,0:T(8,128)(2,1)S(1)} %fusion.16), channel_id=1, source_target_pairs={{0,2},{2,0},{4,6},{6,4},{8,10},{10,8},{12,14},{14,12},{16,18},{18,... | collective-permute-start | bytes 393224 | tf_op jit(solution)/shard_map/ppermute | solution.py:14
  78.2 5.1 %collective-permute-start.22 = (bf16[32,512]{1,0:T(8,128)(2,1)S(1)}, bf16[32,512]{1,0:T(8,128)(2,1)S(1)}, u32[]{:S(2)}, u32[]{:S(2)}) collective-permute-start(bf16[32,512]{1,0:T(8,128)(2,1)S(1)} %get-tuple-element.54), channel_id=1, source_target_pairs={{0,16},{2,18},{4,20},{6,22},{8,24},{10,26},{12,28},{14,30},{16,0},... | collective-permute-start | bytes 98312 | tf_op jit(solution)/shard_map/ppermute | solution.py:14
  81.5 5.8 %collective-permute-start.25 = (bf16[32,512]{1,0:T(8,128)(2,1)S(1)}, bf16[32,512]{1,0:T(8,128)(2,1)S(1)}, u32[]{:S(2)}, u32[]{:S(2)}) collective-permute-start(bf16[32,512]{1,0:T(8,128)(2,1)S(1)} %get-tuple-element.53), channel_id=1, source_target_pairs={{0,24},{2,26},{4,28},{6,30},{8,16},{10,18},{12,20},{14,22},{16,8},... | collective-permute-start | bytes 98312 | tf_op jit(solution)/shard_map/ppermute | solution.py:14
  83.0 4.3 %collective-permute-start.24 = (bf16[32,512]{1,0:T(8,128)(2,1)S(1)}, bf16[32,512]{1,0:T(8,128)(2,1)S(1)}, u32[]{:S(2)}, u32[]{:S(2)}) collective-permute-start(bf16[32,512]{1,0:T(8,128)(2,1)S(1)} %get-tuple-element.52), channel_id=1, source_target_pairs={{0,8},{2,10},{4,12},{6,14},{8,0},{10,2},{12,4},{14,6},{16,24},{18,... | collective-permute-start | bytes 98312 | tf_op jit(solution)/shard_map/ppermute | solution.py:14

commit v6 on v5

--- a/solution.py
+++ b/solution.py
@@ -163,20 +163,21 @@
             blocks_a[-1] = late_hop = after(blocks_a[-1], down[0])
         blocks_a = blocks_a + [swap(block, 1 << bit) for block in blocks_a]
     here_a = jnp.concatenate(blocks_a, axis=0)
-    if tp_count == 2:
-        base = dot(after(tokens, down[-1]), weight, (1, 0))
+    half = features // 2
+    base_low = dot(after(grad_rows, down[-1]), weight[:half], (1, 1))
+    if tp_count == 2:
+        base = dot(after(tokens, late_hop), weight, (1, 0))
         near_base = lax.dynamic_slice_in_dim(base, col * local_rows, local_rows, 0)
         far_base = lax.dynamic_slice_in_dim(base, (1 - col) * local_rows, local_rows, 0).astype(bf16)
-        base_rows = near_base + cross(far_base).astype(f32)
     else:
         far_base = dot(tokens, weight, (1, 0))
         base_rows = lax.psum_scatter(far_base, "tp", scatter_dimension=0, tiled=True)
-    half = features // 2
-    base_low = dot(after(grad_rows, late_hop), weight[:half], (1, 1))
-    here_a = after(here_a, base_low)
+    here_a = after(here_a, far_base)
     there_a = swap(here_a, core)
     sent_a = give_away(here_a, there_a)
 
+    if tp_count == 2:
+        base_rows = near_base + cross(after(far_base, sent_a)).astype(f32)
     got_c = [after(swap(d, far), far_base) for d in down]
     back_c = [swap(core_part(d, g), core) for d, g in zip(down, got_c)]
     mark = sent_a

time: 88.3 us -> 86.4 us (0.978)
  waiting for transfers between devices: 16.4 us -> 13.1 us
  starting transfers between devices: 29.9 us -> 31.4 us
    ppermute x23, waiting for transfers between devices: 16.4 us -> 13.1 us  [swap(): return lax.ppermute(value, 'blk', [(i, i ^ offset) for i in range(count)])]
    ppermute x23, starting transfers between devices: 24.7 us -> 26.8 us  [swap(): return lax.ppermute(value, 'blk', [(i, i ^ offset) for i in range(count)])]
  transfers between devices with their start and end apart: 26 -> 26, of which waited for: 12 -> 8; matrix products, arithmetic and copies ran while one was open for 45% -> 45% of each run, Pallas kernels for 0% -> 0%
where the time goes in v6:
time: 86.4 us; the launch traced here: 86 us
  matrix products  32.5 us (38%)
  starting transfers between devices  31.4 us (36%)
  waiting for transfers between devices  13.1 us (15%)
  other arithmetic  6.75 us (8%)
  between operations  1.15 us (1%)
  local copies, waits for them, and re-layouts  1.08 us (1%)
    dot_general x33, matrix products, dot(): lax.dot_general(a, b, ((contract[:1], contract[1:]), ((), ())), preferred...  32.5 us
    ppermute x23, starting transfers between devices, swap(): return lax.ppermute(value, 'blk', [(i, i ^ offset) for i in range(count)])  26.8 us
    ppermute x23, waiting for transfers between devices, swap(): return lax.ppermute(value, 'blk', [(i, i ^ offset) for i in range(count)])  13.1 us
    ppermute x3, starting transfers between devices, cross(): return lax.ppermute(value, 'tp', [(0, 1), (1, 0)])  4.63 us
  transfers between devices with their start and end apart: 26, of which 8 were waited for; matrix products, arithmetic and copies ran while one was open for 45% of the time, Pallas kernels for 0%

profile of v6, /device:TPU:0, one launch (start us, length us, event | category | flops | bytes accessed | tf_op | source)
XLA Modules:
  0.0 86.0 jit_solution(10700360901721754801)
XLA Ops:
  0.7 4.1 %collective-permute-start.1 = (bf16[32,1024]{1,0:T(8,128)(2,1)}, bf16[32,1024]{1,0:T(8,128)(2,1)S(1)}, u32[]{:S(2)}, u32[]{:S(2)}) collective-permute-start(bf16[32,1024]{1,0:T(8,128)(2,1)} %bitcast.46), channel_id=1, source_target_pairs={{0,16},{2,18},{4,20},{6,22},{8,24},{10,26},{12,28},{14,30},{16,0},... | collective-permute-start | bytes 196616 | tf_op jit(solution)/shard_map/ppermute | solution.py:14
  4.8 1.5 %collective-permute-start = (s32[2,1]{0,1:T(1,128)}, s32[2,1]{0,1:T(1,128)S(1)}, u32[]{:S(2)}, u32[]{:S(2)}) collective-permute-start(s32[2,1]{0,1:T(1,128)} %param.10), channel_id=1, source_target_pairs={{0,4},{2,6},{4,0},{6,2},{8,12},{10,14},{12,8},{14,10},{16,20},{18,... | collective-permute-start | bytes 32 | tf_op jit(solution)/shard_map/ppermute | solution.py:14
  6.2 1.5 %collective-permute-start.6 = (bf16[128,2048]{1,0:T(8,128)(2,1)}, bf16[128,2048]{1,0:T(8,128)(2,1)S(1)}, u32[]{:S(2)}, u32[]{:S(2)}) collective-permute-start(bf16[128,2048]{1,0:T(8,128)(2,1)} %param.11), channel_id=1, source_target_pairs={{0,1},{1,0},{2,3},{3,2},{4,5},{5,4},{6,7},{7,6},{8,9},{9,8},{10,11... | collective-permute-start | bytes 1572872 | tf_op jit(solution)/shard_map/ppermute | solution.py:18
  7.9 0.7 collective-permute-done.1
  8.6 0.9 pad_maximum_fusion.5
  9.5 1.0 %collective-permute-start.2 = (bf16[64,1024]{1,0:T(8,128)(2,1)S(1)}, bf16[64,1024]{1,0:T(8,128)(2,1)S(1)}, u32[]{:S(2)}, u32[]{:S(2)}) collective-permute-start(bf16[64,1024]{1,0:T(8,128)(2,1)S(1)} %pad_maximum_fusion.5), channel_id=1, source_target_pairs={{0,8},{2,10},{4,12},{6,14},{8,0},{10,2},{12,4},{14,6},{16,24},{18,... | collective-permute-start | bytes 393224 | tf_op jit(solution)/shard_map/ppermute | solution.py:14
  10.5 4.0 %collective-permute-done.2 = bf16[64,1024]{1,0:T(8,128)(2,1)S(1)} collective-permute-done((bf16[64,1024]{1,0:T(8,128)(2,1)S(1)}, bf16[64,1024]{1,0:T(8,128)(2,1)S(1)}, u32[]{:S(2)}, u32[]{:S(2)}) %collective-permute-start.2) | collective-permute-done | bytes 131104 | tf_op jit(solution)/shard_map/ppermute | solution.py:14
  14.5 0.9 %pad_maximum_fusion.4 = bf16[128,1024]{1,0:T(8,128)(2,1)S(1)} fusion(bf16[64,1024]{1,0:T(8,128)(2,1)S(1)} %collective-permute-done.2, bf16[32,1024]{1,0:T(8,128)(2,1)S(1)} %collective-permute-done.1, bf16[32,1024]{1,0:T(8,128)(2,1)} %bitcast.48), kind=kLoop, calls=%fused_computation.64 | loop fusion | flops 786432 | bytes 524288 | tf_op jit(solution)/shard_map/concatenate | solution.py:103
  15.4 0.7 xor_bitcast_fusion
  16.4 0.5 collective-permute-done.3
  17.2 1.1 %fusion.14 = bf16[64,1024]{1,0:T(8,128)(2,1)S(1)} fusion(f32[64,1024]{1,0:T(8,128)S(1)} %fusion.64, s32[128]{0:T(128)S(1)} %get-tuple-element.63, s32[128]{0:T(128)S(1)} %get-tuple-element.67, s32[64]{0:T(128)S(1)} %broadcast_in_dim.54, pred[128]{0:T(512)(128)(4,1)S(1)} %get-tuple-element.61, s32[128]{0:T(128)S(1)} %get-tuple-element.64, ...), kind=kOutput, calls=%fused_computation.34 | convolution fusion | flops 17793024 | bytes 658496 | tf_op jit(solution)/shard_map/dot_general | solution.py:22
  18.4 1.8 %collective-permute-start.5 = (bf16[64,1024]{1,0:T(8,128)(2,1)S(1)}, bf16[64,1024]{1,0:T(8,128)(2,1)S(1)}, u32[]{:S(2)}, u32[]{:S(2)}) collective-permute-start(bf16[64,1024]{1,0:T(8,128)(2,1)S(1)} %fusion.14), channel_id=1, source_target_pairs={{0,4},{2,6},{4,0},{6,2},{8,12},{10,14},{12,8},{14,10},{16,20},{18,... | collective-permute-start | bytes 393224 | tf_op jit(solution)/shard_map/ppermute | solution.py:14
  20.1 2.1 %collective-permute-start.4 = (bf16[32,4096]{1,0:T(8,128)(2,1)S(1)}, bf16[32,4096]{1,0:T(8,128)(2,1)S(1)}, u32[]{:S(2)}, u32[]{:S(2)}) collective-permute-start(bf16[32,4096]{1,0:T(8,128)(2,1)S(1)} %bitcast.51), channel_id=1, source_target_pairs={{0,16},{2,18},{4,20},{6,22},{8,24},{10,26},{12,28},{14,30},{16,0},... | collective-permute-start | bytes 786440 | tf_op jit(solution)/shard_map/ppermute | solution.py:14
  22.2 1.7 %collective-permute-start.7 = (bf16[32,4096]{1,0:T(8,128)(2,1)S(1)}, bf16[32,4096]{1,0:T(8,128)(2,1)S(1)}, u32[]{:S(2)}, u32[]{:S(2)}) collective-permute-start(bf16[32,4096]{1,0:T(8,128)(2,1)S(1)} %bitcast.52), channel_id=1, source_target_pairs={{0,8},{2,10},{4,12},{6,14},{8,0},{10,2},{12,4},{14,6},{16,24},{18,... | collective-permute-start | bytes 786440 | tf_op jit(solution)/shard_map/ppermute | solution.py:14
  25.1 0.4 fusion.17
  25.5 0.6 copy-done
  26.7 0.4 fusion.67
  27.2 0.6 collective-permute-start.12
  27.8 0.4 fusion.71
  28.2 1.6 %collective-permute-start.14 = (bf16[64,2048]{1,0:T(8,128)(2,1)S(1)}, bf16[64,2048]{1,0:T(8,128)(2,1)S(1)}, u32[]{:S(2)}, u32[]{:S(2)}) collective-permute-start(bf16[64,2048]{1,0:T(8,128)(2,1)S(1)} %fusion.10), channel_id=1, source_target_pairs={{0,4},{2,6},{4,0},{6,2},{8,12},{10,14},{12,8},{14,10},{16,20},{18,... | collective-permute-start | bytes 786440 | tf_op jit(solution)/shard_map/ppermute | solution.py:14
  29.8 5.9 %fusion = f32[256,2048]{1,0:T(8,128)S(1)} fusion(bf16[256,2048]{1,0:T(8,128)(2,1)S(1)} %maximum_select_fusion, bf16[4096,2048]{1,0:T(8,128)(2,1)} %param.7), kind=kOutput, calls=%fused_computation | convolution fusion | flops 2147483648 | bytes 11534336 | tf_op jit(solution)/shard_map/dot_general | solution.py:22
  35.6 0.4 fusion.66
  36.1 0.4 fusion.70
  36.9 8.2 %fusion.75 = f32[256,2048]{1,0:T(8,128)S(1)} fusion(bf16[256,4096]{1,0:T(8,128)(2,1)S(1)} %copy-done, bf16[4096,2048]{1,0:T(8,128)(2,1)} %param.7), kind=kOutput, calls=%fused_computation.150 | convolution fusion | flops 4294967296 | bytes 20971520 | tf_op jit(solution)/shard_map/dot_general | solution.py:22
  45.3 0.4 fusion.8
  45.8 0.6 collective-permute-start.13
  48.3 0.7 collective-permute-start.11
  49.1 0.4 fusion.7
  49.6 0.4 fusion.6
  50.0 1.7 %collective-permute-start.20 = (bf16[64,2048]{1,0:T(8,128)(2,1)S(1)}, bf16[64,2048]{1,0:T(8,128)(2,1)S(1)}, u32[]{:S(2)}, u32[]{:S(2)}) collective-permute-start(bf16[64,2048]{1,0:T(8,128)(2,1)S(1)} %slice.203), channel_id=1, source_target_pairs={{0,8},{2,10},{4,12},{6,14},{8,0},{10,2},{12,4},{14,6},{16,24},{18,... | collective-permute-start | bytes 786440 | tf_op jit(solution)/shard_map/ppermute | solution.py:14
  52.1 1.5 %collective-permute-start.10 = (bf16[128,2048]{1,0:T(8,128)(2,1)S(1)}, bf16[128,2048]{1,0:T(8,128)(2,1)S(1)}, u32[]{:S(2)}, u32[]{:S(2)}) collective-permute-start(bf16[128,2048]{1,0:T(8,128)(2,1)S(1)} %dynamic-slice_convert_fusion), channel_id=1, source_target_pairs={{0,1},{1,0},{2,3},{3,2},{4,5},{5,4},{6,7},{7,6},{8,9},{9,8},{10,11... | collective-permute-start | bytes 1572872 | tf_op jit(solution)/shard_map/ppermute | solution.py:18
  53.7 5.9 %fusion.2 = f32[256,2048]{1,0:T(8,128)S(1)} fusion(bf16[256,2048]{1,0:T(8,128)(2,1)S(1)} %maximum_select_fusion, bf16[4096,2048]{1,0:T(8,128)(2,1)} %param.7), kind=kOutput, calls=%fused_computation.2 | convolution fusion | flops 2147483648 | bytes 11534336 | tf_op jit(solution)/shard_map/dot_general | solution.py:22
  59.9 2.4 %collective-permute-done.11 = bf16[64,4096]{1,0:T(8,128)(2,1)S(1)} collective-permute-done((bf16[64,4096]{1,0:T(8,128)(2,1)S(1)}, bf16[64,4096]{1,0:T(8,128)(2,1)S(1)}, u32[]{:S(2)}, u32[]{:S(2)}) %collective-permute-start.11) | collective-permute-done | bytes 524320 | tf_op jit(solution)/shard_map/ppermute | solution.py:14
  62.7 0.8 convolution_select_fusion.1
  63.5 1.6 %collective-permute-start.16 = (f32[32,256]{1,0:T(8,128)S(1)}, f32[32,256]{1,0:T(8,128)S(1)}, u32[]{:S(2)}, u32[]{:S(2)}) collective-permute-start(f32[32,256]{1,0:T(8,128)S(1)} %slice_add_fusion.5), channel_id=1, source_target_pairs={{0,1},{1,0},{2,3},{3,2},{4,5},{5,4},{6,7},{7,6},{8,9},{9,8},{10,11... | collective-permute-start | bytes 98312 | tf_op jit(solution)/shard_map/ppermute | solution.py:18
  65.1 2.6 %collective-permute-start.18 = (bf16[32,2048]{1,0:T(8,128)(2,1)S(1)}, bf16[32,2048]{1,0:T(8,128)(2,1)S(1)}, u32[]{:S(2)}, u32[]{:S(2)}) collective-permute-start(bf16[32,2048]{1,0:T(8,128)(2,1)S(1)} %fusion.22), channel_id=1, source_target_pairs={{0,16},{2,18},{4,20},{6,22},{8,24},{10,26},{12,28},{14,30},{16,0},... | collective-permute-start | bytes 393224 | tf_op jit(solution)/shard_map/ppermute | solution.py:14
  68.1 0.5 convolution_multiply_fusion
  68.6 0.5 convolution_multiply_fusion.1
  69.4 1.3 %collective-permute-start.19 = (bf16[64,512]{1,0:T(8,128)(2,1)S(1)}, bf16[64,512]{1,0:T(8,128)(2,1)S(1)}, u32[]{:S(2)}, u32[]{:S(2)}) collective-permute-start(bf16[64,512]{1,0:T(8,128)(2,1)S(1)} %select_convert_fusion), channel_id=1, source_target_pairs={{0,4},{2,6},{4,0},{6,2},{8,12},{10,14},{12,8},{14,10},{16,20},{18,... | collective-permute-start | bytes 196616 | tf_op jit(solution)/shard_map/ppermute | solution.py:14
  71.3 1.5 %pad_maximum_fusion = bf16[256,4096]{1,0:T(8,128)(2,1)} fusion(bf16[256,2048]{1,0:T(8,128)(2,1)S(1)} %add_convert_fusion, bf16[256,2048]{1,0:T(8,128)(2,1)S(1)} %add_convert_fusion.1), kind=kLoop, calls=%fused_computation.25 | loop fusion | flops 4194304 | bytes 4194304 | tf_op jit(solution)/shard_map/concatenate | solution.py:234
  73.2 0.6 collective-permute-done.19
  74.4 1.0 %collective-permute-done.21 = bf16[128,512]{1,0:T(8,128)(2,1)S(1)} collective-permute-done((bf16[128,512]{1,0:T(8,128)(2,1)S(1)}, bf16[128,512]{1,0:T(8,128)(2,1)S(1)}, u32[]{:S(2)}, u32[]{:S(2)}) %collective-permute-start.21) | collective-permute-done | bytes 131104 | tf_op jit(solution)/shard_map/ppermute | solution.py:14
  75.8 2.6 %collective-permute-start.22 = (bf16[32,512]{1,0:T(8,128)(2,1)S(1)}, bf16[32,512]{1,0:T(8,128)(2,1)S(1)}, u32[]{:S(2)}, u32[]{:S(2)}) collective-permute-start(bf16[32,512]{1,0:T(8,128)(2,1)S(1)} %get-tuple-element.56), channel_id=1, source_target_pairs={{0,16},{2,18},{4,20},{6,22},{8,24},{10,26},{12,28},{14,30},{16,0},... | collective-permute-start | bytes 98312 | tf_op jit(solution)/shard_map/ppermute | solution.py:14
  78.4 1.1 %add_convert_fusion.2 = bf16[128,2048]{1,0:T(8,128)(2,1)} fusion(bf16[128,2048]{1,0:T(8,128)(2,1)S(1)} %collective-permute-done.10, f32[256,2048]{1,0:T(8,128)S(1)} %fusion.75, s32[]{:T(128)S(6)} %select_n.168, bf16[64,1024]{1,0:T(8,128)(2,1)S(1)} %get-tuple-element.52, bf16[64,1024]{1,0:T(8,128)(2,1)S(1)} %get-tuple-element.53, pred[]{:T(512)S(6)} %eq.111, ...), kind=kOutput, calls=%fused_computation.42 | convolution fusion | flops 18743296 | bytes 2369536 | tf_op jit(solution)/shard_map/dot_general | solution.py:22
  79.6 1.6 %collective-permute-start.25 = (bf16[32,512]{1,0:T(8,128)(2,1)S(1)}, bf16[32,512]{1,0:T(8,128)(2,1)S(1)}, u32[]{:S(2)}, u32[]{:S(2)}) collective-permute-start(bf16[32,512]{1,0:T(8,128)(2,1)S(1)} %get-tuple-element.55), channel_id=1, source_target_pairs={{0,24},{2,26},{4,28},{6,30},{8,16},{10,18},{12,20},{14,22},{16,8},... | collective-permute-start | bytes 98312 | tf_op jit(solution)/shard_map/ppermute | solution.py:14
  81.2 0.8 maximum_bitcast_fusion
  82.1 3.3 %collective-permute-done.25 = bf16[32,512]{1,0:T(8,128)(2,1)S(1)} collective-permute-done((bf16[32,512]{1,0:T(8,128)(2,1)S(1)}, bf16[32,512]{1,0:T(8,128)(2,1)S(1)}, u32[]{:S(2)}, u32[]{:S(2)}) %collective-permute-start.25) | collective-permute-done | bytes 32800 | tf_op jit(solution)/shard_map/ppermute | solution.py:14
  85.4 0.7 fusion.36
  (81 shorter events, 9.0 us)
Async XLA Ops:
  0.6 23.6 %copy-start.1 = (bf16[128,2048]{1,0:T(8,128)(2,1)S(1)}, bf16[128,2048]{1,0:T(8,128)(2,1)}, u32[]{:S(2)}) copy-start(bf16[128,2048]{1,0:T(8,128)(2,1)} %param.11) | copy-start | bytes 1572868
  0.6 19.5 %copy-start.3 = (bf16[1,4096,32]{1,2,0:T(8,128)(2,1)S(1)}, bf16[1,4096,32]{1,2,0:T(8,128)(2,1)}, u32[]{:S(2)}) copy-start(bf16[1,4096,32]{1,2,0:T(8,128)(2,1)} %param.8) | copy-start | bytes 786436
  0.7 8.0 %collective-permute-start.1 = (bf16[32,1024]{1,0:T(8,128)(2,1)}, bf16[32,1024]{1,0:T(8,128)(2,1)S(1)}, u32[]{:S(2)}, u32[]{:S(2)}) collective-permute-start(bf16[32,1024]{1,0:T(8,128)(2,1)} %bitcast.46), channel_id=1, source_target_pairs={{0,16},{2,18},{4,20},{6,22},{8,24},{10,26},{12,28},{14,30},{16,0},... | collective-permute-start | bytes 196616 | tf_op jit(solution)/shard_map/ppermute | solution.py:14
  4.8 5.7 %collective-permute-start = (s32[2,1]{0,1:T(1,128)}, s32[2,1]{0,1:T(1,128)S(1)}, u32[]{:S(2)}, u32[]{:S(2)}) collective-permute-start(s32[2,1]{0,1:T(1,128)} %param.10), channel_id=1, source_target_pairs={{0,4},{2,6},{4,0},{6,2},{8,12},{10,14},{12,8},{14,10},{16,20},{18,... | collective-permute-start | bytes 32 | tf_op jit(solution)/shard_map/ppermute | solution.py:14
  6.2 18.0 %collective-permute-start.6 = (bf16[128,2048]{1,0:T(8,128)(2,1)}, bf16[128,2048]{1,0:T(8,128)(2,1)S(1)}, u32[]{:S(2)}, u32[]{:S(2)}) collective-permute-start(bf16[128,2048]{1,0:T(8,128)(2,1)} %param.11), channel_id=1, source_target_pairs={{0,1},{1,0},{2,3},{3,2},{4,5},{5,4},{6,7},{7,6},{8,9},{9,8},{10,11... | collective-permute-start | bytes 1572872 | tf_op jit(solution)/shard_map/ppermute | solution.py:18
  9.5 5.0 %collective-permute-start.2 = (bf16[64,1024]{1,0:T(8,128)(2,1)S(1)}, bf16[64,1024]{1,0:T(8,128)(2,1)S(1)}, u32[]{:S(2)}, u32[]{:S(2)}) collective-permute-start(bf16[64,1024]{1,0:T(8,128)(2,1)S(1)} %pad_maximum_fusion.5), channel_id=1, source_target_pairs={{0,8},{2,10},{4,12},{6,14},{8,0},{10,2},{12,4},{14,6},{16,24},{18,... | collective-permute-start | bytes 393224 | tf_op jit(solution)/shard_map/ppermute | solution.py:14
  15.4 1.6 %collective-permute-start.3 = (bf16[128,1024]{1,0:T(8,128)(2,1)S(1)}, bf16[128,1024]{1,0:T(8,128)(2,1)S(1)}, u32[]{:S(2)}, u32[]{:S(2)}) collective-permute-start(bf16[128,1024]{1,0:T(8,128)(2,1)S(1)} %pad_maximum_fusion.4), channel_id=1, source_target_pairs={{0,2},{2,0},{4,6},{6,4},{8,10},{10,8},{12,14},{14,12},{16,18},{18,... | collective-permute-start | bytes 786440 | tf_op jit(solution)/shard_map/ppermute | solution.py:14
  17.2 7.6 %copy-start.2 = (bf16[1,32,1024]{2,1,0:T(8,128)(2,1)S(1)}, bf16[1,32,1024]{2,1,0:T(8,128)(2,1)}, u32[]{:S(2)}) copy-start(bf16[1,32,1024]{2,1,0:T(8,128)(2,1)} %param.9) | copy-start | bytes 196612
  18.4 6.2 %collective-permute-start.5 = (bf16[64,1024]{1,0:T(8,128)(2,1)S(1)}, bf16[64,1024]{1,0:T(8,128)(2,1)S(1)}, u32[]{:S(2)}, u32[]{:S(2)}) collective-permute-start(bf16[64,1024]{1,0:T(8,128)(2,1)S(1)} %fusion.14), channel_id=1, source_target_pairs={{0,4},{2,6},{4,0},{6,2},{8,12},{10,14},{12,8},{14,10},{16,20},{18,... | collective-permute-start | bytes 393224 | tf_op jit(solution)/shard_map/ppermute | solution.py:14
  20.1 16.4 %collective-permute-start.4 = (bf16[32,4096]{1,0:T(8,128)(2,1)S(1)}, bf16[32,4096]{1,0:T(8,128)(2,1)S(1)}, u32[]{:S(2)}, u32[]{:S(2)}) collective-permute-start(bf16[32,4096]{1,0:T(8,128)(2,1)S(1)} %bitcast.51), channel_id=1, source_target_pairs={{0,16},{2,18},{4,20},{6,22},{8,24},{10,26},{12,28},{14,30},{16,0},... | collective-permute-start | bytes 786440 | tf_op jit(solution)/shard_map/ppermute | solution.py:14
  22.2 22.9 %collective-permute-start.7 = (bf16[32,4096]{1,0:T(8,128)(2,1)S(1)}, bf16[32,4096]{1,0:T(8,128)(2,1)S(1)}, u32[]{:S(2)}, u32[]{:S(2)}) collective-permute-start(bf16[32,4096]{1,0:T(8,128)(2,1)S(1)} %bitcast.52), channel_id=1, source_target_pairs={{0,8},{2,10},{4,12},{6,14},{8,0},{10,2},{12,4},{14,6},{16,24},{18,... | collective-permute-start | bytes 786440 | tf_op jit(solution)/shard_map/ppermute | solution.py:14
  24.5 1.6 %copy-start = (bf16[256,4096]{1,0:T(8,128)(2,1)S(1)}, bf16[256,4096]{1,0:T(8,128)(2,1)}, u32[]{:S(2)}) copy-start(bf16[256,4096]{1,0:T(8,128)(2,1)} %param.6) | copy-start | bytes 6291460
  27.2 17.9 %collective-permute-start.12 = (bf16[64,2048]{1,0:T(8,128)(2,1)S(1)}, bf16[64,2048]{1,0:T(8,128)(2,1)S(1)}, u32[]{:S(2)}, u32[]{:S(2)}) collective-permute-start(bf16[64,2048]{1,0:T(8,128)(2,1)S(1)} %fusion.11), channel_id=1, source_target_pairs={{0,4},{2,6},{4,0},{6,2},{8,12},{10,14},{12,8},{14,10},{16,20},{18,... | collective-permute-start | bytes 786440 | tf_op jit(solution)/shard_map/ppermute | solution.py:14
  28.2 18.1 %collective-permute-start.14 = (bf16[64,2048]{1,0:T(8,128)(2,1)S(1)}, bf16[64,2048]{1,0:T(8,128)(2,1)S(1)}, u32[]{:S(2)}, u32[]{:S(2)}) collective-permute-start(bf16[64,2048]{1,0:T(8,128)(2,1)S(1)} %fusion.10), channel_id=1, source_target_pairs={{0,4},{2,6},{4,0},{6,2},{8,12},{10,14},{12,8},{14,10},{16,20},{18,... | collective-permute-start | bytes 786440 | tf_op jit(solution)/shard_map/ppermute | solution.py:14
  36.5 8.6 %collective-permute-start.8 = (bf16[32,4096]{1,0:T(8,128)(2,1)S(1)}, bf16[32,4096]{1,0:T(8,128)(2,1)S(1)}, u32[]{:S(2)}, u32[]{:S(2)}) collective-permute-start(bf16[32,4096]{1,0:T(8,128)(2,1)S(1)} %collective-permute-done.4), channel_id=1, source_target_pairs={{0,8},{2,10},{4,12},{6,14},{8,0},{10,2},{12,4},{14,6},{16,24},{18,... | collective-permute-start | bytes 786440 | tf_op jit(solution)/shard_map/ppermute | solution.py:14
  45.2 2.7 %collective-permute-start.9 = (bf16[128,4096]{1,0:T(8,128)(2,1)S(1)}, bf16[128,4096]{1,0:T(8,128)(2,1)S(1)}, u32[]{:S(2)}, u32[]{:S(2)}) collective-permute-start(bf16[128,4096]{1,0:T(8,128)(2,1)S(1)} %pad_maximum_fusion.1), channel_id=1, source_target_pairs={{0,2},{2,0},{4,6},{6,4},{8,10},{10,8},{12,14},{14,12},{16,18},{18,... | collective-permute-start | bytes 3145736 | tf_op jit(solution)/shard_map/ppermute | solution.py:14
  45.8 3.3 %collective-permute-start.13 = (bf16[128,2048]{1,0:T(8,128)(2,1)S(1)}, bf16[128,2048]{1,0:T(8,128)(2,1)S(1)}, u32[]{:S(2)}, u32[]{:S(2)}) collective-permute-start(bf16[128,2048]{1,0:T(8,128)(2,1)S(1)} %fusion.8), channel_id=1, source_target_pairs={{0,2},{2,0},{4,6},{6,4},{8,10},{10,8},{12,14},{14,12},{16,18},{18,... | collective-permute-start | bytes 1572872 | tf_op jit(solution)/shard_map/ppermute | solution.py:14
  46.8 2.8 %collective-permute-start.15 = (bf16[128,2048]{1,0:T(8,128)(2,1)S(1)}, bf16[128,2048]{1,0:T(8,128)(2,1)S(1)}, u32[]{:S(2)}, u32[]{:S(2)}) collective-permute-start(bf16[128,2048]{1,0:T(8,128)(2,1)S(1)} %fusion.9), channel_id=1, source_target_pairs={{0,2},{2,0},{4,6},{6,4},{8,10},{10,8},{12,14},{14,12},{16,18},{18,... | collective-permute-start | bytes 1572872 | tf_op jit(solution)/shard_map/ppermute | solution.py:14
  48.3 14.0 %collective-permute-start.11 = (bf16[64,4096]{1,0:T(8,128)(2,1)S(1)}, bf16[64,4096]{1,0:T(8,128)(2,1)S(1)}, u32[]{:S(2)}, u32[]{:S(2)}) collective-permute-start(bf16[64,4096]{1,0:T(8,128)(2,1)S(1)} %fusion.5), channel_id=1, source_target_pairs={{0,4},{2,6},{4,0},{6,2},{8,12},{10,14},{12,8},{14,10},{16,20},{18,... | collective-permute-start | bytes 1572872 | tf_op jit(solution)/shard_map/ppermute | solution.py:14
  50.0 9.8 %collective-permute-start.20 = (bf16[64,2048]{1,0:T(8,128)(2,1)S(1)}, bf16[64,2048]{1,0:T(8,128)(2,1)S(1)}, u32[]{:S(2)}, u32[]{:S(2)}) collective-permute-start(bf16[64,2048]{1,0:T(8,128)(2,1)S(1)} %slice.203), channel_id=1, source_target_pairs={{0,8},{2,10},{4,12},{6,14},{8,0},{10,2},{12,4},{14,6},{16,24},{18,... | collective-permute-start | bytes 786440 | tf_op jit(solution)/shard_map/ppermute | solution.py:14
  51.8 13.3 %collective-permute-start.17 = (bf16[64,2048]{1,0:T(8,128)(2,1)S(1)}, bf16[64,2048]{1,0:T(8,128)(2,1)S(1)}, u32[]{:S(2)}, u32[]{:S(2)}) collective-permute-start(bf16[64,2048]{1,0:T(8,128)(2,1)S(1)} %slice.202), channel_id=1, source_target_pairs={{0,8},{2,10},{4,12},{6,14},{8,0},{10,2},{12,4},{14,6},{16,24},{18,... | collective-permute-start | bytes 786440 | tf_op jit(solution)/shard_map/ppermute | solution.py:14
  52.1 26.3 %collective-permute-start.10 = (bf16[128,2048]{1,0:T(8,128)(2,1)S(1)}, bf16[128,2048]{1,0:T(8,128)(2,1)S(1)}, u32[]{:S(2)}, u32[]{:S(2)}) collective-permute-start(bf16[128,2048]{1,0:T(8,128)(2,1)S(1)} %dynamic-slice_convert_fusion), channel_id=1, source_target_pairs={{0,1},{1,0},{2,3},{3,2},{4,5},{5,4},{6,7},{7,6},{8,9},{9,8},{10,11... | collective-permute-start | bytes 1572872 | tf_op jit(solution)/shard_map/ppermute | solution.py:18
  63.5 4.6 %collective-permute-start.16 = (f32[32,256]{1,0:T(8,128)S(1)}, f32[32,256]{1,0:T(8,128)S(1)}, u32[]{:S(2)}, u32[]{:S(2)}) collective-permute-start(f32[32,256]{1,0:T(8,128)S(1)} %slice_add_fusion.5), channel_id=1, source_target_pairs={{0,1},{1,0},{2,3},{3,2},{4,5},{5,4},{6,7},{7,6},{8,9},{9,8},{10,11... | collective-permute-start | bytes 98312 | tf_op jit(solution)/shard_map/ppermute | solution.py:18
  65.1 16.0 %collective-permute-start.18 = (bf16[32,2048]{1,0:T(8,128)(2,1)S(1)}, bf16[32,2048]{1,0:T(8,128)(2,1)S(1)}, u32[]{:S(2)}, u32[]{:S(2)}) collective-permute-start(bf16[32,2048]{1,0:T(8,128)(2,1)S(1)} %fusion.22), channel_id=1, source_target_pairs={{0,16},{2,18},{4,20},{6,22},{8,24},{10,26},{12,28},{14,30},{16,0},... | collective-permute-start | bytes 393224 | tf_op jit(solution)/shard_map/ppermute | solution.py:14
  67.7 13.4 %collective-permute-start.23 = (bf16[32,2048]{1,0:T(8,128)(2,1)S(1)}, bf16[32,2048]{1,0:T(8,128)(2,1)S(1)}, u32[]{:S(2)}, u32[]{:S(2)}) collective-permute-start(bf16[32,2048]{1,0:T(8,128)(2,1)S(1)} %fusion.21), channel_id=1, source_target_pairs={{0,16},{2,18},{4,20},{6,22},{8,24},{10,26},{12,28},{14,30},{16,0},... | collective-permute-start | bytes 393224 | tf_op jit(solution)/shard_map/ppermute | solution.py:14
  69.4 4.3 %collective-permute-start.19 = (bf16[64,512]{1,0:T(8,128)(2,1)S(1)}, bf16[64,512]{1,0:T(8,128)(2,1)S(1)}, u32[]{:S(2)}, u32[]{:S(2)}) collective-permute-start(bf16[64,512]{1,0:T(8,128)(2,1)S(1)} %select_convert_fusion), channel_id=1, source_target_pairs={{0,4},{2,6},{4,0},{6,2},{8,12},{10,14},{12,8},{14,10},{16,20},{18,... | collective-permute-start | bytes 196616 | tf_op jit(solution)/shard_map/ppermute | solution.py:14
  74.0 1.4 %collective-permute-start.21 = (bf16[128,512]{1,0:T(8,128)(2,1)S(1)}, bf16[128,512]{1,0:T(8,128)(2,1)S(1)}, u32[]{:S(2)}, u32[]{:S(2)}) collective-permute-start(bf16[128,512]{1,0:T(8,128)(2,1)S(1)} %fusion.16), channel_id=1, source_target_pairs={{0,2},{2,0},{4,6},{6,4},{8,10},{10,8},{12,14},{14,12},{16,18},{18,... | collective-permute-start | bytes 393224 | tf_op jit(solution)/shard_map/ppermute | solution.py:14
  75.8 5.3 %collective-permute-start.22 = (bf16[32,512]{1,0:T(8,128)(2,1)S(1)}, bf16[32,512]{1,0:T(8,128)(2,1)S(1)}, u32[]{:S(2)}, u32[]{:S(2)}) collective-permute-start(bf16[32,512]{1,0:T(8,128)(2,1)S(1)} %get-tuple-element.56), channel_id=1, source_target_pairs={{0,16},{2,18},{4,20},{6,22},{8,24},{10,26},{12,28},{14,30},{16,0},... | collective-permute-start | bytes 98312 | tf_op jit(solution)/shard_map/ppermute | solution.py:14
  79.6 5.8 %collective-permute-start.25 = (bf16[32,512]{1,0:T(8,128)(2,1)S(1)}, bf16[32,512]{1,0:T(8,128)(2,1)S(1)}, u32[]{:S(2)}, u32[]{:S(2)}) collective-permute-start(bf16[32,512]{1,0:T(8,128)(2,1)S(1)} %get-tuple-element.55), channel_id=1, source_target_pairs={{0,24},{2,26},{4,28},{6,30},{8,16},{10,18},{12,20},{14,22},{16,8},... | collective-permute-start | bytes 98312 | tf_op jit(solution)/shard_map/ppermute | solution.py:14
  81.1 4.3 %collective-permute-start.24 = (bf16[32,512]{1,0:T(8,128)(2,1)S(1)}, bf16[32,512]{1,0:T(8,128)(2,1)S(1)}, u32[]{:S(2)}, u32[]{:S(2)}) collective-permute-start(bf16[32,512]{1,0:T(8,128)(2,1)S(1)} %get-tuple-element.54), channel_id=1, source_target_pairs={{0,8},{2,10},{4,12},{6,14},{8,0},{10,2},{12,4},{14,6},{16,24},{18,... | collective-permute-start | bytes 98312 | tf_op jit(solution)/shard_map/ppermute | solution.py:14

commit v7 on v6

--- a/solution.py
+++ b/solution.py
@@ -112,11 +112,16 @@
         ).astype(bf16)
 
     def sums(sent, got, back):
-        kept = dot(near_here, sent, (0, 0)) + dot(far_here, got, (0, 0)) + back.astype(f32)
+        kept = near_part(sent)[half_rows:] + dot(far_here, got, (0, 0)) + back.astype(f32)
         return dict(zip(places, split(kept)))
 
     def core_part(sent, got):
-        return (dot(near_there, sent, (0, 0)) + dot(far_there, got, (0, 0))).astype(bf16)
+        return (near_part(sent)[:half_rows] + dot(far_there, got, (0, 0))).astype(bf16)
+
+    half_rows = len(places) * rank_two
+
+    def near_part(sent):
+        return dot(jnp.concatenate([near_there, near_here], axis=1), sent, (0, 0))
 
     def leaving(total, bit):
         return jnp.concatenate([total[o].astype(bf16) for o in total if o >> bit & 1], axis=0)

time: 86.4 us -> 86.9 us (level)
  matrix products: 32.5 us -> 31.2 us
  starting transfers between devices: 31.4 us -> 32.4 us
    dot_general x33 -> x30, matrix products: 32.5 us -> 31.2 us  [dot(): lax.dot_general(a, b, ((contract[:1], contract[1:]), ((), ())), preferred...]
    ppermute x23, starting transfers between devices: 26.8 us -> 27.8 us  [swap(): return lax.ppermute(value, 'blk', [(i, i ^ offset) for i in range(count)])]
  transfers between devices with their start and end apart: 26 -> 26, of which waited for: 8 -> 10; matrix products, arithmetic and copies ran while one was open for 45% -> 44% of each run, Pallas kernels for 0% -> 0%
where the time goes in v7:
time: 86.9 us; the launch traced here: 86.5 us
  starting transfers between devices  32.4 us (37%)
  matrix products  31.2 us (36%)
  waiting for transfers between devices  13.9 us (16%)
  other arithmetic  6.77 us (8%)
  between operations  1.13 us (1%)
  local copies, waits for them, and re-layouts  1.08 us (1%)
    dot_general x30, matrix products, dot(): lax.dot_general(a, b, ((contract[:1], contract[1:]), ((), ())), preferred...  31.2 us
    ppermute x23, starting transfers between devices, swap(): return lax.ppermute(value, 'blk', [(i, i ^ offset) for i in range(count)])  27.8 us
    ppermute x23, waiting for transfers between devices, swap(): return lax.ppermute(value, 'blk', [(i, i ^ offset) for i in range(count)])  13.9 us
    ppermute x3, starting transfers between devices, cross(): return lax.ppermute(value, 'tp', [(0, 1), (1, 0)])  4.62 us
  transfers between devices with their start and end apart: 26, of which 10 were waited for; matrix products, arithmetic and copies ran while one was open for 44% of the time, Pallas kernels for 0%

profile of v7, /device:TPU:0, one launch (start us, length us, event | category | flops | bytes accessed | tf_op | source)
XLA Modules:
  0.0 86.5 jit_solution(8611696579868323586)
XLA Ops:
  0.7 3.0 %collective-permute-start = (s32[2,1]{0,1:T(1,128)}, s32[2,1]{0,1:T(1,128)S(1)}, u32[]{:S(2)}, u32[]{:S(2)}) collective-permute-start(s32[2,1]{0,1:T(1,128)} %param.10), channel_id=1, source_target_pairs={{0,4},{2,6},{4,0},{6,2},{8,12},{10,14},{12,8},{14,10},{16,20},{18,... | collective-permute-start | bytes 32 | tf_op jit(solution)/shard_map/ppermute | solution.py:14
  3.7 2.6 %collective-permute-start.1 = (bf16[32,1024]{1,0:T(8,128)(2,1)}, bf16[32,1024]{1,0:T(8,128)(2,1)S(1)}, u32[]{:S(2)}, u32[]{:S(2)}) collective-permute-start(bf16[32,1024]{1,0:T(8,128)(2,1)} %bitcast.43), channel_id=1, source_target_pairs={{0,16},{2,18},{4,20},{6,22},{8,24},{10,26},{12,28},{14,30},{16,0},... | collective-permute-start | bytes 196616 | tf_op jit(solution)/shard_map/ppermute | solution.py:14
  6.2 1.5 %collective-permute-start.6 = (bf16[128,2048]{1,0:T(8,128)(2,1)}, bf16[128,2048]{1,0:T(8,128)(2,1)S(1)}, u32[]{:S(2)}, u32[]{:S(2)}) collective-permute-start(bf16[128,2048]{1,0:T(8,128)(2,1)} %param.11), channel_id=1, source_target_pairs={{0,1},{1,0},{2,3},{3,2},{4,5},{5,4},{6,7},{7,6},{8,9},{9,8},{10,11... | collective-permute-start | bytes 1572872 | tf_op jit(solution)/shard_map/ppermute | solution.py:18
  8.0 1.4 %collective-permute-done.1 = bf16[32,1024]{1,0:T(8,128)(2,1)S(1)} collective-permute-done((bf16[32,1024]{1,0:T(8,128)(2,1)}, bf16[32,1024]{1,0:T(8,128)(2,1)S(1)}, u32[]{:S(2)}, u32[]{:S(2)}) %collective-permute-start.1) | collective-permute-done | bytes 65568 | tf_op jit(solution)/shard_map/ppermute | solution.py:14
  9.3 0.8 pad_maximum_fusion.5
  10.2 1.3 %collective-permute-start.2 = (bf16[64,1024]{1,0:T(8,128)(2,1)S(1)}, bf16[64,1024]{1,0:T(8,128)(2,1)S(1)}, u32[]{:S(2)}, u32[]{:S(2)}) collective-permute-start(bf16[64,1024]{1,0:T(8,128)(2,1)S(1)} %pad_maximum_fusion.5), channel_id=1, source_target_pairs={{0,8},{2,10},{4,12},{6,14},{8,0},{10,2},{12,4},{14,6},{16,24},{18,... | collective-permute-start | bytes 393224 | tf_op jit(solution)/shard_map/ppermute | solution.py:14
  11.5 0.7 xor_bitcast_fusion
  12.3 2.9 %collective-permute-done.2 = bf16[64,1024]{1,0:T(8,128)(2,1)S(1)} collective-permute-done((bf16[64,1024]{1,0:T(8,128)(2,1)S(1)}, bf16[64,1024]{1,0:T(8,128)(2,1)S(1)}, u32[]{:S(2)}, u32[]{:S(2)}) %collective-permute-start.2) | collective-permute-done | bytes 131104 | tf_op jit(solution)/shard_map/ppermute | solution.py:14
  15.2 0.9 pad_maximum_fusion.4
  16.4 1.2 %collective-permute-done.3 = bf16[128,1024]{1,0:T(8,128)(2,1)S(1)} collective-permute-done((bf16[128,1024]{1,0:T(8,128)(2,1)S(1)}, bf16[128,1024]{1,0:T(8,128)(2,1)S(1)}, u32[]{:S(2)}, u32[]{:S(2)}) %collective-permute-start.3) | collective-permute-done | bytes 262176 | tf_op jit(solution)/shard_map/ppermute | solution.py:14
  17.9 1.1 %fusion.14 = bf16[64,1024]{1,0:T(8,128)(2,1)S(1)} fusion(f32[64,1024]{1,0:T(8,128)S(1)} %fusion.69, s32[128]{0:T(128)S(1)} %get-tuple-element.65, s32[128]{0:T(128)S(1)} %get-tuple-element.69, s32[64]{0:T(128)S(1)} %broadcast_in_dim.54, pred[128]{0:T(512)(128)(4,1)S(1)} %get-tuple-element.63, s32[128]{0:T(128)S(1)} %get-tuple-element.66, ...), kind=kOutput, calls=%fused_computation.34 | convolution fusion | flops 17793024 | bytes 658496 | tf_op jit(solution)/shard_map/dot_general | solution.py:22
  19.1 0.6 collective-permute-start.5
  19.7 1.3 %collective-permute-start.7 = (bf16[32,4096]{1,0:T(8,128)(2,1)S(1)}, bf16[32,4096]{1,0:T(8,128)(2,1)S(1)}, u32[]{:S(2)}, u32[]{:S(2)}) collective-permute-start(bf16[32,4096]{1,0:T(8,128)(2,1)S(1)} %bitcast.48), channel_id=1, source_target_pairs={{0,8},{2,10},{4,12},{6,14},{8,0},{10,2},{12,4},{14,6},{16,24},{18,... | collective-permute-start | bytes 786440 | tf_op jit(solution)/shard_map/ppermute | solution.py:14
  21.0 3.2 %collective-permute-start.4 = (bf16[32,4096]{1,0:T(8,128)(2,1)S(1)}, bf16[32,4096]{1,0:T(8,128)(2,1)S(1)}, u32[]{:S(2)}, u32[]{:S(2)}) collective-permute-start(bf16[32,4096]{1,0:T(8,128)(2,1)S(1)} %bitcast.49), channel_id=1, source_target_pairs={{0,16},{2,18},{4,20},{6,22},{8,24},{10,26},{12,28},{14,30},{16,0},... | collective-permute-start | bytes 786440 | tf_op jit(solution)/shard_map/ppermute | solution.py:14
  25.2 0.4 fusion.17
  25.6 0.6 copy-done
  26.9 1.6 %collective-permute-start.12 = (bf16[64,2048]{1,0:T(8,128)(2,1)S(1)}, bf16[64,2048]{1,0:T(8,128)(2,1)S(1)}, u32[]{:S(2)}, u32[]{:S(2)}) collective-permute-start(bf16[64,2048]{1,0:T(8,128)(2,1)S(1)} %fusion.11), channel_id=1, source_target_pairs={{0,4},{2,6},{4,0},{6,2},{8,12},{10,14},{12,8},{14,10},{16,20},{18,... | collective-permute-start | bytes 786440 | tf_op jit(solution)/shard_map/ppermute | solution.py:14
  28.4 0.5 collective-permute-start.14
  29.0 0.5 fusion.63
  29.4 5.7 %fusion = f32[256,2048]{1,0:T(8,128)S(1)} fusion(bf16[256,2048]{1,0:T(8,128)(2,1)S(1)} %maximum_select_fusion, bf16[4096,2048]{1,0:T(8,128)(2,1)} %param.7), kind=kOutput, calls=%fused_computation | convolution fusion | flops 2147483648 | bytes 11534336 | tf_op jit(solution)/shard_map/dot_general | solution.py:22
  35.2 0.5 fusion.64
  35.8 0.6 collective-permute-start.8
  36.4 8.2 %fusion.72 = f32[256,2048]{1,0:T(8,128)S(1)} fusion(bf16[256,4096]{1,0:T(8,128)(2,1)S(1)} %copy-done, bf16[4096,2048]{1,0:T(8,128)(2,1)} %param.7), kind=kOutput, calls=%fused_computation.148 | convolution fusion | flops 4294967296 | bytes 20971520 | tf_op jit(solution)/shard_map/dot_general | solution.py:22
  44.9 0.4 fusion.9
  45.3 0.6 collective-permute-start.15
  47.1 0.4 collective-permute-done.9
  47.9 1.3 %collective-permute-start.11 = (bf16[64,4096]{1,0:T(8,128)(2,1)S(1)}, bf16[64,4096]{1,0:T(8,128)(2,1)S(1)}, u32[]{:S(2)}, u32[]{:S(2)}) collective-permute-start(bf16[64,4096]{1,0:T(8,128)(2,1)S(1)} %fusion.5), channel_id=1, source_target_pairs={{0,4},{2,6},{4,0},{6,2},{8,12},{10,14},{12,8},{14,10},{16,20},{18,... | collective-permute-start | bytes 1572872 | tf_op jit(solution)/shard_map/ppermute | solution.py:14
  49.2 0.4 fusion.6
  49.7 1.8 %collective-permute-start.17 = (bf16[64,2048]{1,0:T(8,128)(2,1)S(1)}, bf16[64,2048]{1,0:T(8,128)(2,1)S(1)}, u32[]{:S(2)}, u32[]{:S(2)}) collective-permute-start(bf16[64,2048]{1,0:T(8,128)(2,1)S(1)} %slice.238), channel_id=1, source_target_pairs={{0,8},{2,10},{4,12},{6,14},{8,0},{10,2},{12,4},{14,6},{16,24},{18,... | collective-permute-start | bytes 786440 | tf_op jit(solution)/shard_map/ppermute | solution.py:14
  51.5 0.4 fusion.7
  52.3 1.5 %collective-permute-start.10 = (bf16[128,2048]{1,0:T(8,128)(2,1)S(1)}, bf16[128,2048]{1,0:T(8,128)(2,1)S(1)}, u32[]{:S(2)}, u32[]{:S(2)}) collective-permute-start(bf16[128,2048]{1,0:T(8,128)(2,1)S(1)} %dynamic-slice_convert_fusion), channel_id=1, source_target_pairs={{0,1},{1,0},{2,3},{3,2},{4,5},{5,4},{6,7},{7,6},{8,9},{9,8},{10,11... | collective-permute-start | bytes 1572872 | tf_op jit(solution)/shard_map/ppermute | solution.py:18
  53.8 5.7 %fusion.2 = f32[256,2048]{1,0:T(8,128)S(1)} fusion(bf16[256,2048]{1,0:T(8,128)(2,1)S(1)} %maximum_select_fusion, bf16[4096,2048]{1,0:T(8,128)(2,1)} %param.7), kind=kOutput, calls=%fused_computation.2 | convolution fusion | flops 2147483648 | bytes 11534336 | tf_op jit(solution)/shard_map/dot_general | solution.py:22
  60.0 1.9 %collective-permute-done.11 = bf16[64,4096]{1,0:T(8,128)(2,1)S(1)} collective-permute-done((bf16[64,4096]{1,0:T(8,128)(2,1)S(1)}, bf16[64,4096]{1,0:T(8,128)(2,1)S(1)}, u32[]{:S(2)}, u32[]{:S(2)}) %collective-permute-start.11) | collective-permute-done | bytes 524320 | tf_op jit(solution)/shard_map/ppermute | solution.py:14
  62.3 0.8 convolution_select_fusion.1
  63.0 1.6 %collective-permute-start.16 = (f32[32,256]{1,0:T(8,128)S(1)}, f32[32,256]{1,0:T(8,128)S(1)}, u32[]{:S(2)}, u32[]{:S(2)}) collective-permute-start(f32[32,256]{1,0:T(8,128)S(1)} %slice_add_fusion.5), channel_id=1, source_target_pairs={{0,1},{1,0},{2,3},{3,2},{4,5},{5,4},{6,7},{7,6},{8,9},{9,8},{10,11... | collective-permute-start | bytes 98312 | tf_op jit(solution)/shard_map/ppermute | solution.py:18
  64.7 3.2 %collective-permute-start.18 = (bf16[32,2048]{1,0:T(8,128)(2,1)S(1)}, bf16[32,2048]{1,0:T(8,128)(2,1)S(1)}, u32[]{:S(2)}, u32[]{:S(2)}) collective-permute-start(bf16[32,2048]{1,0:T(8,128)(2,1)S(1)} %fusion.22), channel_id=1, source_target_pairs={{0,16},{2,18},{4,20},{6,22},{8,24},{10,26},{12,28},{14,30},{16,0},... | collective-permute-start | bytes 393224 | tf_op jit(solution)/shard_map/ppermute | solution.py:14
  68.4 0.5 convolution_multiply_fusion
  68.8 0.5 convolution_multiply_fusion.1
  69.3 1.0 %collective-permute-start.19 = (bf16[64,512]{1,0:T(8,128)(2,1)S(1)}, bf16[64,512]{1,0:T(8,128)(2,1)S(1)}, u32[]{:S(2)}, u32[]{:S(2)}) collective-permute-start(bf16[64,512]{1,0:T(8,128)(2,1)S(1)} %select_convert_fusion), channel_id=1, source_target_pairs={{0,4},{2,6},{4,0},{6,2},{8,12},{10,14},{12,8},{14,10},{16,20},{18,... | collective-permute-start | bytes 196616 | tf_op jit(solution)/shard_map/ppermute | solution.py:14
  71.2 2.4 %collective-permute-done.19 = bf16[64,512]{1,0:T(8,128)(2,1)S(1)} collective-permute-done((bf16[64,512]{1,0:T(8,128)(2,1)S(1)}, bf16[64,512]{1,0:T(8,128)(2,1)S(1)}, u32[]{:S(2)}, u32[]{:S(2)}) %collective-permute-start.19) | collective-permute-done | bytes 65568 | tf_op jit(solution)/shard_map/ppermute | solution.py:14
  74.0 1.5 %pad_maximum_fusion = bf16[256,4096]{1,0:T(8,128)(2,1)} fusion(bf16[256,2048]{1,0:T(8,128)(2,1)S(1)} %add_convert_fusion, bf16[256,2048]{1,0:T(8,128)(2,1)S(1)} %add_convert_fusion.1), kind=kLoop, calls=%fused_computation.25 | loop fusion | flops 4194304 | bytes 4194304 | tf_op jit(solution)/shard_map/concatenate | solution.py:239
  75.9 2.9 %collective-permute-start.22 = (bf16[32,512]{1,0:T(8,128)(2,1)S(1)}, bf16[32,512]{1,0:T(8,128)(2,1)S(1)}, u32[]{:S(2)}, u32[]{:S(2)}) collective-permute-start(bf16[32,512]{1,0:T(8,128)(2,1)S(1)} %get-tuple-element.56), channel_id=1, source_target_pairs={{0,16},{2,18},{4,20},{6,22},{8,24},{10,26},{12,28},{14,30},{16,0},... | collective-permute-start | bytes 98312 | tf_op jit(solution)/shard_map/ppermute | solution.py:14
  78.8 1.1 %add_convert_fusion.2 = bf16[128,2048]{1,0:T(8,128)(2,1)} fusion(bf16[128,2048]{1,0:T(8,128)(2,1)S(1)} %collective-permute-done.10, f32[256,2048]{1,0:T(8,128)S(1)} %fusion.72, s32[]{:T(128)S(6)} %select_n.168, bf16[64,1024]{1,0:T(8,128)(2,1)S(1)} %get-tuple-element.52, bf16[64,1024]{1,0:T(8,128)(2,1)S(1)} %get-tuple-element.53, pred[]{:T(512)S(6)} %eq.111, ...), kind=kOutput, calls=%fused_computation.42 | convolution fusion | flops 18743296 | bytes 2369536 | tf_op jit(solution)/shard_map/dot_general | solution.py:22
  80.1 1.3 %collective-permute-start.25 = (bf16[32,512]{1,0:T(8,128)(2,1)S(1)}, bf16[32,512]{1,0:T(8,128)(2,1)S(1)}, u32[]{:S(2)}, u32[]{:S(2)}) collective-permute-start(bf16[32,512]{1,0:T(8,128)(2,1)S(1)} %get-tuple-element.55), channel_id=1, source_target_pairs={{0,24},{2,26},{4,28},{6,30},{8,16},{10,18},{12,20},{14,22},{16,8},... | collective-permute-start | bytes 98312 | tf_op jit(solution)/shard_map/ppermute | solution.py:14
  81.7 0.8 maximum_bitcast_fusion
  82.5 1.4 %collective-permute-done.24 = bf16[32,512]{1,0:T(8,128)(2,1)S(1)} collective-permute-done((bf16[32,512]{1,0:T(8,128)(2,1)S(1)}, bf16[32,512]{1,0:T(8,128)(2,1)S(1)}, u32[]{:S(2)}, u32[]{:S(2)}) %collective-permute-start.24) | collective-permute-done | bytes 32800 | tf_op jit(solution)/shard_map/ppermute | solution.py:14
  83.9 2.0 %collective-permute-done.25 = bf16[32,512]{1,0:T(8,128)(2,1)S(1)} collective-permute-done((bf16[32,512]{1,0:T(8,128)(2,1)S(1)}, bf16[32,512]{1,0:T(8,128)(2,1)S(1)}, u32[]{:S(2)}, u32[]{:S(2)}) %collective-permute-start.25) | collective-permute-done | bytes 32800 | tf_op jit(solution)/shard_map/ppermute | solution.py:14
  85.9 0.6 fusion.36
  (79 shorter events, 8.1 us)
Async XLA Ops:
  0.6 23.8 %copy-start.1 = (bf16[128,2048]{1,0:T(8,128)(2,1)S(1)}, bf16[128,2048]{1,0:T(8,128)(2,1)}, u32[]{:S(2)}) copy-start(bf16[128,2048]{1,0:T(8,128)(2,1)} %param.11) | copy-start | bytes 1572868
  0.6 19.0 %copy-start.3 = (bf16[1,4096,32]{1,2,0:T(8,128)(2,1)S(1)}, bf16[1,4096,32]{1,2,0:T(8,128)(2,1)}, u32[]{:S(2)}) copy-start(bf16[1,4096,32]{1,2,0:T(8,128)(2,1)} %param.8) | copy-start | bytes 786436
  0.7 8.7 %collective-permute-start = (s32[2,1]{0,1:T(1,128)}, s32[2,1]{0,1:T(1,128)S(1)}, u32[]{:S(2)}, u32[]{:S(2)}) collective-permute-start(s32[2,1]{0,1:T(1,128)} %param.10), channel_id=1, source_target_pairs={{0,4},{2,6},{4,0},{6,2},{8,12},{10,14},{12,8},{14,10},{16,20},{18,... | collective-permute-start | bytes 32 | tf_op jit(solution)/shard_map/ppermute | solution.py:14
  3.7 5.7 %collective-permute-start.1 = (bf16[32,1024]{1,0:T(8,128)(2,1)}, bf16[32,1024]{1,0:T(8,128)(2,1)S(1)}, u32[]{:S(2)}, u32[]{:S(2)}) collective-permute-start(bf16[32,1024]{1,0:T(8,128)(2,1)} %bitcast.43), channel_id=1, source_target_pairs={{0,16},{2,18},{4,20},{6,22},{8,24},{10,26},{12,28},{14,30},{16,0},... | collective-permute-start | bytes 196616 | tf_op jit(solution)/shard_map/ppermute | solution.py:14
  6.2 18.1 %collective-permute-start.6 = (bf16[128,2048]{1,0:T(8,128)(2,1)}, bf16[128,2048]{1,0:T(8,128)(2,1)S(1)}, u32[]{:S(2)}, u32[]{:S(2)}) collective-permute-start(bf16[128,2048]{1,0:T(8,128)(2,1)} %param.11), channel_id=1, source_target_pairs={{0,1},{1,0},{2,3},{3,2},{4,5},{5,4},{6,7},{7,6},{8,9},{9,8},{10,11... | collective-permute-start | bytes 1572872 | tf_op jit(solution)/shard_map/ppermute | solution.py:18
  10.2 5.0 %collective-permute-start.2 = (bf16[64,1024]{1,0:T(8,128)(2,1)S(1)}, bf16[64,1024]{1,0:T(8,128)(2,1)S(1)}, u32[]{:S(2)}, u32[]{:S(2)}) collective-permute-start(bf16[64,1024]{1,0:T(8,128)(2,1)S(1)} %pad_maximum_fusion.5), channel_id=1, source_target_pairs={{0,8},{2,10},{4,12},{6,14},{8,0},{10,2},{12,4},{14,6},{16,24},{18,... | collective-permute-start | bytes 393224 | tf_op jit(solution)/shard_map/ppermute | solution.py:14
  16.1 1.6 %collective-permute-start.3 = (bf16[128,1024]{1,0:T(8,128)(2,1)S(1)}, bf16[128,1024]{1,0:T(8,128)(2,1)S(1)}, u32[]{:S(2)}, u32[]{:S(2)}) collective-permute-start(bf16[128,1024]{1,0:T(8,128)(2,1)S(1)} %pad_maximum_fusion.4), channel_id=1, source_target_pairs={{0,2},{2,0},{4,6},{6,4},{8,10},{10,8},{12,14},{14,12},{16,18},{18,... | collective-permute-start | bytes 786440 | tf_op jit(solution)/shard_map/ppermute | solution.py:14
  17.9 7.0 %copy-start.2 = (bf16[1,32,1024]{2,1,0:T(8,128)(2,1)S(1)}, bf16[1,32,1024]{2,1,0:T(8,128)(2,1)}, u32[]{:S(2)}) copy-start(bf16[1,32,1024]{2,1,0:T(8,128)(2,1)} %param.9) | copy-start | bytes 196612
  19.1 5.6 %collective-permute-start.5 = (bf16[64,1024]{1,0:T(8,128)(2,1)S(1)}, bf16[64,1024]{1,0:T(8,128)(2,1)S(1)}, u32[]{:S(2)}, u32[]{:S(2)}) collective-permute-start(bf16[64,1024]{1,0:T(8,128)(2,1)S(1)} %fusion.14), channel_id=1, source_target_pairs={{0,4},{2,6},{4,0},{6,2},{8,12},{10,14},{12,8},{14,10},{16,20},{18,... | collective-permute-start | bytes 393224 | tf_op jit(solution)/shard_map/ppermute | solution.py:14
  19.7 25.0 %collective-permute-start.7 = (bf16[32,4096]{1,0:T(8,128)(2,1)S(1)}, bf16[32,4096]{1,0:T(8,128)(2,1)S(1)}, u32[]{:S(2)}, u32[]{:S(2)}) collective-permute-start(bf16[32,4096]{1,0:T(8,128)(2,1)S(1)} %bitcast.48), channel_id=1, source_target_pairs={{0,8},{2,10},{4,12},{6,14},{8,0},{10,2},{12,4},{14,6},{16,24},{18,... | collective-permute-start | bytes 786440 | tf_op jit(solution)/shard_map/ppermute | solution.py:14
  21.0 14.9 %collective-permute-start.4 = (bf16[32,4096]{1,0:T(8,128)(2,1)S(1)}, bf16[32,4096]{1,0:T(8,128)(2,1)S(1)}, u32[]{:S(2)}, u32[]{:S(2)}) collective-permute-start(bf16[32,4096]{1,0:T(8,128)(2,1)S(1)} %bitcast.49), channel_id=1, source_target_pairs={{0,16},{2,18},{4,20},{6,22},{8,24},{10,26},{12,28},{14,30},{16,0},... | collective-permute-start | bytes 786440 | tf_op jit(solution)/shard_map/ppermute | solution.py:14
  24.7 1.6 %copy-start = (bf16[256,4096]{1,0:T(8,128)(2,1)S(1)}, bf16[256,4096]{1,0:T(8,128)(2,1)}, u32[]{:S(2)}) copy-start(bf16[256,4096]{1,0:T(8,128)(2,1)} %param.6) | copy-start | bytes 6291460
  26.9 17.8 %collective-permute-start.12 = (bf16[64,2048]{1,0:T(8,128)(2,1)S(1)}, bf16[64,2048]{1,0:T(8,128)(2,1)S(1)}, u32[]{:S(2)}, u32[]{:S(2)}) collective-permute-start(bf16[64,2048]{1,0:T(8,128)(2,1)S(1)} %fusion.11), channel_id=1, source_target_pairs={{0,4},{2,6},{4,0},{6,2},{8,12},{10,14},{12,8},{14,10},{16,20},{18,... | collective-permute-start | bytes 786440 | tf_op jit(solution)/shard_map/ppermute | solution.py:14
  28.4 16.3 %collective-permute-start.14 = (bf16[64,2048]{1,0:T(8,128)(2,1)S(1)}, bf16[64,2048]{1,0:T(8,128)(2,1)S(1)}, u32[]{:S(2)}, u32[]{:S(2)}) collective-permute-start(bf16[64,2048]{1,0:T(8,128)(2,1)S(1)} %fusion.10), channel_id=1, source_target_pairs={{0,4},{2,6},{4,0},{6,2},{8,12},{10,14},{12,8},{14,10},{16,20},{18,... | collective-permute-start | bytes 786440 | tf_op jit(solution)/shard_map/ppermute | solution.py:14
  35.8 8.9 %collective-permute-start.8 = (bf16[32,4096]{1,0:T(8,128)(2,1)S(1)}, bf16[32,4096]{1,0:T(8,128)(2,1)S(1)}, u32[]{:S(2)}, u32[]{:S(2)}) collective-permute-start(bf16[32,4096]{1,0:T(8,128)(2,1)S(1)} %collective-permute-done.4), channel_id=1, source_target_pairs={{0,8},{2,10},{4,12},{6,14},{8,0},{10,2},{12,4},{14,6},{16,24},{18,... | collective-permute-start | bytes 786440 | tf_op jit(solution)/shard_map/ppermute | solution.py:14
  44.8 2.7 %collective-permute-start.9 = (bf16[128,4096]{1,0:T(8,128)(2,1)S(1)}, bf16[128,4096]{1,0:T(8,128)(2,1)S(1)}, u32[]{:S(2)}, u32[]{:S(2)}) collective-permute-start(bf16[128,4096]{1,0:T(8,128)(2,1)S(1)} %pad_maximum_fusion.1), channel_id=1, source_target_pairs={{0,2},{2,0},{4,6},{6,4},{8,10},{10,8},{12,14},{14,12},{16,18},{18,... | collective-permute-start | bytes 3145736 | tf_op jit(solution)/shard_map/ppermute | solution.py:14
  45.3 3.9 %collective-permute-start.15 = (bf16[128,2048]{1,0:T(8,128)(2,1)S(1)}, bf16[128,2048]{1,0:T(8,128)(2,1)S(1)}, u32[]{:S(2)}, u32[]{:S(2)}) collective-permute-start(bf16[128,2048]{1,0:T(8,128)(2,1)S(1)} %fusion.9), channel_id=1, source_target_pairs={{0,2},{2,0},{4,6},{6,4},{8,10},{10,8},{12,14},{14,12},{16,18},{18,... | collective-permute-start | bytes 1572872 | tf_op jit(solution)/shard_map/ppermute | solution.py:14
  46.3 5.1 %collective-permute-start.13 = (bf16[128,2048]{1,0:T(8,128)(2,1)S(1)}, bf16[128,2048]{1,0:T(8,128)(2,1)S(1)}, u32[]{:S(2)}, u32[]{:S(2)}) collective-permute-start(bf16[128,2048]{1,0:T(8,128)(2,1)S(1)} %fusion.8), channel_id=1, source_target_pairs={{0,2},{2,0},{4,6},{6,4},{8,10},{10,8},{12,14},{14,12},{16,18},{18,... | collective-permute-start | bytes 1572872 | tf_op jit(solution)/shard_map/ppermute | solution.py:14
  47.9 14.0 %collective-permute-start.11 = (bf16[64,4096]{1,0:T(8,128)(2,1)S(1)}, bf16[64,4096]{1,0:T(8,128)(2,1)S(1)}, u32[]{:S(2)}, u32[]{:S(2)}) collective-permute-start(bf16[64,4096]{1,0:T(8,128)(2,1)S(1)} %fusion.5), channel_id=1, source_target_pairs={{0,4},{2,6},{4,0},{6,2},{8,12},{10,14},{12,8},{14,10},{16,20},{18,... | collective-permute-start | bytes 1572872 | tf_op jit(solution)/shard_map/ppermute | solution.py:14
  49.7 10.3 %collective-permute-start.17 = (bf16[64,2048]{1,0:T(8,128)(2,1)S(1)}, bf16[64,2048]{1,0:T(8,128)(2,1)S(1)}, u32[]{:S(2)}, u32[]{:S(2)}) collective-permute-start(bf16[64,2048]{1,0:T(8,128)(2,1)S(1)} %slice.238), channel_id=1, source_target_pairs={{0,8},{2,10},{4,12},{6,14},{8,0},{10,2},{12,4},{14,6},{16,24},{18,... | collective-permute-start | bytes 786440 | tf_op jit(solution)/shard_map/ppermute | solution.py:14
  51.9 12.7 %collective-permute-start.20 = (bf16[64,2048]{1,0:T(8,128)(2,1)S(1)}, bf16[64,2048]{1,0:T(8,128)(2,1)S(1)}, u32[]{:S(2)}, u32[]{:S(2)}) collective-permute-start(bf16[64,2048]{1,0:T(8,128)(2,1)S(1)} %slice.239), channel_id=1, source_target_pairs={{0,8},{2,10},{4,12},{6,14},{8,0},{10,2},{12,4},{14,6},{16,24},{18,... | collective-permute-start | bytes 786440 | tf_op jit(solution)/shard_map/ppermute | solution.py:14
  52.3 26.5 %collective-permute-start.10 = (bf16[128,2048]{1,0:T(8,128)(2,1)S(1)}, bf16[128,2048]{1,0:T(8,128)(2,1)S(1)}, u32[]{:S(2)}, u32[]{:S(2)}) collective-permute-start(bf16[128,2048]{1,0:T(8,128)(2,1)S(1)} %dynamic-slice_convert_fusion), channel_id=1, source_target_pairs={{0,1},{1,0},{2,3},{3,2},{4,5},{5,4},{6,7},{7,6},{8,9},{9,8},{10,11... | collective-permute-start | bytes 1572872 | tf_op jit(solution)/shard_map/ppermute | solution.py:18
  63.0 5.0 %collective-permute-start.16 = (f32[32,256]{1,0:T(8,128)S(1)}, f32[32,256]{1,0:T(8,128)S(1)}, u32[]{:S(2)}, u32[]{:S(2)}) collective-permute-start(f32[32,256]{1,0:T(8,128)S(1)} %slice_add_fusion.5), channel_id=1, source_target_pairs={{0,1},{1,0},{2,3},{3,2},{4,5},{5,4},{6,7},{7,6},{8,9},{9,8},{10,11... | collective-permute-start | bytes 98312 | tf_op jit(solution)/shard_map/ppermute | solution.py:18
  64.7 16.9 %collective-permute-start.18 = (bf16[32,2048]{1,0:T(8,128)(2,1)S(1)}, bf16[32,2048]{1,0:T(8,128)(2,1)S(1)}, u32[]{:S(2)}, u32[]{:S(2)}) collective-permute-start(bf16[32,2048]{1,0:T(8,128)(2,1)S(1)} %fusion.22), channel_id=1, source_target_pairs={{0,16},{2,18},{4,20},{6,22},{8,24},{10,26},{12,28},{14,30},{16,0},... | collective-permute-start | bytes 393224 | tf_op jit(solution)/shard_map/ppermute | solution.py:14
  67.9 13.6 %collective-permute-start.23 = (bf16[32,2048]{1,0:T(8,128)(2,1)S(1)}, bf16[32,2048]{1,0:T(8,128)(2,1)S(1)}, u32[]{:S(2)}, u32[]{:S(2)}) collective-permute-start(bf16[32,2048]{1,0:T(8,128)(2,1)S(1)} %fusion.21), channel_id=1, source_target_pairs={{0,16},{2,18},{4,20},{6,22},{8,24},{10,26},{12,28},{14,30},{16,0},... | collective-permute-start | bytes 393224 | tf_op jit(solution)/shard_map/ppermute | solution.py:14
  69.3 4.3 %collective-permute-start.19 = (bf16[64,512]{1,0:T(8,128)(2,1)S(1)}, bf16[64,512]{1,0:T(8,128)(2,1)S(1)}, u32[]{:S(2)}, u32[]{:S(2)}) collective-permute-start(bf16[64,512]{1,0:T(8,128)(2,1)S(1)} %select_convert_fusion), channel_id=1, source_target_pairs={{0,4},{2,6},{4,0},{6,2},{8,12},{10,14},{12,8},{14,10},{16,20},{18,... | collective-permute-start | bytes 196616 | tf_op jit(solution)/shard_map/ppermute | solution.py:14
  74.0 1.6 %collective-permute-start.21 = (bf16[128,512]{1,0:T(8,128)(2,1)S(1)}, bf16[128,512]{1,0:T(8,128)(2,1)S(1)}, u32[]{:S(2)}, u32[]{:S(2)}) collective-permute-start(bf16[128,512]{1,0:T(8,128)(2,1)S(1)} %fusion.16), channel_id=1, source_target_pairs={{0,2},{2,0},{4,6},{6,4},{8,10},{10,8},{12,14},{14,12},{16,18},{18,... | collective-permute-start | bytes 393224 | tf_op jit(solution)/shard_map/ppermute | solution.py:14
  75.9 5.7 %collective-permute-start.22 = (bf16[32,512]{1,0:T(8,128)(2,1)S(1)}, bf16[32,512]{1,0:T(8,128)(2,1)S(1)}, u32[]{:S(2)}, u32[]{:S(2)}) collective-permute-start(bf16[32,512]{1,0:T(8,128)(2,1)S(1)} %get-tuple-element.56), channel_id=1, source_target_pairs={{0,16},{2,18},{4,20},{6,22},{8,24},{10,26},{12,28},{14,30},{16,0},... | collective-permute-start | bytes 98312 | tf_op jit(solution)/shard_map/ppermute | solution.py:14
  79.9 3.9 %collective-permute-start.24 = (bf16[32,512]{1,0:T(8,128)(2,1)S(1)}, bf16[32,512]{1,0:T(8,128)(2,1)S(1)}, u32[]{:S(2)}, u32[]{:S(2)}) collective-permute-start(bf16[32,512]{1,0:T(8,128)(2,1)S(1)} %get-tuple-element.54), channel_id=1, source_target_pairs={{0,8},{2,10},{4,12},{6,14},{8,0},{10,2},{12,4},{14,6},{16,24},{18,... | collective-permute-start | bytes 98312 | tf_op jit(solution)/shard_map/ppermute | solution.py:14
  80.1 5.7 %collective-permute-start.25 = (bf16[32,512]{1,0:T(8,128)(2,1)S(1)}, bf16[32,512]{1,0:T(8,128)(2,1)S(1)}, u32[]{:S(2)}, u32[]{:S(2)}) collective-permute-start(bf16[32,512]{1,0:T(8,128)(2,1)S(1)} %get-tuple-element.55), channel_id=1, source_target_pairs={{0,24},{2,26},{4,28},{6,30},{8,16},{10,18},{12,20},{14,22},{16,8},... | collective-permute-start | bytes 98312 | tf_op jit(solution)/shard_map/ppermute | solution.py:14
